TPU v7x, 32 devices: a whole 2x2x4 slice. The times are simulated.
32 devices in a mesh: expert: 8 (over z, x), shard: 4 (over y, core).
Axes of the slice: x: 2, y: 2, z: 4, core: 2. Of those that a mesh axis runs over, the one named last changes fastest.
Arguments:
- hidden_in: bfloat16 [8, 1024, 768], P('expert', 'shard'), may hold values from -6 to 6
- gain_attn: bfloat16 [768], P('shard'), may hold values from 0.25 to 1.75
- gain_ffn: bfloat16 [768], P('shard'), may hold values from 0.25 to 1.75
- w_query: bfloat16 [768, 768], P('shard'), may hold values from -0.21875 to 0.21875
- w_key: bfloat16 [768, 768], P('shard'), may hold values from -0.21875 to 0.21875
- w_value: bfloat16 [768, 768], P('shard'), may hold values from -0.21875 to 0.21875
- w_out: bfloat16 [768, 768], P('shard'), may hold values from -1.25 to 1.25
- shared_gate: bfloat16 [768, 2048], P('shard'), may hold values from -0.21875 to 0.21875
- shared_up: bfloat16 [768, 2048], P('shard'), may hold values from -0.21875 to 0.21875
- shared_down: bfloat16 [2048, 768], P('shard'), may hold values from -0.125 to 0.125
- expert_gate: bfloat16 [8, 768, 2048], P('expert', 'shard'), may hold values from -0.21875 to 0.21875
- expert_up: bfloat16 [8, 768, 2048], P('expert', 'shard'), may hold values from -0.21875 to 0.21875
- expert_down: bfloat16 [8, 2048, 768], P('expert', 'shard'), may hold values from -0.125 to 0.125
- gate_logits: float32 [8, 1024, 2], P('expert', 'shard'), may hold values from -3.5 to 3.5
- routes: int32 [8, 1024, 2], P('expert', 'shard'), may hold values from 0 to 7, all different within a row; in each aligned block of 256 rows (0 to 255, 256 to 511, ..., all dimensions but the last counted through in order) at most 128 rows name the same one
- segment: int32 [8, 1024], P('expert'), may hold values from 0 to 2, as said below
- padding: int32 [8, 1024], P('expert'), may hold values 0 or 1
- cotangent: bfloat16 [8, 1024, 768], P('expert', 'shard'), may hold values from -6 to 6
Outputs:
- output: bfloat16 [8, 1024, 768], P('expert', 'shard')
- input_grad: float32 [8, 1024, 768], P('expert', 'shard')
- logit_grad: float32 [8, 1024, 2], P('expert', 'shard')
- gain_attn_grad: float32 [768], P('shard')
- gain_ffn_grad: float32 [768], P('shard')
- w_query_grad: float32 [768, 768], P('shard')
- w_key_grad: float32 [768, 768], P('shard')
- w_value_grad: float32 [768, 768], P('shard')
- w_out_grad: float32 [768, 768], P('shard')
- shared_gate_grad: float32 [768, 2048], P('shard')
- shared_up_grad: float32 [768, 2048], P('shard')
- shared_down_grad: float32 [2048, 768], P('shard')
- expert_gate_grad: float32 [8, 768, 2048], P('expert', 'shard')
- expert_up_grad: float32 [8, 768, 2048], P('expert', 'shard')
- expert_down_grad: float32 [8, 2048, 768], P('expert', 'shard')
Inputs may be any that keep to these rules, and one draw needn't show every extreme that they name: `routes`: in every aligned block of 256 tokens of a row (the tokens of one device) no expert is named more than 128 times, and in some blocks one is named exactly 128 times; a token's 2 experts differ. `segment`: within each row the numbers never fall and rise exactly twice: once at a position from 1 to 255 and once at a position from 769 to 1023.
All inputs are finite; a program needn't handle non-finite values. No bound on the sum of `padding` on one device may be relied on, other than what follows from the above.
Results may differ from a plain program's by a relative error of at most 0.02.
Values may be sent and summed in bfloat16 or wider, within the bound.
A program may use at most 256 MiB of HBM per device.

v0:
```python
import jax
import jax.numpy as jnp
from jax import lax
from jax.sharding import PartitionSpec as P

HEADS = 12
TOP = 2
WINDOW = 1024


norm_eps = 1e-06
neg_fill = -1e30
rope_base = 10000.0


def from_behind(value, axis, steps):
    count = lax.axis_size(axis)
    first, last = (max(0, -steps), min(count, count - steps))
    return lax.ppermute(value, axis, [(source, source + steps) for source in range(first, last)])


def dense_product(left, right):
    return jnp.dot(left, right, preferred_element_type=jnp.float32)


def rms_scale(values):
    return lax.rsqrt(jnp.mean(values * values, axis=-1, keepdims=True) + norm_eps)


def rotate(values, positions, direction):
    half_size = values.shape[-1] // 2
    frequency = rope_base ** (-jnp.arange(half_size, dtype=jnp.float32) / half_size)
    angles = positions.astype(jnp.float32)[:, None] * frequency[None, :]
    cosine = jnp.cos(angles)[:, None, :]
    sine_part = direction * jnp.sin(angles)[:, None, :]
    first_half = values[..., :half_size]
    second_half = values[..., half_size:]
    return jnp.concatenate(
        [
            first_half * cosine - second_half * sine_part,
            second_half * cosine + first_half * sine_part,
        ],
        axis=-1,
    )


def swiglu_back(grad_middle, gate_pre, up_pre):
    sigmoid_gate = jax.nn.sigmoid(gate_pre)
    activated = gate_pre * sigmoid_gate
    grad_gate = grad_middle * up_pre * sigmoid_gate * (1.0 + gate_pre * (1.0 - sigmoid_gate))
    grad_up = grad_middle * activated
    return (grad_gate.astype(jnp.bfloat16), grad_up.astype(jnp.bfloat16))


def shards(
    hidden_in,
    gain_attn,
    gain_ffn,
    w_query,
    w_key,
    w_value,
    w_out,
    shared_gate,
    shared_up,
    shared_down,
    expert_gate,
    expert_up,
    expert_down,
    gate_logits,
    routes,
    segment,
    padding,
    cotangent,
):
    bfloat = jnp.bfloat16
    tokens = hidden_in.shape[1]
    model_width = hidden_in.shape[2]
    head_size = model_width // HEADS
    experts = lax.axis_size("expert")
    capacity = max(2, 2 * tokens * TOP // experts)
    shard_count = lax.axis_size("shard")
    shard_index = lax.axis_index("shard")
    key_reach = min((WINDOW + tokens - 2) // tokens, shard_count - 1)
    key_rows = (key_reach + 1) * tokens
    score_scale = head_size ** (-0.5)
    head_shape = (tokens, HEADS, head_size)
    dense_all = (
        lax.all_gather(gain_attn, "shard", axis=0, tiled=True),
        lax.all_gather(gain_ffn, "shard", axis=0, tiled=True),
        lax.all_gather(w_query, "shard", axis=0, tiled=True),
        lax.all_gather(w_key, "shard", axis=0, tiled=True),
        lax.all_gather(w_value, "shard", axis=0, tiled=True),
        lax.all_gather(w_out, "shard", axis=0, tiled=True),
        lax.all_gather(shared_gate, "shard", axis=0, tiled=True),
        lax.all_gather(shared_up, "shard", axis=0, tiled=True),
        lax.all_gather(shared_down, "shard", axis=0, tiled=True),
    )
    expert_all = (
        lax.all_gather(expert_gate, "shard", axis=1, tiled=True),
        lax.all_gather(expert_up, "shard", axis=1, tiled=True),
        lax.all_gather(expert_down, "shard", axis=1, tiled=True),
    )
    gain_first = dense_all[0].astype(jnp.float32)
    gain_second = dense_all[1].astype(jnp.float32)
    gate_expert_all = expert_all[0][0]
    up_expert_all = expert_all[1][0]
    down_expert_all = expert_all[2][0]
    rows_in = hidden_in[0].astype(jnp.float32)
    scale_first = rms_scale(rows_in)
    normed = (rows_in * scale_first * gain_first).astype(bfloat)
    positions = shard_index * tokens + jnp.arange(tokens, dtype=jnp.int32)
    query_low = rotate(
        dense_product(normed, dense_all[2]).reshape(head_shape), positions, 1.0
    ).astype(bfloat)
    key_low = (
        rotate(dense_product(normed, dense_all[3]).reshape(head_shape), positions, 1.0)
        .astype(bfloat)
        .reshape(tokens, model_width)
    )
    value_low = dense_product(normed, dense_all[4]).astype(bfloat)
    key_parts = [key_low]
    value_parts = [value_low]
    for offset in range(1, key_reach + 1):
        earlier = from_behind((key_low, value_low), "shard", offset)
        key_parts.insert(0, earlier[0])
        value_parts.insert(0, earlier[1])
    keys_all = jnp.concatenate(key_parts, axis=0).reshape(key_rows, HEADS, head_size)
    values_all = jnp.concatenate(value_parts, axis=0).reshape(key_rows, HEADS, head_size)
    segment_row = segment[0]
    padding_row = padding[0]
    lead_rows = key_reach * tokens
    segment_ext = jnp.concatenate([jnp.full((lead_rows,), -1, jnp.int32), segment_row])
    padding_ext = jnp.concatenate([jnp.zeros((lead_rows,), jnp.int32), padding_row])
    key_segment = lax.dynamic_slice_in_dim(segment_ext, shard_index * tokens, key_rows)
    key_padding = lax.dynamic_slice_in_dim(padding_ext, shard_index * tokens, key_rows)
    query_segment = lax.dynamic_slice_in_dim(segment_row, shard_index * tokens, tokens)
    key_positions = (shard_index - key_reach) * tokens + jnp.arange(key_rows, dtype=jnp.int32)
    distance = positions[:, None] - key_positions[None, :]
    allowed = (
        (query_segment[:, None] == key_segment[None, :])
        & (distance >= 0)
        & (distance < WINDOW)
        & ((key_padding[None, :] == 1) | (distance == 0))
    )

    def score_block():
        raw_scores = (
            jnp.einsum("qhd,khd->hqk", query_low, keys_all, preferred_element_type=jnp.float32)
            * score_scale
        )
        return jnp.where(allowed[None], raw_scores, neg_fill)

    scores = score_block()
    top_score = jnp.max(scores, axis=-1, keepdims=True)
    exponent = jnp.exp(scores - top_score)
    exp_total = jnp.sum(exponent, axis=-1, keepdims=True)
    attn_probs = exponent / exp_total
    log_total = top_score + jnp.log(exp_total)
    attended = (
        jnp.einsum(
            "hqk,khd->qhd",
            attn_probs.astype(bfloat),
            values_all,
            preferred_element_type=jnp.float32,
        )
        .astype(bfloat)
        .reshape(tokens, model_width)
    )
    mixed_rows = rows_in + dense_product(attended, dense_all[5])
    scale_second = rms_scale(mixed_rows)
    normed_ffn = (mixed_rows * scale_second * gain_second).astype(bfloat)
    shared_pre = dense_product(normed_ffn, dense_all[6])
    shared_lin = dense_product(normed_ffn, dense_all[7])
    shared_mid = (jax.nn.silu(shared_pre) * shared_lin).astype(bfloat)
    shared_out = dense_product(shared_mid, dense_all[8])
    route_flat = routes[0].reshape(-1)
    route_total = tokens * TOP
    onehot = (route_flat[:, None] == jnp.arange(experts, dtype=jnp.int32)[None, :]).astype(
        jnp.int32
    )
    slot_rank = jnp.sum((jnp.cumsum(onehot, axis=0) - onehot) * onehot, axis=1)
    places = route_flat * capacity + slot_rank
    slot_table = (
        jnp.full((experts * capacity,), route_total, dtype=jnp.int32)
        .at[places]
        .set(jnp.arange(route_total, dtype=jnp.int32))
    )
    padded_rows = jnp.concatenate([normed_ffn, jnp.zeros((1, model_width), bfloat)], axis=0)
    send_rows = padded_rows[slot_table // TOP].reshape(experts, capacity, model_width)
    received = lax.all_to_all(send_rows, "expert", split_axis=0, concat_axis=0, tiled=True)
    gate_pre = jnp.einsum(
        "sid,df->sif", received, gate_expert_all, preferred_element_type=jnp.float32
    )
    up_pre = jnp.einsum("sid,df->sif", received, up_expert_all, preferred_element_type=jnp.float32)
    middle = (jax.nn.silu(gate_pre) * up_pre).astype(bfloat)
    result = jnp.einsum(
        "sif,fd->sid", middle, down_expert_all, preferred_element_type=jnp.float32
    ).astype(bfloat)
    returned = lax.all_to_all(result, "expert", split_axis=0, concat_axis=0, tiled=True)
    outcome = (returned, received, gate_pre, up_pre)
    per_route = (
        outcome[0]
        .reshape(experts * capacity, model_width)[places]
        .astype(jnp.float32)
        .reshape(tokens, TOP, model_width)
    )
    gate_probs = jax.nn.softmax(gate_logits[0], axis=-1)
    routed = jnp.sum(gate_probs[:, :, None] * per_route, axis=1)
    output = (mixed_rows + shared_out + routed).astype(bfloat)
    grad_low = cotangent[0]
    grad_out = grad_low.astype(jnp.float32)
    contrib = jnp.sum(per_route * grad_out[:, None, :], axis=-1)
    logit_grad = gate_probs * (contrib - jnp.sum(gate_probs * contrib, axis=-1, keepdims=True))
    route_grad = (
        (gate_probs[:, :, None] * grad_out[:, None, :])
        .astype(bfloat)
        .reshape(route_total, model_width)
    )
    route_padded = jnp.concatenate([route_grad, jnp.zeros((1, model_width), bfloat)], axis=0)
    send_grad = route_padded[slot_table].reshape(experts, capacity, model_width)
    held_weights = lax.optimization_barrier(
        (
            gain_attn,
            gain_ffn,
            w_query,
            w_key,
            w_value,
            w_out,
            shared_gate,
            shared_up,
            shared_down,
            expert_gate,
            expert_up,
            expert_down,
            send_grad,
        )
    )
    dense_back = (
        lax.all_gather(held_weights[0], "shard", axis=0, tiled=True),
        lax.all_gather(held_weights[1], "shard", axis=0, tiled=True),
        lax.all_gather(held_weights[2], "shard", axis=0, tiled=True),
        lax.all_gather(held_weights[3], "shard", axis=0, tiled=True),
        lax.all_gather(held_weights[4], "shard", axis=0, tiled=True),
        lax.all_gather(held_weights[5], "shard", axis=0, tiled=True),
        lax.all_gather(held_weights[6], "shard", axis=0, tiled=True),
        lax.all_gather(held_weights[7], "shard", axis=0, tiled=True),
        lax.all_gather(held_weights[8], "shard", axis=0, tiled=True),
    )
    expert_back = (
        lax.all_gather(held_weights[9], "shard", axis=1, tiled=True),
        lax.all_gather(held_weights[10], "shard", axis=1, tiled=True),
        lax.all_gather(held_weights[11], "shard", axis=1, tiled=True),
    )
    gate_expert_back = expert_back[0][0]
    up_expert_back = expert_back[1][0]
    down_expert_back = expert_back[2][0]
    grad_received = lax.all_to_all(send_grad, "expert", split_axis=0, concat_axis=0, tiled=True)
    received = outcome[1]
    gate_pre = outcome[2]
    up_pre = outcome[3]
    middle = (jax.nn.silu(gate_pre) * up_pre).astype(bfloat)
    grad_middle = jnp.einsum(
        "sid,fd->sif", grad_received, down_expert_back, preferred_element_type=jnp.float32
    )
    grad_gate_pre, grad_up_pre = swiglu_back(grad_middle, gate_pre, up_pre)
    expert_down_grad = jnp.einsum(
        "sif,sid->fd", middle, grad_received, preferred_element_type=jnp.float32
    )
    expert_gate_grad = jnp.einsum(
        "sid,sif->df", received, grad_gate_pre, preferred_element_type=jnp.float32
    )
    expert_up_grad = jnp.einsum(
        "sid,sif->df", received, grad_up_pre, preferred_element_type=jnp.float32
    )
    grad_rows = (
        jnp.einsum(
            "sif,df->sid", grad_gate_pre, gate_expert_back, preferred_element_type=jnp.float32
        )
        + jnp.einsum("sif,df->sid", grad_up_pre, up_expert_back, preferred_element_type=jnp.float32)
    ).astype(bfloat)
    grad_back = lax.all_to_all(grad_rows, "expert", split_axis=0, concat_axis=0, tiled=True)
    expert_grads = (
        lax.psum_scatter(
            expert_gate_grad[None].astype(jnp.bfloat16), "shard", scatter_dimension=1, tiled=True
        ).astype(jnp.float32),
        lax.psum_scatter(
            expert_up_grad[None].astype(jnp.bfloat16), "shard", scatter_dimension=1, tiled=True
        ).astype(jnp.float32),
        lax.psum_scatter(
            expert_down_grad[None].astype(jnp.bfloat16), "shard", scatter_dimension=1, tiled=True
        ).astype(jnp.float32),
    )
    grad_routes = (
        grad_back.reshape(experts * capacity, model_width)[places]
        .astype(jnp.float32)
        .reshape(tokens, TOP, model_width)
    )
    grad_normed_ffn = jnp.sum(grad_routes, axis=1)
    grad_shared_mid = dense_product(grad_low, dense_back[8].T)
    grad_shared_pre, grad_shared_lin = swiglu_back(grad_shared_mid, shared_pre, shared_lin)
    shared_down_grad = dense_product(shared_mid.T, grad_low)
    shared_gate_grad = dense_product(normed_ffn.T, grad_shared_pre)
    shared_up_grad = dense_product(normed_ffn.T, grad_shared_lin)
    grad_normed_ffn = (
        grad_normed_ffn
        + dense_product(grad_shared_pre, dense_back[6].T)
        + dense_product(grad_shared_lin, dense_back[7].T)
    )
    gain_ffn_grad = jnp.sum(grad_normed_ffn * mixed_rows * scale_second, axis=0)
    scaled_second = grad_normed_ffn * dense_back[1].astype(jnp.float32)
    grad_mixed = (
        grad_out
        + scale_second * scaled_second
        - mixed_rows
        * scale_second**3
        * jnp.mean(scaled_second * mixed_rows, axis=-1, keepdims=True)
    )
    grad_mixed_low = grad_mixed.astype(bfloat)
    w_out_grad = dense_product(attended.T, grad_mixed_low)
    grad_attended = (
        dense_product(grad_mixed_low, dense_back[5].T).astype(bfloat).reshape(head_shape)
    )
    attn_probs = jnp.exp(score_block() - log_total)
    grad_probs = jnp.einsum(
        "qhd,khd->hqk", grad_attended, values_all, preferred_element_type=jnp.float32
    )
    delta_rows = jnp.sum(attn_probs * grad_probs, axis=-1, keepdims=True)
    grad_scores = (attn_probs * (grad_probs - delta_rows)).astype(bfloat)
    grad_query = (
        jnp.einsum("hqk,khd->qhd", grad_scores, keys_all, preferred_element_type=jnp.float32)
        * score_scale
    )
    grad_keys = (
        jnp.einsum("hqk,qhd->khd", grad_scores, query_low, preferred_element_type=jnp.float32)
        * score_scale
    ).reshape(key_reach + 1, tokens, model_width)
    grad_values = jnp.einsum(
        "hqk,qhd->khd", attn_probs.astype(bfloat), grad_attended, preferred_element_type=jnp.float32
    ).reshape(key_reach + 1, tokens, model_width)
    key_total = grad_keys[key_reach]
    value_total = grad_values[key_reach]
    for offset in range(1, key_reach + 1):
        from_later = (
            from_behind(
                grad_keys[key_reach - offset].astype(jnp.bfloat16), "shard", -offset
            ).astype(jnp.float32),
            from_behind(
                grad_values[key_reach - offset].astype(jnp.bfloat16), "shard", -offset
            ).astype(jnp.float32),
        )
        key_total = key_total + from_later[0]
        value_total = value_total + from_later[1]
    grad_query_low = rotate(grad_query, positions, -1.0).astype(bfloat).reshape(tokens, model_width)
    grad_key_low = (
        rotate(key_total.reshape(head_shape), positions, -1.0)
        .astype(bfloat)
        .reshape(tokens, model_width)
    )
    grad_value_low = value_total.astype(bfloat)
    w_query_grad = dense_product(normed.T, grad_query_low)
    w_key_grad = dense_product(normed.T, grad_key_low)
    w_value_grad = dense_product(normed.T, grad_value_low)
    grad_normed = (
        dense_product(grad_query_low, dense_back[2].T)
        + dense_product(grad_key_low, dense_back[3].T)
        + dense_product(grad_value_low, dense_back[4].T)
    )
    gain_attn_grad = jnp.sum(grad_normed * rows_in * scale_first, axis=0)
    scaled_first = grad_normed * dense_back[0].astype(jnp.float32)
    input_grad = (
        grad_mixed
        + scale_first * scaled_first
        - rows_in * scale_first**3 * jnp.mean(scaled_first * rows_in, axis=-1, keepdims=True)
    )
    pieces = (
        lax.psum_scatter(
            gain_attn_grad.astype(jnp.bfloat16), "shard", scatter_dimension=0, tiled=True
        ).astype(jnp.float32),
        lax.psum_scatter(
            gain_ffn_grad.astype(jnp.bfloat16), "shard", scatter_dimension=0, tiled=True
        ).astype(jnp.float32),
        lax.psum_scatter(
            w_query_grad.astype(jnp.bfloat16), "shard", scatter_dimension=0, tiled=True
        ).astype(jnp.float32),
        lax.psum_scatter(
            w_key_grad.astype(jnp.bfloat16), "shard", scatter_dimension=0, tiled=True
        ).astype(jnp.float32),
        lax.psum_scatter(
            w_value_grad.astype(jnp.bfloat16), "shard", scatter_dimension=0, tiled=True
        ).astype(jnp.float32),
        lax.psum_scatter(
            w_out_grad.astype(jnp.bfloat16), "shard", scatter_dimension=0, tiled=True
        ).astype(jnp.float32),
        lax.psum_scatter(
            shared_gate_grad.astype(jnp.bfloat16), "shard", scatter_dimension=0, tiled=True
        ).astype(jnp.float32),
        lax.psum_scatter(
            shared_up_grad.astype(jnp.bfloat16), "shard", scatter_dimension=0, tiled=True
        ).astype(jnp.float32),
        lax.psum_scatter(
            shared_down_grad.astype(jnp.bfloat16), "shard", scatter_dimension=0, tiled=True
        ).astype(jnp.float32),
    )
    totals = (
        lax.psum(pieces[0].astype(jnp.bfloat16), "expert").astype(jnp.float32),
        lax.psum(pieces[1].astype(jnp.bfloat16), "expert").astype(jnp.float32),
        lax.psum(pieces[2].astype(jnp.bfloat16), "expert").astype(jnp.float32),
        lax.psum(pieces[3].astype(jnp.bfloat16), "expert").astype(jnp.float32),
        lax.psum(pieces[4].astype(jnp.bfloat16), "expert").astype(jnp.float32),
        lax.psum(pieces[5].astype(jnp.bfloat16), "expert").astype(jnp.float32),
        lax.psum(pieces[6].astype(jnp.bfloat16), "expert").astype(jnp.float32),
        lax.psum(pieces[7].astype(jnp.bfloat16), "expert").astype(jnp.float32),
        lax.psum(pieces[8].astype(jnp.bfloat16), "expert").astype(jnp.float32),
    )
    return (
        output[None],
        input_grad[None],
        logit_grad[None],
        totals[0],
        totals[1],
        totals[2],
        totals[3],
        totals[4],
        totals[5],
        totals[6],
        totals[7],
        totals[8],
        expert_grads[0],
        expert_grads[1],
        expert_grads[2],
    )


def solution(mesh):
    placed = (
        P("expert", "shard", None),
        P("shard"),
        P("shard"),
        P("shard", None),
        P("shard", None),
        P("shard", None),
        P("shard", None),
        P("shard", None),
        P("shard", None),
        P("shard", None),
        P("expert", "shard", None),
        P("expert", "shard", None),
        P("expert", "shard", None),
        P("expert", "shard", None),
        P("expert", "shard", None),
        P("expert", None),
        P("expert", None),
        P("expert", "shard", None),
    )
    return jax.shard_map(
        shards,
        mesh=mesh,
        in_specs=placed,
        out_specs=(
            P("expert", "shard", None),
            P("expert", "shard", None),
            P("expert", "shard", None),
            P("shard"),
            P("shard"),
            P("shard", None),
            P("shard", None),
            P("shard", None),
            P("shard", None),
            P("shard", None),
            P("shard", None),
            P("shard", None),
            P("expert", "shard", None),
            P("expert", "shard", None),
            P("expert", "shard", None),
        ),
        check_vma=False,
    )
```

profile of v0, /device:TPU:0, one launch (start us, length us, event | category | flops | bytes accessed | tf_op | source)
XLA Modules:
  0.0 1059.3 jit_solution(5024927332860699779)
XLA Ops:
  85.0 11.9 %collective-permute-done.4 = bf16[256,768]{0,1:T(8,128)(2,1)} collective-permute-done((bf16[256,768]{0,1:T(8,128)(2,1)}, bf16[256,768]{0,1:T(8,128)(2,1)}, u32[]{:S(2)}, u32[]{:S(2)}) %collective-permute-start.4) | collective-permute-done | bytes 393248 | tf_op jit(solution)/shard_map/ppermute | solution.py:19
  140.0 18.5 %all-gather.37.cloned.1.call-done = bf16[1,768,2048]{2,1,0:T(8,128)(2,1)} async-done(((bf16[1,192,2048]{2,1,0:T(8,128)(2,1)}), bf16[1,768,2048]{2,1,0:T(8,128)(2,1)}) %all-gather.37.cloned.1.call-update) | async-done | bytes 3145744 | tf_op jit(solution)/shard_map/all_gather | solution.py:100
  175.0 13.6 %all-gather.35.cloned.1.call-done = bf16[1,768,2048]{2,1,0:T(8,128)(2,1)} async-done(((bf16[1,192,2048]{2,1,0:T(8,128)(2,1)}), bf16[1,768,2048]{2,1,0:T(8,128)(2,1)}) %all-gather.35.cloned.1.call-update) | async-done | bytes 3145744 | tf_op jit(solution)/shard_map/all_gather | solution.py:99
  188.7 13.9 %multiply_convert_fusion.2 = (bf16[8,128,2048]{2,1,0:T(8,128)(2,1)}, bf16[8,128,2048]{2,1,0:T(8,128)(2,1)}, bf16[8,128,2048]{2,1,0:T(8,128)(2,1)}) fusion(f32[8,128,2048]{2,1,0:T(8,128)} %fusion.12, f32[8,128,2048]{2,1,0:T(8,128)} %fusion.16, bf16[8,128,768]{2,1,0:T(8,128)(2,1)S(1)} %all-to-all-done, bf16[1,768,2048]{2,1,0:T(8,128)(2,1)} %all-gather.35.cloned.1.call-done), kind=kOutput, calls=%fused_computation.14 | convolution fusion | flops 3252682752 | bytes 34078720 | tf_op jit(solution)/shard_map/sid,df->sif/dot_general | solution.py:191
  202.6 16.2 %all-gather.45.cloned.1.call-done = bf16[1,768,2048]{2,1,0:T(8,128)(2,1)} async-done(((bf16[1,192,2048]{2,1,0:T(8,128)(2,1)}), bf16[1,768,2048]{2,1,0:T(8,128)(2,1)}) %all-gather.45.cloned.1.call-update) | async-done | bytes 3145744 | tf_op jit(solution)/shard_map/all_gather | solution.py:251
  227.0 21.9 %all-gather.43.cloned.1.call-done = bf16[1,768,2048]{2,1,0:T(8,128)(2,1)} async-done(((bf16[1,192,2048]{2,1,0:T(8,128)(2,1)}), bf16[1,768,2048]{2,1,0:T(8,128)(2,1)}) %all-gather.43.cloned.1.call-update) | async-done | bytes 3145744 | tf_op jit(solution)/shard_map/all_gather | solution.py:250
  263.7 15.2 %all-gather.29.cloned.1.call-done = bf16[768,2048]{1,0:T(8,128)(2,1)} async-done(((bf16[192,2048]{1,0:T(8,128)(2,1)}), bf16[768,2048]{1,0:T(8,128)(2,1)}) %all-gather.29.cloned.1.call-update) | async-done | bytes 3145744 | tf_op jit(solution)/shard_map/all_gather | solution.py:94
  283.1 26.0 %all-gather.31.cloned.1.call-done = bf16[768,2048]{1,0:T(8,128)(2,1)} async-done(((bf16[192,2048]{1,0:T(8,128)(2,1)}), bf16[768,2048]{1,0:T(8,128)(2,1)}) %all-gather.31.cloned.1.call-update) | async-done | bytes 3145744 | tf_op jit(solution)/shard_map/all_gather | solution.py:95
  313.2 25.8 %all-gather.47.cloned.1.call-done = bf16[2048,768]{1,0:T(8,128)(2,1)} async-done(((bf16[512,768]{1,0:T(8,128)(2,1)}), bf16[2048,768]{1,0:T(8,128)(2,1)}) %all-gather.47.cloned.1.call-update) | async-done | bytes 3145744 | tf_op jit(solution)/shard_map/all_gather | solution.py:247
  353.8 15.4 %all-gather.49.cloned.1.call-done = bf16[768,2048]{1,0:T(8,128)(2,1)} async-done(((bf16[192,2048]{1,0:T(8,128)(2,1)}), bf16[768,2048]{1,0:T(8,128)(2,1)}) %all-gather.49.cloned.1.call-update) | async-done | bytes 3145744 | tf_op jit(solution)/shard_map/all_gather | solution.py:245
  373.4 25.7 %all-gather.51.cloned.1.call-done = bf16[768,2048]{1,0:T(8,128)(2,1)} async-done(((bf16[192,2048]{1,0:T(8,128)(2,1)}), bf16[768,2048]{1,0:T(8,128)(2,1)}) %all-gather.51.cloned.1.call-update) | async-done | bytes 3145744 | tf_op jit(solution)/shard_map/all_gather | solution.py:246
  403.3 14.7 %all-gather.53.cloned.1.call-done = bf16[768,768]{1,0:T(8,128)(2,1)} async-done(((bf16[192,768]{1,0:T(8,128)(2,1)}), bf16[768,768]{1,0:T(8,128)(2,1)}) %all-gather.53.cloned.1.call-update) | async-done | bytes 1179664 | tf_op jit(solution)/shard_map/all_gather | solution.py:244
  545.9 17.8 %reduce-scatter.15.cloned.1.call-done = bf16[192,768]{1,0:T(8,128)(2,1)} async-done(((bf16[768,768]{1,0:T(8,128)(2,1)}), bf16[192,768]{1,0:T(8,128)(2,1)}) %reduce-scatter.15.cloned.1.call-update) | async-done | bytes 294928 | tf_op jit(solution)/shard_map/reduce_scatter | solution.py:388
  563.7 40.5 %reduce-scatter.19.cloned.1.call-done = bf16[192,2048]{1,0:T(8,128)(2,1)} async-done(((bf16[768,2048]{1,0:T(8,128)(2,1)}), bf16[192,2048]{1,0:T(8,128)(2,1)}) %reduce-scatter.19.cloned.1.call-update) | async-done | bytes 786448 | tf_op jit(solution)/shard_map/reduce_scatter | solution.py:394
  604.3 40.7 %reduce-scatter.21.cloned.1.call-done = bf16[192,2048]{1,0:T(8,128)(2,1)} async-done(((bf16[768,2048]{1,0:T(8,128)(2,1)}), bf16[192,2048]{1,0:T(8,128)(2,1)}) %reduce-scatter.21.cloned.1.call-update) | async-done | bytes 786448 | tf_op jit(solution)/shard_map/reduce_scatter | solution.py:397
  644.9 40.5 %reduce-scatter.23.cloned.1.call-done = bf16[512,768]{1,0:T(8,128)(2,1)} async-done(((bf16[2048,768]{1,0:T(8,128)(2,1)}), bf16[512,768]{1,0:T(8,128)(2,1)}) %reduce-scatter.23.cloned.1.call-update) | async-done | bytes 786448 | tf_op jit(solution)/shard_map/reduce_scatter | solution.py:400
  700.3 15.3 %all-gather.33.cloned.1.call-done = bf16[2048,768]{1,0:T(8,128)(2,1)} async-done(((bf16[512,768]{1,0:T(8,128)(2,1)}), bf16[2048,768]{1,0:T(8,128)(2,1)}) %all-gather.33.cloned.1.call-update) | async-done | bytes 3145744 | tf_op jit(solution)/shard_map/all_gather | solution.py:96
  719.8 14.9 %all-gather.55.cloned.1.call-done = bf16[768,768]{1,0:T(8,128)(2,1)} async-done(((bf16[192,768]{1,0:T(8,128)(2,1)}), bf16[768,768]{1,0:T(8,128)(2,1)}) %all-gather.55.cloned.1.call-update) | async-done | bytes 1179664 | tf_op jit(solution)/shard_map/all_gather | solution.py:241
  737.3 16.3 %all-gather.57.cloned.1.call-done = bf16[768,768]{1,0:T(8,128)(2,1)} async-done(((bf16[192,768]{1,0:T(8,128)(2,1)}), bf16[768,768]{1,0:T(8,128)(2,1)}) %all-gather.57.cloned.1.call-update) | async-done | bytes 1179664 | tf_op jit(solution)/shard_map/all_gather | solution.py:242
  755.7 17.0 %all-gather.59.cloned.1.call-done = bf16[768,768]{1,0:T(8,128)(2,1)} async-done(((bf16[192,768]{1,0:T(8,128)(2,1)}), bf16[768,768]{1,0:T(8,128)(2,1)}) %all-gather.59.cloned.1.call-update) | async-done | bytes 1179664 | tf_op jit(solution)/shard_map/all_gather | solution.py:243
  780.6 21.5 %all-reduce.10 = (bf16[192]{0:T(256)(128)(2,1)S(1)}, bf16[192]{0:T(256)(128)(2,1)S(1)}) all-reduce(bf16[192]{0:T(256)(128)(2,1)S(1)} %dynamic-slice.6, bf16[192]{0:T(256)(128)(2,1)S(1)} %dynamic-slice.8), channel_id=1, replica_groups=mesh['expert'=8,'shard'=4] {'expert'}, use_global_device_ids=true, to_apply=%region_19.20 | all-reduce | flops 384 | bytes 1536 | tf_op jit(solution)/shard_map/psum | solution.py:405
  815.7 38.1 %reduce-scatter.27.cloned.1.call-done = bf16[1,192,2048]{2,1,0:T(8,128)(2,1)} async-done(((bf16[1,768,2048]{2,1,0:T(8,128)(2,1)}), bf16[1,192,2048]{2,1,0:T(8,128)(2,1)}) %reduce-scatter.27.cloned.1.call-update) | async-done | bytes 786448 | tf_op jit(solution)/shard_map/reduce_scatter | solution.py:286
  856.2 38.0 %reduce-scatter.29.cloned.1.call-done = bf16[1,512,768]{2,1,0:T(8,128)(2,1)} async-done(((bf16[1,2048,768]{2,1,0:T(8,128)(2,1)}), bf16[1,512,768]{2,1,0:T(8,128)(2,1)}) %reduce-scatter.29.cloned.1.call-update) | async-done | bytes 786448 | tf_op jit(solution)/shard_map/reduce_scatter | solution.py:289
  896.7 144.0 %all-reduce.16.cloned.1.call-done = (bf16[192,768]{1,0:T(8,128)(2,1)}, bf16[192,768]{1,0:T(8,128)(2,1)}, bf16[192,768]{1,0:T(8,128)(2,1)}, bf16[192,768]{1,0:T(8...) async-done(((bf16[192,768]{1,0:T(8,128)(2,1)}, bf16[192,768]{1,0:T(8,128)(2,1)}, bf16[192,768]{1,0:T(8,128)(2,1)}, ...) | async-done | bytes 3538960 | tf_op jit(solution)/shard_map/psum | solution.py:407
  (343 shorter events, 378.8 us)
Async XLA Ops:
  10.0 120.7 %all-gather.41.cloned.1.call-start = ((), (), s32[]{:S(2)}) async-start(), calls=%async_computation.24 | async-start | bytes 3932160 | tf_op jit(solution)/shard_map/all_gather | solution.py:252
  27.9 130.6 %all-gather.37.cloned.1.call-start = ((), (), s32[]{:S(2)}) async-start(), calls=%async_computation.22 | async-start | bytes 3932160 | tf_op jit(solution)/shard_map/all_gather | solution.py:100
  28.5 160.2 %all-gather.35.cloned.1.call-start = ((), (), s32[]{:S(2)}) async-start(), calls=%async_computation.21 | async-start | bytes 3932160 | tf_op jit(solution)/shard_map/all_gather | solution.py:99
  29.2 189.6 %all-gather.45.cloned.1.call-start = ((), (), s32[]{:S(2)}) async-start(), calls=%async_computation.26 | async-start | bytes 3932160 | tf_op jit(solution)/shard_map/all_gather | solution.py:251
  30.0 219.0 %all-gather.43.cloned.1.call-start = ((), (), s32[]{:S(2)}) async-start(), calls=%async_computation.25 | async-start | bytes 3932160 | tf_op jit(solution)/shard_map/all_gather | solution.py:250
  30.7 248.2 %all-gather.29.cloned.1.call-start = ((), (), s32[]{:S(2)}) async-start(), calls=%async_computation.18 | async-start | bytes 3932160 | tf_op jit(solution)/shard_map/all_gather | solution.py:94
  31.3 277.7 %all-gather.31.cloned.1.call-start = ((), (), s32[]{:S(2)}) async-start(), calls=%async_computation.19 | async-start | bytes 3932160 | tf_op jit(solution)/shard_map/all_gather | solution.py:95
  32.1 306.9 %all-gather.47.cloned.1.call-start = ((), (), s32[]{:S(2)}) async-start(), calls=%async_computation.27 | async-start | bytes 3932160 | tf_op jit(solution)/shard_map/all_gather | solution.py:247
  32.7 336.5 %all-gather.49.cloned.1.call-start = ((), (), s32[]{:S(2)}) async-start(), calls=%async_computation.28 | async-start | bytes 3932160 | tf_op jit(solution)/shard_map/all_gather | solution.py:245
  40.6 358.5 %all-gather.51.cloned.1.call-start = ((), (), s32[]{:S(2)}) async-start(), calls=%async_computation.29 | async-start | bytes 3932160 | tf_op jit(solution)/shard_map/all_gather | solution.py:246
  130.1 287.9 %all-gather.53.cloned.1.call-start = ((), (), s32[]{:S(2)}) async-start(), calls=%async_computation.30 | async-start | bytes 1474560 | tf_op jit(solution)/shard_map/all_gather | solution.py:244
  263.1 268.5 %all-gather.39.cloned.1.call-start = ((), (), s32[]{:S(2)}) async-start(), calls=%async_computation.23 | async-start | bytes 3932160 | tf_op jit(solution)/shard_map/all_gather | solution.py:101
  263.6 282.2 %reduce-scatter.17.cloned.1.call-start = ((), (), s32[]{:S(2)}) async-start(), calls=%async_computation.37 | async-start | bytes 1474560 | tf_op jit(solution)/shard_map/reduce_scatter | solution.py:391
  498.4 146.6 %reduce-scatter.21.cloned.1.call-start = ((), (), s32[]{:S(2)}) async-start(), calls=%async_computation.39 | async-start | bytes 3932160 | tf_op jit(solution)/shard_map/reduce_scatter | solution.py:397
  502.2 183.2 %reduce-scatter.23.cloned.1.call-start = ((), (), s32[]{:S(2)}) async-start(), calls=%async_computation.40 | async-start | bytes 3932160 | tf_op jit(solution)/shard_map/reduce_scatter | solution.py:400
  506.2 209.3 %all-gather.33.cloned.1.call-start = ((), (), s32[]{:S(2)}) async-start(), calls=%async_computation.20 | async-start | bytes 3932160 | tf_op jit(solution)/shard_map/all_gather | solution.py:96
  506.8 227.9 %all-gather.55.cloned.1.call-start = ((), (), s32[]{:S(2)}) async-start(), calls=%async_computation.31 | async-start | bytes 1474560 | tf_op jit(solution)/shard_map/all_gather | solution.py:241
  507.5 246.1 %all-gather.57.cloned.1.call-start = ((), (), s32[]{:S(2)}) async-start(), calls=%async_computation.32 | async-start | bytes 1474560 | tf_op jit(solution)/shard_map/all_gather | solution.py:242
  508.1 264.5 %all-gather.59.cloned.1.call-start = ((), (), s32[]{:S(2)}) async-start(), calls=%async_computation.33 | async-start | bytes 1474560 | tf_op jit(solution)/shard_map/all_gather | solution.py:243
  508.7 304.6 %reduce-scatter.25.cloned.1.call-start = ((), (), s32[]{:S(2)}) async-start(), calls=%async_computation.41 | async-start | bytes 3932160 | tf_op jit(solution)/shard_map/reduce_scatter | solution.py:283
  516.0 337.8 %reduce-scatter.27.cloned.1.call-start = ((), (), s32[]{:S(2)}) async-start(), calls=%async_computation.42 | async-start | bytes 3932160 | tf_op jit(solution)/shard_map/reduce_scatter | solution.py:286
  523.4 370.9 %reduce-scatter.29.cloned.1.call-start = ((), (), s32[]{:S(2)}) async-start(), calls=%async_computation.43 | async-start | bytes 3932160 | tf_op jit(solution)/shard_map/reduce_scatter | solution.py:289
  539.4 147.6 %all-to-all-start.1 = ((bf16[8,128,768]{2,1,0:T(8,128)(2,1)}), bf16[8,128,768]{2,1,0:T(8,128)(2,1)S(1)}, u32[]{:S(2)}, u32[]{:S(2)}) async-start(bf16[8,128,768]{2,1,0:T(8,128)(2,1)} %fusion.29), calls=%async_computation.1 | async-start | bytes 3145728 | tf_op jit(solution)/shard_map/all_to_all | solution.py:199
  545.6 495.1 %all-reduce.16.cloned.1.call-start = ((), (), s32[]{:S(2)}) async-start(), calls=%async_computation.44 | async-start | bytes 7077888 | tf_op jit(solution)/shard_map/psum | solution.py:407
  (71 other events, 2443.9 us)
Sparse Core Ops, SparseCore 0:
  71.2 23.8 all-gather.26
  96.5 32.0 all-gather.40
  130.0 28.5 all-gather.36
  160.1 28.5 all-gather.34
  190.2 28.5 all-gather.44
  220.4 28.5 all-gather.42
  250.3 28.5 all-gather.28
  280.5 28.5 all-gather.30
  310.5 28.5 all-gather.46
  340.6 28.5 all-gather.48
  370.6 28.5 all-gather.50
  419.4 28.5 all-gather.38
  451.0 26.0 reduce-scatter.16
  480.3 25.6 reduce-scatter.10
  509.1 25.7 reduce-scatter.12
  538.0 25.7 reduce-scatter.14
  566.3 37.9 reduce-scatter.18
  607.0 37.9 reduce-scatter.20
  647.5 37.9 reduce-scatter.22
  687.0 28.5 all-gather.32
  775.3 37.9 reduce-scatter.24
  815.8 37.9 reduce-scatter.26
  856.3 37.9 reduce-scatter.28
  898.8 141.8 all-reduce.15
  (7 shorter events, 126.4 us)
where the time goes:
time: 1070 us; the launch traced here: 1060 us
  waiting for transfers between devices  688 us (64%)
  matrix products  169 us (16%)
  other arithmetic  55.3 us (5%)
  starting transfers between devices  52.2 us (5%)
  local copies, waits for them, and re-layouts  43.2 us (4%)
  blocking collectives  34.8 us (3%)
  between operations  17.2 us (2%)
    psum x1, waiting for transfers between devices, shards(): lax.psum(pieces[2].astype(jnp.bfloat16), 'expert').astype(jnp.float32)  144 us
    dot_general x21, matrix products, dense_product(): return jnp.dot(left, right, preferred_element_type=jnp.float32)  58 us
    ppermute x12, waiting for transfers between devices, from_behind(): lax.ppermute(value, axis, [(source, source + steps) for source in range(f...  43.1 us
    reduce_scatter x1, waiting for transfers between devices, shards(): lax.psum_scatter(shared_up_grad.astype(jnp.bfloat16), 'shard', scatter_di...  40.7 us
    reduce_scatter x1, waiting for transfers between devices, shards(): lax.psum_scatter(shared_gate_grad.astype(jnp.bfloat16), 'shard', scatter_...  40.5 us
    reduce_scatter x1, waiting for transfers between devices, shards(): lax.psum_scatter(shared_down_grad.astype(jnp.bfloat16), 'shard', scatter_...  40.5 us
    reduce_scatter x1, waiting for transfers between devices, shards(): lax.psum_scatter(expert_up_grad[None].astype(jnp.bfloat16), 'shard', scat...  38.1 us
    reduce_scatter x1, waiting for transfers between devices, shards(): lax.psum_scatter(expert_down_grad[None].astype(jnp.bfloat16), 'shard', sc...  38 us
  transfers between devices with their start and end apart: 47, of which 31 were waited for; matrix products, arithmetic and copies ran while one was open for 24% of the time, Pallas kernels for 0%

commit v1 on v0

--- a/solution.py
+++ b/solution.py
@@ -1,11 +1,20 @@
+import functools
+
 import jax
 import jax.numpy as jnp
 from jax import lax
+from jax.experimental import pallas as pl
+from jax.experimental.pallas import tpu as pltpu
 from jax.sharding import PartitionSpec as P
 
 HEADS = 12
 TOP = 2
 WINDOW = 1024
+MESH = pl.DeviceIdType.MESH
+NAMES = ("wq", "wk", "wv", "wo", "gains", "sg", "su", "sd", "eg", "eu", "ed")
+EARLY = ("wq", "wk", "wv")
+SPREAD = ("wo", "gains", "sg", "su", "sd")
+LATE = ("eg", "eu", "ed")
 
 
 norm_eps = 1e-06
@@ -50,6 +59,308 @@
     grad_gate = grad_middle * up_pre * sigmoid_gate * (1.0 + gate_pre * (1.0 - sigmoid_gate))
     grad_up = grad_middle * activated
     return (grad_gate.astype(jnp.bfloat16), grad_up.astype(jnp.bfloat16))
+
+
+def gather_kernel(*refs):
+    count = len(NAMES)
+    own = dict(zip(NAMES, refs[:count]))
+    full = dict(zip(NAMES, refs[count : 2 * count]))
+    (own_sem, y_send, y_recv, x_send, x_recv, z_send, z_recv, core_send, core_recv) = refs[2 * count :]
+    number = {name: index for index, name in enumerate(NAMES)}
+    expert, shard = (lax.axis_index("expert"), lax.axis_index("shard"))
+    zed, ex = (expert // 2, expert % 2)
+    other = (shard + 2) % 4
+    y_peer = (expert, other)
+    core_peer = (expert, shard + 1 - 2 * (shard % 2))
+    x_peer = (expert + 1 - 2 * ex, shard)
+    z_up, z_down = (((expert + 2) % 8, shard), ((expert + 6) % 8, shard))
+
+    barrier = pltpu.get_barrier_semaphore()
+    for peer in (y_peer, core_peer, x_peer):
+        pl.semaphore_signal(barrier, inc=1, device_id=peer, device_id_type=MESH)
+
+    @pl.when(zed < 3)
+    def _():
+        pl.semaphore_signal(barrier, inc=1, device_id=z_up, device_id_type=MESH)
+
+    @pl.when(zed > 0)
+    def _():
+        pl.semaphore_signal(barrier, inc=1, device_id=z_down, device_id_type=MESH)
+
+    pl.semaphore_wait(barrier, 3 + jnp.minimum(3 - zed, 1) + jnp.minimum(zed, 1))
+
+    def place(name, slot, at_z=None, at_x=None):
+        whole, rows = (full[name], own[name].shape[0])
+        base = slot * rows
+        if at_z is None and at_x is None:
+            return whole.at[pl.ds(base, rows)]
+        if name in EARLY:
+            return whole.at[pl.ds(base + at_x * (rows // 2), rows // 2)]
+        if name in ("sg", "su"):
+            width = whole.shape[1] // 4
+            if at_x is None:
+                return whole.at[pl.ds(base, rows), pl.ds(at_z * width, width)]
+            half = width // 2
+            return whole.at[pl.ds(base, rows), pl.ds(at_z * width + at_x * half, half)]
+        size = rows // 4
+        if name == "sd" and at_x is not None:
+            return whole.at[pl.ds(base + at_z * size + at_x * (size // 2), size // 2)]
+        return whole.at[pl.ds(base + at_z * size, size)]
+
+    def mine(name, at_z=None, at_x=None):
+        block, rows = (own[name], own[name].shape[0])
+        if at_z is None and at_x is None:
+            return block
+        if name in EARLY:
+            return block.at[pl.ds(at_x * (rows // 2), rows // 2)]
+        if name in ("sg", "su"):
+            half = block.shape[1] // 8
+            return block.at[:, pl.ds((at_z * 2 + at_x) * half, half)]
+        size = rows // 4
+        if name == "sd":
+            return block.at[pl.ds(at_z * size + at_x * (size // 2), size // 2)]
+        return block.at[pl.ds(at_z * size, size)]
+
+    def send(source, target, send_sem, recv_sem, peer):
+        copy = pltpu.make_async_remote_copy(
+            src_ref=source, dst_ref=target, send_sem=send_sem, recv_sem=recv_sem,
+            device_id=peer, device_id_type=MESH,
+        )
+        copy.start()
+        return copy
+
+    def wait_recv(target, recv_sem):
+        pltpu.make_async_remote_copy(
+            src_ref=target, dst_ref=target, send_sem=recv_sem, recv_sem=recv_sem,
+            device_id=core_peer, device_id_type=MESH,
+        ).wait_recv()
+
+    def wait_send(source, send_sem):
+        pltpu.make_async_remote_copy(
+            src_ref=source, dst_ref=source, send_sem=send_sem, recv_sem=send_sem,
+            device_id=core_peer, device_id_type=MESH,
+        ).wait_send()
+
+    def cross(name, at_z=None, at_x=None):
+        n = number[name]
+        send(mine(name, at_z, at_x), place(name, shard, at_z, at_x), y_send.at[n], y_recv.at[n], y_peer)
+
+    def to_core(name, step, at_z=None, at_x=None):
+        n = number[name]
+        part = place(name, other, at_z, at_x)
+        send(part, part, core_send.at[n, 1 + step], core_recv.at[n, 1 + step], core_peer)
+
+    split_x = tuple(name for name in ("sg", "su", "sd") if name in SPREAD)
+    for name in EARLY:
+        cross(name, None, ex)
+    for name in SPREAD:
+        cross(name, zed, ex if name in split_x else None)
+    for name in NAMES:
+        n = number[name]
+        send(own[name], place(name, shard), core_send.at[n, 0], core_recv.at[n, 0], core_peer)
+        pltpu.make_async_copy(own[name], place(name, shard), own_sem.at[n]).start()
+
+    for name in EARLY:
+        n = number[name]
+        part = place(name, other, None, ex)
+        wait_recv(part, y_recv.at[n])
+        send(part, part, x_send.at[n, 0], x_recv.at[n, 0], x_peer)
+        to_core(name, 0, None, ex)
+    for name in LATE:
+        cross(name)
+    for name in EARLY:
+        n = number[name]
+        wait_recv(place(name, other, None, 1 - ex), x_recv.at[n, 0])
+        to_core(name, 1, None, 1 - ex)
+
+    def on_part(name, at_z, step):
+        n = number[name]
+        at_x = ex if name in split_x else None
+        part = place(name, other, at_z, at_x)
+        if name in split_x:
+            send(part, part, x_send.at[n, step], x_recv.at[n, step], x_peer)
+        to_core(name, step, at_z, at_x)
+
+    for name in SPREAD:
+        n = number[name]
+        wait_recv(place(name, other, zed, ex if name in split_x else None), y_recv.at[n])
+    for step in range(3):
+        def forward(direction, cond, at_z, peer):
+            @pl.when(cond)
+            def _():
+                for name in SPREAD:
+                    n = number[name]
+                    part = place(name, other, at_z, ex if name in split_x else None)
+                    send(part, part, z_send.at[n, direction, step], z_recv.at[n, direction, step], peer)
+
+        forward(0, (zed < 3) & (zed >= step), zed - step, z_up)
+        forward(1, (zed > 0) & (zed + step <= 3), zed + step, z_down)
+        if step == 0:
+            for name in SPREAD:
+                on_part(name, zed, 0)
+
+        def arrived(direction, cond, at_z):
+            @pl.when(cond)
+            def _():
+                for name in SPREAD:
+                    n = number[name]
+                    at_x = ex if name in split_x else None
+                    wait_recv(place(name, other, at_z, at_x), z_recv.at[n, direction, step])
+                    on_part(name, at_z, 1 + direction * 3 + step)
+
+        arrived(0, zed >= step + 1, zed - 1 - step)
+        arrived(1, zed + 1 + step <= 3, zed + 1 + step)
+
+    def from_x(cond, at_z, step):
+        @pl.when(cond)
+        def _():
+            for name in split_x:
+                n = number[name]
+                wait_recv(place(name, other, at_z, 1 - ex), x_recv.at[n, step])
+                to_core(name, 7 + step, at_z, 1 - ex)
+
+    from_x(zed >= 0, zed, 0)
+    for step in range(3):
+        from_x(zed >= step + 1, zed - 1 - step, 1 + step)
+        from_x(zed + 1 + step <= 3, zed + 1 + step, 4 + step)
+
+    for name in LATE:
+        n = number[name]
+        wait_recv(place(name, other), y_recv.at[n])
+        to_core(name, 0)
+
+    far = shard + 1 - 2 * (shard % 2)
+    far_other = (far + 2) % 4
+    for name in NAMES:
+        n = number[name]
+        pltpu.make_async_copy(own[name], place(name, shard), own_sem.at[n]).wait()
+        wait_recv(place(name, far), core_recv.at[n, 0])
+        wait_send(own[name], core_send.at[n, 0])
+
+    def finish(name, step, at_z, at_x):
+        n = number[name]
+        wait_recv(place(name, far_other, at_z, at_x), core_recv.at[n, 1 + step])
+        wait_send(place(name, other, at_z, at_x), core_send.at[n, 1 + step])
+
+    for name in EARLY:
+        n = number[name]
+        wait_send(mine(name, None, ex), y_send.at[n])
+        wait_send(place(name, other, None, ex), x_send.at[n, 0])
+        finish(name, 0, None, ex)
+        finish(name, 1, None, 1 - ex)
+    for name in LATE:
+        n = number[name]
+        wait_send(own[name], y_send.at[n])
+        finish(name, 0, None, None)
+
+    def finish_spread(cond, at_z, step):
+        @pl.when(cond)
+        def _():
+            for name in SPREAD:
+                n = number[name]
+                at_x = ex if name in split_x else None
+                finish(name, step, at_z, at_x)
+                if name in split_x:
+                    wait_send(place(name, other, at_z, ex), x_send.at[n, step])
+                    finish(name, 7 + step, at_z, 1 - ex)
+
+    for name in SPREAD:
+        n = number[name]
+        wait_send(mine(name, zed, ex if name in split_x else None), y_send.at[n])
+    finish_spread(zed >= 0, zed, 0)
+    for step in range(3):
+        finish_spread(zed >= step + 1, zed - 1 - step, 1 + step)
+        finish_spread(zed + 1 + step <= 3, zed + 1 + step, 4 + step)
+
+        def sent(direction, cond, at_z):
+            @pl.when(cond)
+            def _():
+                for name in SPREAD:
+                    n = number[name]
+                    at_x = ex if name in split_x else None
+                    wait_send(place(name, other, at_z, at_x), z_send.at[n, direction, step])
+
+        sent(0, (zed < 3) & (zed >= step), zed - step)
+        sent(1, (zed > 0) & (zed + step <= 3), zed + step)
+
+
+def gather_weights(blocks):
+    count = len(NAMES)
+    shapes = [jax.ShapeDtypeStruct((4 * block.shape[0], block.shape[1]), block.dtype) for block in blocks]
+    dma = pltpu.SemaphoreType.DMA
+    return pl.pallas_call(
+        gather_kernel,
+        out_shape=shapes,
+        in_specs=[pl.BlockSpec(memory_space=pltpu.VMEM)] * count,
+        out_specs=[pl.BlockSpec(memory_space=pl.ANY)] * count,
+        scratch_shapes=[
+            dma((count,)), dma((count,)), dma((count,)), dma((count, 7)), dma((count, 7)),
+            dma((count, 2, 3)), dma((count, 2, 3)), dma((count, 15)), dma((count, 15)),
+        ],
+        compiler_params=pltpu.CompilerParams(collective_id=0, has_side_effects=True, vmem_limit_bytes=48 << 20),
+        cost_estimate=pl.CostEstimate(flops=0, bytes_accessed=47000000, transcendentals=0),
+    )(*blocks)
+
+
+def whole_weights(gain_attn, gain_ffn, dense, experts):
+    expert_count, shard_count = (lax.axis_size("expert"), lax.axis_size("shard"))
+    if (expert_count, shard_count) == (8, 4):
+        gains = jnp.zeros((64, gain_attn.shape[0]), jnp.bfloat16)
+        gains = gains.at[0].set(gain_attn).at[1].set(gain_ffn)
+        blocks = dense[:4] + (gains,) + dense[4:] + tuple(weight[0] for weight in experts)
+        out = gather_weights(blocks)
+        gains = out[4].reshape(4, 64, -1)[:, :2].transpose(1, 0, 2).reshape(2, -1)
+        return gains, tuple(out[:4]) + tuple(out[5:8]), tuple(out[8:])
+    gather = functools.partial(lax.all_gather, axis_name="shard", tiled=True)
+    gains = jnp.stack([gather(gain_attn), gather(gain_ffn)])
+    return gains, tuple(gather(weight) for weight in dense), tuple(gather(weight[0]) for weight in experts)
+
+
+def swap(value, axis, bit):
+    size = lax.axis_size(axis)
+    return lax.ppermute(value, axis, [(index, index ^ bit) for index in range(size)])
+
+
+def halves(value, bit_set, dim):
+    half = value.shape[dim] // 2
+    keep = lax.dynamic_slice_in_dim(value, bit_set * half, half, dim)
+    give = lax.dynamic_slice_in_dim(value, (1 - bit_set) * half, half, dim)
+    return keep, give
+
+
+def fold(value, axis, bit, dim):
+    bit_set = (lax.axis_index(axis) // bit) % 2
+    keep, give = halves(value, bit_set, dim)
+    return (keep.astype(jnp.float32) + swap(give.astype(jnp.bfloat16), axis, bit).astype(jnp.float32)).astype(jnp.bfloat16)
+
+
+def unfold(value, axis, bit, dim):
+    bit_set = (lax.axis_index(axis) // bit) % 2
+    come = swap(value, axis, bit)
+    return jnp.where(bit_set == 0, jnp.concatenate([value, come], dim), jnp.concatenate([come, value], dim))
+
+
+def bits_of(axis):
+    size = lax.axis_size(axis)
+    return [1 << place for place in range(size.bit_length() - 1)]
+
+
+def scatter_shards(value):
+    count = lax.axis_size("shard")
+    blocks = value.reshape((count // 2, 2, value.shape[0] // count) + value.shape[1:])
+    blocks = fold(blocks, "shard", 1, 1)[:, 0]
+    for bit in reversed(bits_of("shard")[1:]):
+        blocks = fold(blocks, "shard", bit, 0)
+    return blocks[0]
+
+
+def sum_plane(value, dim):
+    bits = bits_of("expert")
+    for bit in bits:
+        value = fold(value, "expert", bit, dim)
+    for bit in reversed(bits):
+        value = unfold(value, "expert", bit, dim)
+    return value.astype(jnp.float32)
 
 
 def shards(
@@ -84,27 +395,19 @@
     key_rows = (key_reach + 1) * tokens
     score_scale = head_size ** (-0.5)
     head_shape = (tokens, HEADS, head_size)
-    dense_all = (
-        lax.all_gather(gain_attn, "shard", axis=0, tiled=True),
-        lax.all_gather(gain_ffn, "shard", axis=0, tiled=True),
-        lax.all_gather(w_query, "shard", axis=0, tiled=True),
-        lax.all_gather(w_key, "shard", axis=0, tiled=True),
-        lax.all_gather(w_value, "shard", axis=0, tiled=True),
-        lax.all_gather(w_out, "shard", axis=0, tiled=True),
-        lax.all_gather(shared_gate, "shard", axis=0, tiled=True),
-        lax.all_gather(shared_up, "shard", axis=0, tiled=True),
-        lax.all_gather(shared_down, "shard", axis=0, tiled=True),
-    )
-    expert_all = (
-        lax.all_gather(expert_gate, "shard", axis=1, tiled=True),
-        lax.all_gather(expert_up, "shard", axis=1, tiled=True),
-        lax.all_gather(expert_down, "shard", axis=1, tiled=True),
-    )
+    gains, dense_all, expert_all = whole_weights(
+        gain_attn,
+        gain_ffn,
+        (w_query, w_key, w_value, w_out, shared_gate, shared_up, shared_down),
+        (expert_gate, expert_up, expert_down),
+    )
+    dense_all = (gains[0], gains[1]) + dense_all
+    dense_back = dense_all
     gain_first = dense_all[0].astype(jnp.float32)
     gain_second = dense_all[1].astype(jnp.float32)
-    gate_expert_all = expert_all[0][0]
-    up_expert_all = expert_all[1][0]
-    down_expert_all = expert_all[2][0]
+    gate_expert_all = expert_all[0]
+    up_expert_all = expert_all[1]
+    down_expert_all = expert_all[2]
     rows_in = hidden_in[0].astype(jnp.float32)
     scale_first = rms_scale(rows_in)
     normed = (rows_in * scale_first * gain_first).astype(bfloat)
@@ -218,42 +521,9 @@
     )
     route_padded = jnp.concatenate([route_grad, jnp.zeros((1, model_width), bfloat)], axis=0)
     send_grad = route_padded[slot_table].reshape(experts, capacity, model_width)
-    held_weights = lax.optimization_barrier(
-        (
-            gain_attn,
-            gain_ffn,
-            w_query,
-            w_key,
-            w_value,
-            w_out,
-            shared_gate,
-            shared_up,
-            shared_down,
-            expert_gate,
-            expert_up,
-            expert_down,
-            send_grad,
-        )
-    )
-    dense_back = (
-        lax.all_gather(held_weights[0], "shard", axis=0, tiled=True),
-        lax.all_gather(held_weights[1], "shard", axis=0, tiled=True),
-        lax.all_gather(held_weights[2], "shard", axis=0, tiled=True),
-        lax.all_gather(held_weights[3], "shard", axis=0, tiled=True),
-        lax.all_gather(held_weights[4], "shard", axis=0, tiled=True),
-        lax.all_gather(held_weights[5], "shard", axis=0, tiled=True),
-        lax.all_gather(held_weights[6], "shard", axis=0, tiled=True),
-        lax.all_gather(held_weights[7], "shard", axis=0, tiled=True),
-        lax.all_gather(held_weights[8], "shard", axis=0, tiled=True),
-    )
-    expert_back = (
-        lax.all_gather(held_weights[9], "shard", axis=1, tiled=True),
-        lax.all_gather(held_weights[10], "shard", axis=1, tiled=True),
-        lax.all_gather(held_weights[11], "shard", axis=1, tiled=True),
-    )
-    gate_expert_back = expert_back[0][0]
-    up_expert_back = expert_back[1][0]
-    down_expert_back = expert_back[2][0]
+    gate_expert_back = gate_expert_all
+    up_expert_back = up_expert_all
+    down_expert_back = down_expert_all
     grad_received = lax.all_to_all(send_grad, "expert", split_axis=0, concat_axis=0, tiled=True)
     received = outcome[1]
     gate_pre = outcome[2]
@@ -279,16 +549,9 @@
         + jnp.einsum("sif,df->sid", grad_up_pre, up_expert_back, preferred_element_type=jnp.float32)
     ).astype(bfloat)
     grad_back = lax.all_to_all(grad_rows, "expert", split_axis=0, concat_axis=0, tiled=True)
-    expert_grads = (
-        lax.psum_scatter(
-            expert_gate_grad[None].astype(jnp.bfloat16), "shard", scatter_dimension=1, tiled=True
-        ).astype(jnp.float32),
-        lax.psum_scatter(
-            expert_up_grad[None].astype(jnp.bfloat16), "shard", scatter_dimension=1, tiled=True
-        ).astype(jnp.float32),
-        lax.psum_scatter(
-            expert_down_grad[None].astype(jnp.bfloat16), "shard", scatter_dimension=1, tiled=True
-        ).astype(jnp.float32),
+    expert_grads = tuple(
+        scatter_shards(grad.astype(bfloat))[None].astype(jnp.float32)
+        for grad in (expert_gate_grad, expert_up_grad, expert_down_grad)
     )
     grad_routes = (
         grad_back.reshape(experts * capacity, model_width)[places]
@@ -372,45 +635,21 @@
         + scale_first * scaled_first
         - rows_in * scale_first**3 * jnp.mean(scaled_first * rows_in, axis=-1, keepdims=True)
     )
-    pieces = (
-        lax.psum_scatter(
-            gain_attn_grad.astype(jnp.bfloat16), "shard", scatter_dimension=0, tiled=True
-        ).astype(jnp.float32),
-        lax.psum_scatter(
-            gain_ffn_grad.astype(jnp.bfloat16), "shard", scatter_dimension=0, tiled=True
-        ).astype(jnp.float32),
-        lax.psum_scatter(
-            w_query_grad.astype(jnp.bfloat16), "shard", scatter_dimension=0, tiled=True
-        ).astype(jnp.float32),
-        lax.psum_scatter(
-            w_key_grad.astype(jnp.bfloat16), "shard", scatter_dimension=0, tiled=True
-        ).astype(jnp.float32),
-        lax.psum_scatter(
-            w_value_grad.astype(jnp.bfloat16), "shard", scatter_dimension=0, tiled=True
-        ).astype(jnp.float32),
-        lax.psum_scatter(
-            w_out_grad.astype(jnp.bfloat16), "shard", scatter_dimension=0, tiled=True
-        ).astype(jnp.float32),
-        lax.psum_scatter(
-            shared_gate_grad.astype(jnp.bfloat16), "shard", scatter_dimension=0, tiled=True
-        ).astype(jnp.float32),
-        lax.psum_scatter(
-            shared_up_grad.astype(jnp.bfloat16), "shard", scatter_dimension=0, tiled=True
-        ).astype(jnp.float32),
-        lax.psum_scatter(
-            shared_down_grad.astype(jnp.bfloat16), "shard", scatter_dimension=0, tiled=True
-        ).astype(jnp.float32),
-    )
+    gain_rows = jnp.stack([gain_attn_grad, gain_ffn_grad], axis=1).astype(bfloat)
+    gain_total = lax.psum(scatter_shards(gain_rows), "expert").astype(jnp.float32)
+    attn_grads = jnp.stack([w_query_grad, w_key_grad, w_value_grad, w_out_grad]).astype(bfloat)
+    attn_rows = scatter_shards(attn_grads.transpose(1, 0, 2)).transpose(1, 0, 2)
+    attn_total = sum_plane(attn_rows.reshape(-1, model_width), 0).reshape(attn_rows.shape)
     totals = (
-        lax.psum(pieces[0].astype(jnp.bfloat16), "expert").astype(jnp.float32),
-        lax.psum(pieces[1].astype(jnp.bfloat16), "expert").astype(jnp.float32),
-        lax.psum(pieces[2].astype(jnp.bfloat16), "expert").astype(jnp.float32),
-        lax.psum(pieces[3].astype(jnp.bfloat16), "expert").astype(jnp.float32),
-        lax.psum(pieces[4].astype(jnp.bfloat16), "expert").astype(jnp.float32),
-        lax.psum(pieces[5].astype(jnp.bfloat16), "expert").astype(jnp.float32),
-        lax.psum(pieces[6].astype(jnp.bfloat16), "expert").astype(jnp.float32),
-        lax.psum(pieces[7].astype(jnp.bfloat16), "expert").astype(jnp.float32),
-        lax.psum(pieces[8].astype(jnp.bfloat16), "expert").astype(jnp.float32),
+        gain_total[:, 0],
+        gain_total[:, 1],
+        attn_total[0],
+        attn_total[1],
+        attn_total[2],
+        attn_total[3],
+        sum_plane(scatter_shards(shared_gate_grad.astype(bfloat)), 1),
+        sum_plane(scatter_shards(shared_up_grad.astype(bfloat)), 1),
+        sum_plane(scatter_shards(shared_down_grad.astype(bfloat)), 0),
     )
     return (
         output[None],

time: 1070 us -> 674 us (0.63)
  waiting for transfers between devices: 688 us -> 202 us
  Pallas kernels: 0 us -> 81.4 us
  matrix products: 169 us -> 117 us
  starting transfers between devices: 52.2 us -> 97.4 us
  local copies, waits for them, and re-layouts: 43.2 us -> 82.6 us
  blocking collectives: 34.8 us -> 19.9 us
  between operations: 17.2 us -> 2.79 us
    all_gather x20 -> x0, waiting for transfers between devices: 257 us -> none  [the longest x1 26 us: shards(): lax.all_gather(shared_up, 'shard', axis=0, tiled=True)]
    reduce_scatter x10 -> x0, waiting for transfers between devices: 225 us -> none  [the longest x1 40.7 us: shards(): lax.psum_scatter(shared_up_grad.astype(jnp.bfloat16), 'shard', scatter_di...]
    ppermute x0 -> x40, waiting for transfers between devices: none -> 177 us  [swap(): lax.ppermute(value, axis, [(index, index ^ bit) for index in range(size)])]
    psum x1 -> x0, waiting for transfers between devices: 144 us -> none  [shards(): lax.psum(pieces[2].astype(jnp.bfloat16), 'expert').astype(jnp.float32)]
    pallas_call x0 -> x1, Pallas kernels: none -> 81.4 us  [gather_weights(): pl.pallas_call(gather_kernel, out_shape=shapes, in_specs=[pl.BlockSpec(me...]
    ppermute x0 -> x40, starting transfers between devices: none -> 46.5 us  [swap(): lax.ppermute(value, axis, [(index, index ^ bit) for index in range(size)])]
    dot_general x21, matrix products: 58 us -> 26.3 us  [dense_product(): return jnp.dot(left, right, preferred_element_type=jnp.float32)]
    unnamed x109 -> x244, local copies, waits for them, and re-layouts: 7.57 us -> 27.1 us
  transfers between devices with their start and end apart: 47 -> 56, of which waited for: 31 -> 26; matrix products, arithmetic and copies ran while one was open for 24% -> 34% of each run, Pallas kernels for 0% -> 0%
where the time goes in v1:
time: 674 us; the launch traced here: 668 us
  waiting for transfers between devices  202 us (30%)
  matrix products  117 us (17%)
  starting transfers between devices  97.4 us (14%)
  local copies, waits for them, and re-layouts  82.6 us (12%)
  Pallas kernels  81.4 us (12%)
  other arithmetic  65 us (10%)
  blocking collectives  19.9 us (3%)
    ppermute x40, waiting for transfers between devices, swap(): lax.ppermute(value, axis, [(index, index ^ bit) for index in range(size)])  177 us
    pallas_call x1, Pallas kernels, gather_weights(): pl.pallas_call(gather_kernel, out_shape=shapes, in_specs=[pl.BlockSpec(me...  81.4 us
    ppermute x40, starting transfers between devices, swap(): lax.ppermute(value, axis, [(index, index ^ bit) for index in range(size)])  46.5 us
    ppermute x12, starting transfers between devices, from_behind(): lax.ppermute(value, axis, [(source, source + steps) for source in range(f...  31.5 us
    unnamed x244, local copies, waits for them, and re-layouts  27.1 us
    dot_general x21, matrix products, dense_product(): return jnp.dot(left, right, preferred_element_type=jnp.float32)  26.3 us
    ppermute x12, waiting for transfers between devices, from_behind(): lax.ppermute(value, axis, [(source, source + steps) for source in range(f...  24.9 us
    convert_element_type x25, other arithmetic, fold(): (keep.astype(jnp.float32) + swap(give.astype(jnp.bfloat16), axis, bit).as...  20.9 us
  transfers between devices with their start and end apart: 56, of which 26 were waited for; matrix products, arithmetic and copies ran while one was open for 34% of the time, Pallas kernels for 0%

profile of v1, /device:TPU:0, one launch (start us, length us, event | category | flops | bytes accessed | tf_op | source)
XLA Modules:
  0.0 668.1 jit_solution(15162909227817259399)
XLA Ops:
  12.7 81.4 %shard_map.289 = (bf16[768,768]{1,0:T(8,128)(2,1)}, bf16[768,768]{1,0:T(8,128)(2,1)}, bf16[768,768]{1,0:T(8,128)(2,1)}, bf16[768,768]{1,0:T(8,128)(2,1)}, bf16[2...) custom-call(bf16[192,768]{1,0:T(8,128)(2,1)S(1)} %copy-done.6, ...), custom_call_target="tpu_custom_call" | custom-call | bytes 47000000 | tf_op jit(solution)/shard_map/pallas_call | solution.py:291
  128.9 5.9 all-to-all-start.2
  137.6 12.3 %collective-permute-start.5 = (bf16[256,768]{0,1:T(8,128)(2,1)}, bf16[256,768]{0,1:T(8,128)(2,1)}, u32[]{:S(2)}, u32[]{:S(2)}) collective-permute-start(bf16[256,768]{0,1:T(8,128)(2,1)} %bitcast.16), channel_id=1, source_target_pairs={{0,1},{1,2},{2,3},{4,5},{5,6},{6,7},{8,9},{9,10},{10,11},{12,13},{... | collective-permute-start | bytes 1179656 | tf_op jit(solution)/shard_map/ppermute | solution.py:28
  202.1 6.2 all-to-all-start
  219.6 13.5 %collective-permute-done.31 = bf16[1,192,2048]{2,1,0:T(8,128)(2,1)} collective-permute-done((bf16[1,192,2048]{2,1,0:T(8,128)(2,1)}, bf16[1,192,2048]{2,1,0:T(8,128)(2,1)}, u32[]{:S(2)}, u32[]{:S(2)}) %collective-permute-start.31) | collective-permute-done | bytes 786464 | tf_op jit(solution)/shard_map/ppermute | solution.py:321
  237.2 12.0 %collective-permute-done.23 = bf16[1,192,2048]{2,1,0:T(8,128)(2,1)S(1)} collective-permute-done((bf16[1,192,2048]{2,1,0:T(8,128)(2,1)S(1)}, bf16[1,192,2048]{2,1,0:T(8,128)(2,1)S(1)}, u32[]{:S(2)}, u32[]{:S(2)}) %collective-permute-start.23) | collective-permute-done | bytes 786464 | tf_op jit(solution)/shard_map/ppermute | solution.py:321
  252.1 7.0 %fusion.8 = f32[8,128,2048]{2,1,0:T(8,128)} fusion(bf16[8,128,768]{2,1,0:T(8,128)(2,1)} %all-to-all-done.2, bf16[2048,768]{1,0:T(8,128)(2,1)S(1)} %copy-done.112), kind=kOutput, calls=%fused_computation.30 | convolution fusion | flops 3221225472 | bytes 13107200 | tf_op jit(solution)/shard_map/sid,fd->sif/dot_general | solution.py:532
  259.1 9.3 %fusion.14 = f32[8,128,2048]{2,1,0:T(8,128)} fusion(bf16[8,128,768]{2,1,0:T(8,128)(2,1)} %all-to-all-done, bf16[768,2048]{1,0:T(8,128)(2,1)} %get-tuple-element.59), kind=kOutput, calls=%fused_computation.36 | convolution fusion | flops 3221225472 | bytes 13107200 | tf_op jit(solution)/shard_map/sid,df->sif/dot_general | solution.py:497
  268.4 13.1 %multiply_convert_fusion.2 = (bf16[8,128,2048]{2,1,0:T(8,128)(2,1)S(1)}, bf16[8,128,2048]{2,1,0:T(8,128)(2,1)}, bf16[8,128,2048]{2,1,0:T(8,128)(2,1)}) fusion(f32[8,128,2048]{2,1,0:T(8,128)} %fusion.8, f32[8,128,2048]{2,1,0:T(8,128)} %fusion.14, bf16[8,128,768]{2,1,0:T(8,128)(2,1)} %all-to-all-done, bf16[768,2048]{1,0:T(8,128)(2,1)S(1)} %copy-done.110), kind=kOutput, calls=%fused_computation.14 | convolution fusion | flops 3252682752 | bytes 34078720 | tf_op jit(solution)/shard_map/sid,df->sif/dot_general | solution.py:494
  281.5 8.3 %fusion.27 = bf16[8,128,768]{2,1,0:T(8,128)(2,1)} fusion(bf16[8,128,2048]{2,1,0:T(8,128)(2,1)} %get-tuple-element.86, bf16[2048,768]{1,0:T(8,128)(2,1)S(1)} %copy-done.113), kind=kOutput, calls=%fused_computation.62 | convolution fusion | flops 3222011904 | bytes 8912896 | tf_op jit(solution)/shard_map/sif,fd->sid/dot_general | solution.py:499
  322.9 6.1 bitcast_convert_fusion.2
  337.4 33.4 %collective-permute-done.42 = bf16[64,768]{1,0:T(8,128)(2,1)S(1)} collective-permute-done((bf16[64,768]{1,0:T(8,128)(2,1)S(1)}, bf16[64,768]{1,0:T(8,128)(2,1)S(1)}, u32[]{:S(2)}, u32[]{:S(2)}) %collective-permute-start.42) | collective-permute-done | bytes 98336 | tf_op jit(solution)/shard_map/ppermute | solution.py:321
  370.9 6.2 collective-permute-done.34
  403.2 7.0 %collective-permute-done.37 = bf16[192,1024]{1,0:T(8,128)(2,1)S(1)} collective-permute-done((bf16[192,1024]{1,0:T(8,128)(2,1)S(1)}, bf16[192,1024]{1,0:T(8,128)(2,1)S(1)}, u32[]{:S(2)}, u32[]{:S(2)}) %collective-permute-start.37) | collective-permute-done | bytes 393248 | tf_op jit(solution)/shard_map/ppermute | solution.py:321
  439.6 12.0 %multiply_reduce_fusion = (f32[12,256]{1,0:T(8,128)S(1)}, f32[12,256,1024]{2,1,0:T(8,128)}) fusion(f32[12,256]{1,0:T(8,128)S(1)} %log_add_fusion, f32[12,256,1024]{2,1,0:T(8,128)} %copy-done.10, pred[256,1024]{1,0:T(8,128)(4,1)S(1)} %copy-done.27, bf16[256,12,64]{0,2,1:T(8,128)(2,1)} %bitcast.333, bf16[1024,12,64]{0,2,1:T(8,128)(2,1)} %bitcast.323), kind=kOutput, calls=%fused_computation.6 | convolution fusion | flops 418378752 | bytes 27418624 | tf_op jit(solution)/shard_map/qhd,khd->hqk/dot_general | solution.py:587
  452.8 7.1 %multiply_convert_fusion = bf16[12,256,1024]{2,1,0:T(8,128)(2,1)S(1)} fusion(f32[12,256,1024]{2,1,0:T(8,128)} %get-tuple-element.127, f32[12,256]{1,0:T(8,128)S(1)} %get-tuple-element.126, f32[12,256]{1,0:T(8,128)S(1)} %log_add_fusion, f32[12,256,1024]{2,1,0:T(8,128)S(1)} %bitcast.309, pred[256,1024]{1,0:T(8,128)(4,1)S(1)} %copy-done.27), kind=kLoop, calls=%fused_computation.5 | loop fusion | flops 18874368 | bytes 31744000 | tf_op jit(solution)/shard_map/convert_element_type | solution.py:591
  474.9 14.1 %collective-permute-done.7 = bf16[256,768]{0,1:T(8,128)(2,1)S(1)} collective-permute-done((bf16[256,768]{0,1:T(8,128)(2,1)S(1)}, bf16[256,768]{0,1:T(8,128)(2,1)S(1)}, u32[]{:S(2)}, u32[]{:S(2)}) %collective-permute-start.7) | collective-permute-done | bytes 393248 | tf_op jit(solution)/shard_map/ppermute | solution.py:28
  500.9 6.8 %collective-permute-done.11 = bf16[256,768]{0,1:T(8,128)(2,1)S(1)} collective-permute-done((bf16[256,768]{0,1:T(8,128)(2,1)S(1)}, bf16[256,768]{0,1:T(8,128)(2,1)S(1)}, u32[]{:S(2)}, u32[]{:S(2)}) %collective-permute-start.11) | collective-permute-done | bytes 393248 | tf_op jit(solution)/shard_map/ppermute | solution.py:28
  518.9 15.5 %collective-permute-done.49 = bf16[1,192,2048]{2,1,0:T(8,128)(2,1)S(1)} collective-permute-done((bf16[1,192,2048]{2,1,0:T(8,128)(2,1)S(1)}, bf16[1,192,2048]{2,1,0:T(8,128)(2,1)S(1)}, u32[]{:S(2)}, u32[]{:S(2)}) %collective-permute-start.49) | collective-permute-done | bytes 786464 | tf_op jit(solution)/shard_map/ppermute | solution.py:321
  537.6 30.6 %collective-permute-done.47 = bf16[1,192,2048]{2,1,0:T(8,128)(2,1)S(1)} collective-permute-done((bf16[1,192,2048]{2,1,0:T(8,128)(2,1)S(1)}, bf16[1,192,2048]{2,1,0:T(8,128)(2,1)S(1)}, u32[]{:S(2)}, u32[]{:S(2)}) %collective-permute-start.47) | collective-permute-done | bytes 786464 | tf_op jit(solution)/shard_map/ppermute | solution.py:321
  600.4 8.2 %collective-permute-done.16 = bf16[384,768]{1,0:T(8,128)(2,1)} collective-permute-done((bf16[384,768]{1,0:T(8,128)(2,1)}, bf16[384,768]{1,0:T(8,128)(2,1)}, u32[]{:S(2)}, u32[]{:S(2)}) %collective-permute-start.16) | collective-permute-done | bytes 589856 | tf_op jit(solution)/shard_map/ppermute | solution.py:321
  620.8 6.9 %collective-permute-done.18 = bf16[96,768]{1,0:T(8,128)(2,1)S(1)} collective-permute-done((bf16[96,768]{1,0:T(8,128)(2,1)S(1)}, bf16[96,768]{1,0:T(8,128)(2,1)S(1)}, u32[]{:S(2)}, u32[]{:S(2)}) %collective-permute-start.18) | collective-permute-done | bytes 147488 | tf_op jit(solution)/shard_map/ppermute | solution.py:321
  629.2 6.2 collective-permute-done.19
  645.7 19.9 %psum.7 = bf16[192,2]{0,1:T(2,128)(2,1)S(1)} all-reduce(bf16[192,2]{0,1:T(2,128)(2,1)S(1)} %bitcast.355), channel_id=1, replica_groups=mesh['expert'=8,'shard'=4] {'expert'}, use_global_device_ids=true, to_apply=%region_19.20 | all-reduce | flops 384 | bytes 1536 | tf_op jit(solution)/shard_map/psum | solution.py:639
  (531 shorter events, 316.2 us)
Async XLA Ops:
  99.5 53.8 %collective-permute-start.3 = (bf16[256,768]{0,1:T(8,128)(2,1)}, bf16[256,768]{0,1:T(8,128)(2,1)}, u32[]{:S(2)}, u32[]{:S(2)}) collective-permute-start(bf16[256,768]{0,1:T(8,128)(2,1)} %bitcast.16), channel_id=1, source_target_pairs={{0,3},{4,7},{8,11},{12,15},{16,19},{20,23},{24,27},{28,31}} | collective-permute-start | bytes 1179656 | tf_op jit(solution)/shard_map/ppermute | solution.py:28
  102.6 50.6 %collective-permute-start.4 = (bf16[256,768]{0,1:T(8,128)(2,1)}, bf16[256,768]{0,1:T(8,128)(2,1)}, u32[]{:S(2)}, u32[]{:S(2)}) collective-permute-start(bf16[256,768]{0,1:T(8,128)(2,1)} %bitcast.16), channel_id=1, source_target_pairs={{0,2},{1,3},{4,6},{5,7},{8,10},{9,11},{12,14},{13,15},{16,18},{17,... | collective-permute-start | bytes 1179656 | tf_op jit(solution)/shard_map/ppermute | solution.py:28
  105.9 31.6 %collective-permute-start = (bf16[256,768]{1,0:T(8,128)(2,1)}, bf16[256,768]{1,0:T(8,128)(2,1)}, u32[]{:S(2)}, u32[]{:S(2)}) collective-permute-start(bf16[256,768]{1,0:T(8,128)(2,1)} %convolution_convert_fusion.8), channel_id=1, source_target_pairs={{0,3},{4,7},{8,11},{12,15},{16,19},{20,23},{24,27},{28,31}} | collective-permute-start | bytes 1179656 | tf_op jit(solution)/shard_map/ppermute | solution.py:28
  108.0 42.1 %collective-permute-start.1 = (bf16[256,768]{1,0:T(8,128)(2,1)}, bf16[256,768]{1,0:T(8,128)(2,1)}, u32[]{:S(2)}, u32[]{:S(2)}) collective-permute-start(bf16[256,768]{1,0:T(8,128)(2,1)} %convolution_convert_fusion.8), channel_id=1, source_target_pairs={{0,2},{1,3},{4,6},{5,7},{8,10},{9,11},{12,14},{13,15},{16,18},{17,... | collective-permute-start | bytes 1179656 | tf_op jit(solution)/shard_map/ppermute | solution.py:28
  110.0 40.0 %collective-permute-start.2 = (bf16[256,768]{1,0:T(8,128)(2,1)}, bf16[256,768]{1,0:T(8,128)(2,1)}, u32[]{:S(2)}, u32[]{:S(2)}) collective-permute-start(bf16[256,768]{1,0:T(8,128)(2,1)} %convolution_convert_fusion.8), channel_id=1, source_target_pairs={{0,1},{1,2},{2,3},{4,5},{5,6},{6,7},{8,9},{9,10},{10,11},{12,13},{... | collective-permute-start | bytes 1179656 | tf_op jit(solution)/shard_map/ppermute | solution.py:28
  128.9 73.2 %all-to-all-start.2 = ((bf16[8,128,768]{2,1,0:T(8,128)(2,1)}), bf16[8,128,768]{2,1,0:T(8,128)(2,1)}, u32[]{:S(2)}, u32[]{:S(2)}) async-start(bf16[8,128,768]{2,1,0:T(8,128)(2,1)} %bitcast.34), calls=%async_computation.2 | async-start | bytes 3145728 | tf_op jit(solution)/shard_map/all_to_all | solution.py:527
  183.3 25.0 %collective-permute-start.22 = (bf16[2,1,192,2048]{3,2,1,0:T(8,128)(2,1)}, bf16[2,1,192,2048]{3,2,1,0:T(8,128)(2,1)}, u32[]{:S(2)}, u32[]{:S(2)}) collective-permute-start(bf16[2,1,192,2048]{3,2,1,0:T(8,128)(2,1)} %constant_dynamic-slice_fusion.11), channel_id=1, source_target_pairs={{0,1},{1,0},{2,3},{3,2},{4,5},{5,4},{6,7},{7,6},{8,9},{9,8},{10,11... | collective-permute-start | bytes 4718600 | tf_op jit(solution)/shard_map/ppermute | solution.py:321
  201.8 31.4 %collective-permute-start.31 = (bf16[1,192,2048]{2,1,0:T(8,128)(2,1)}, bf16[1,192,2048]{2,1,0:T(8,128)(2,1)}, u32[]{:S(2)}, u32[]{:S(2)}) collective-permute-start(bf16[1,192,2048]{2,1,0:T(8,128)(2,1)} %dynamic-slice_bitcast_fusion.5), channel_id=1, source_target_pairs={{0,2},{1,3},{2,0},{3,1},{4,6},{5,7},{6,4},{7,5},{8,10},{9,11},{10,... | collective-permute-start | bytes 2359304 | tf_op jit(solution)/shard_map/ppermute | solution.py:321
  202.1 57.0 %all-to-all-start = ((bf16[8,128,768]{2,1,0:T(8,128)(2,1)}), bf16[8,128,768]{2,1,0:T(8,128)(2,1)}, u32[]{:S(2)}, u32[]{:S(2)}) async-start(bf16[8,128,768]{2,1,0:T(8,128)(2,1)} %bitcast.322), calls=%async_computation | async-start | bytes 3145728 | tf_op jit(solution)/shard_map/all_to_all | solution.py:493
  210.5 38.8 %collective-permute-start.23 = (bf16[1,192,2048]{2,1,0:T(8,128)(2,1)S(1)}, bf16[1,192,2048]{2,1,0:T(8,128)(2,1)S(1)}, u32[]{:S(2)}, u32[]{:S(2)}) collective-permute-start(bf16[1,192,2048]{2,1,0:T(8,128)(2,1)S(1)} %dynamic-slice_bitcast_fusion.6), channel_id=1, source_target_pairs={{0,2},{1,3},{2,0},{3,1},{4,6},{5,7},{6,4},{7,5},{8,10},{9,11},{10,... | collective-permute-start | bytes 2359304 | tf_op jit(solution)/shard_map/ppermute | solution.py:321
  217.7 91.1 %collective-permute-start.40 = (bf16[256,768]{1,0:T(8,128)(2,1)S(1)}, bf16[256,768]{1,0:T(8,128)(2,1)S(1)}, u32[]{:S(2)}, u32[]{:S(2)}) collective-permute-start(bf16[256,768]{1,0:T(8,128)(2,1)S(1)} %dynamic-slice_bitcast_fusion.7), channel_id=1, source_target_pairs={{0,4},{4,0},{8,12},{12,8},{16,20},{20,16},{24,28},{28,24},{1,5},{5... | collective-permute-start | bytes 1179656 | tf_op jit(solution)/shard_map/ppermute | solution.py:321
  235.4 75.8 %collective-permute-start.32 = (bf16[192,1024]{1,0:T(8,128)(2,1)}, bf16[192,1024]{1,0:T(8,128)(2,1)S(1)}, u32[]{:S(2)}, u32[]{:S(2)}) collective-permute-start(bf16[192,1024]{1,0:T(8,128)(2,1)} %dynamic-slice_bitcast_fusion.8), channel_id=1, source_target_pairs={{0,4},{4,0},{8,12},{12,8},{16,20},{20,16},{24,28},{28,24},{1,5},{5... | collective-permute-start | bytes 1179656 | tf_op jit(solution)/shard_map/ppermute | solution.py:321
  250.3 61.6 %collective-permute-start.24 = (bf16[192,1024]{1,0:T(8,128)(2,1)}, bf16[192,1024]{1,0:T(8,128)(2,1)}, u32[]{:S(2)}, u32[]{:S(2)}) collective-permute-start(bf16[192,1024]{1,0:T(8,128)(2,1)} %dynamic-slice_bitcast_fusion.9), channel_id=1, source_target_pairs={{0,4},{4,0},{8,12},{12,8},{16,20},{20,16},{24,28},{28,24},{1,5},{5... | collective-permute-start | bytes 1179656 | tf_op jit(solution)/shard_map/ppermute | solution.py:321
  298.3 215.7 %collective-permute-start.50 = (bf16[2,1,512,768]{3,2,1,0:T(8,128)(2,1)}, bf16[2,1,512,768]{3,2,1,0:T(8,128)(2,1)}, u32[]{:S(2)}, u32[]{:S(2)}) collective-permute-start(bf16[2,1,512,768]{3,2,1,0:T(8,128)(2,1)} %constant_dynamic-slice_fusion), channel_id=1, source_target_pairs={{0,1},{1,0},{2,3},{3,2},{4,5},{5,4},{6,7},{7,6},{8,9},{9,8},{10,11... | collective-permute-start | bytes 4718600 | tf_op jit(solution)/shard_map/ppermute | solution.py:321
  308.8 201.4 %collective-permute-start.48 = (bf16[2,1,192,2048]{3,2,1,0:T(8,128)(2,1)}, bf16[2,1,192,2048]{3,2,1,0:T(8,128)(2,1)}, u32[]{:S(2)}, u32[]{:S(2)}) collective-permute-start(bf16[2,1,192,2048]{3,2,1,0:T(8,128)(2,1)} %constant_dynamic-slice_fusion.1), channel_id=1, source_target_pairs={{0,1},{1,0},{2,3},{3,2},{4,5},{5,4},{6,7},{7,6},{8,9},{9,8},{10,11... | collective-permute-start | bytes 4718600 | tf_op jit(solution)/shard_map/ppermute | solution.py:321
  319.2 98.6 %all-to-all-start.3 = ((bf16[8,128,768]{2,1,0:T(8,128)(2,1)}), bf16[8,128,768]{2,1,0:T(8,128)(2,1)S(1)}, u32[]{:S(2)}, u32[]{:S(2)}) async-start(bf16[8,128,768]{2,1,0:T(8,128)(2,1)} %add_convert_fusion.7), calls=%async_computation.3 | async-start | bytes 3145728 | tf_op jit(solution)/shard_map/all_to_all | solution.py:551
  330.3 40.5 %collective-permute-start.42 = (bf16[64,768]{1,0:T(8,128)(2,1)S(1)}, bf16[64,768]{1,0:T(8,128)(2,1)S(1)}, u32[]{:S(2)}, u32[]{:S(2)}) collective-permute-start(bf16[64,768]{1,0:T(8,128)(2,1)S(1)} %constant_dynamic-slice_fusion.3), channel_id=1, source_target_pairs={{0,16},{4,20},{8,24},{12,28},{16,0},{20,4},{24,8},{28,12},{1,17},{... | collective-permute-start | bytes 294920 | tf_op jit(solution)/shard_map/ppermute | solution.py:321
  333.4 43.8 %collective-permute-start.34 = (bf16[192,256]{1,0:T(8,128)(2,1)S(1)}, bf16[192,256]{1,0:T(8,128)(2,1)S(1)}, u32[]{:S(2)}, u32[]{:S(2)}) collective-permute-start(bf16[192,256]{1,0:T(8,128)(2,1)S(1)} %constant_dynamic-slice_fusion.6), channel_id=1, source_target_pairs={{0,16},{4,20},{8,24},{12,28},{16,0},{20,4},{24,8},{28,12},{1,17},{... | collective-permute-start | bytes 294920 | tf_op jit(solution)/shard_map/ppermute | solution.py:321
  334.5 44.8 %collective-permute-start.26 = (bf16[192,256]{1,0:T(8,128)(2,1)S(1)}, bf16[192,256]{1,0:T(8,128)(2,1)S(1)}, u32[]{:S(2)}, u32[]{:S(2)}) collective-permute-start(bf16[192,256]{1,0:T(8,128)(2,1)S(1)} %constant_dynamic-slice_fusion.9), channel_id=1, source_target_pairs={{0,16},{4,20},{8,24},{12,28},{16,0},{20,4},{24,8},{28,12},{1,17},{... | collective-permute-start | bytes 294920 | tf_op jit(solution)/shard_map/ppermute | solution.py:321
  417.9 153.0 %all-to-all-start.1 = ((bf16[8,128,768]{2,1,0:T(8,128)(2,1)}), bf16[8,128,768]{2,1,0:T(8,128)(2,1)S(1)}, u32[]{:S(2)}, u32[]{:S(2)}) async-start(bf16[8,128,768]{2,1,0:T(8,128)(2,1)} %fusion.27), calls=%async_computation.1 | async-start | bytes 3145728 | tf_op jit(solution)/shard_map/all_to_all | solution.py:502
  510.1 25.7 %collective-permute-start.14 = (bf16[2,1,192,4,768]{4,2,1,0,3:T(8,128)(2,1)S(1)}, bf16[2,1,192,4,768]{4,2,1,0,3:T(8,128)(2,1)S(1)}, u32[]{:S(2)}, u32[]{:S(2)}) collective-permute-start(bf16[2,1,192,4,768]{4,2,1,0,3:T(8,128)(2,1)S(1)} %constant_dynamic-slice_fusion.15), channel_id=1, source_target_pairs={{0,1},{1,0},{2,3},{3,2},{4,5},{5,4},{6,7},{7,6},{8,9},{9,8},{10,11... | collective-permute-start | bytes 7077896 | tf_op jit(solution)/shard_map/ppermute | solution.py:321
  516.1 53.5 %collective-permute-start.51 = (bf16[1,512,768]{2,1,0:T(8,128)(2,1)S(1)}, bf16[1,512,768]{2,1,0:T(8,128)(2,1)S(1)}, u32[]{:S(2)}, u32[]{:S(2)}) collective-permute-start(bf16[1,512,768]{2,1,0:T(8,128)(2,1)S(1)} %dynamic-slice_bitcast_fusion.1), channel_id=1, source_target_pairs={{0,2},{1,3},{2,0},{3,1},{4,6},{5,7},{6,4},{7,5},{8,10},{9,11},{10,... | collective-permute-start | bytes 2359304 | tf_op jit(solution)/shard_map/ppermute | solution.py:321
  518.7 49.5 %collective-permute-start.47 = (bf16[1,192,2048]{2,1,0:T(8,128)(2,1)S(1)}, bf16[1,192,2048]{2,1,0:T(8,128)(2,1)S(1)}, u32[]{:S(2)}, u32[]{:S(2)}) collective-permute-start(bf16[1,192,2048]{2,1,0:T(8,128)(2,1)S(1)} %dynamic-slice_bitcast_fusion.3), channel_id=1, source_target_pairs={{0,2},{1,3},{2,0},{3,1},{4,6},{5,7},{6,4},{7,5},{8,10},{9,11},{10,... | collective-permute-start | bytes 2359304 | tf_op jit(solution)/shard_map/ppermute | solution.py:321
  537.6 53.8 %collective-permute-start.15 = (bf16[1,192,4,768]{3,1,2,0:T(8,128)(2,1)}, bf16[1,192,4,768]{3,1,2,0:T(8,128)(2,1)}, u32[]{:S(2)}, u32[]{:S(2)}) collective-permute-start(bf16[1,192,4,768]{3,1,2,0:T(8,128)(2,1)} %dynamic-slice_bitcast_fusion), channel_id=1, source_target_pairs={{0,2},{1,3},{2,0},{3,1},{4,6},{5,7},{6,4},{7,5},{8,10},{9,11},{10,... | collective-permute-start | bytes 3538952 | tf_op jit(solution)/shard_map/ppermute | solution.py:321
  (152 other events, 1514.5 us)

commit v2 on v1

v2 whole, which is shorter than its diff:
```python
import functools

import jax
import jax.numpy as jnp
import numpy as np
from jax import lax
from jax.experimental import pallas as pl
from jax.experimental.pallas import tpu as pltpu
from jax.sharding import PartitionSpec as P

HEADS = 12
TOP = 2
WINDOW = 1024
MESH = pl.DeviceIdType.MESH
norm_eps = 1e-06
neg_fill = -1e30
rope_base = 10000.0

DIRECT = ("hid", "gains")
EARLY = ("wk", "wv", "wq")
SPREAD = ("wo", "sg", "su", "sd")
SPLIT_X = ("sg", "su", "sd")
LATE = ("eg", "eu", "ed")
NAMES = DIRECT + EARLY + SPREAD + LATE
IN_VMEM = DIRECT + EARLY + ("wo",)


def dense_product(left, right):
    return jnp.dot(left, right, preferred_element_type=jnp.float32)


def product_t(left, right):
    return lax.dot_general(left, right, (((1,), (1,)), ((), ())), preferred_element_type=jnp.float32)


def t_product(left, right):
    return lax.dot_general(left, right, (((0,), (0,)), ((), ())), preferred_element_type=jnp.float32)


def rms_scale(values):
    return lax.rsqrt(jnp.mean(values * values, axis=-1, keepdims=True) + norm_eps)


def rotary_tables(length, head_size):
    half = head_size // 2
    frequency = np.float32(rope_base) ** (-np.arange(half, dtype=np.float32) / np.float32(half))
    angles = np.arange(length, dtype=np.float32)[:, None] * frequency[None, :]
    cosine, sine = np.cos(angles).astype(np.float32), np.sin(angles).astype(np.float32)
    return np.concatenate([cosine] * 4, axis=1), np.concatenate([-sine, sine] * 2, axis=1)


def rotate_pair(values, cosine, sine):
    lane = lax.broadcasted_iota(jnp.int32, values.shape, 1)
    partner = jnp.where(lane % 64 < 32, pltpu.roll(values, 96, 1), pltpu.roll(values, 32, 1))
    return values * cosine + partner * sine


def rotate(values, positions, direction):
    half_size = values.shape[-1] // 2
    frequency = rope_base ** (-jnp.arange(half_size, dtype=jnp.float32) / half_size)
    angles = positions.astype(jnp.float32)[:, None] * frequency[None, :]
    cosine = jnp.cos(angles)[:, None, :]
    sine_part = direction * jnp.sin(angles)[:, None, :]
    first_half = values[..., :half_size]
    second_half = values[..., half_size:]
    return jnp.concatenate(
        [
            first_half * cosine - second_half * sine_part,
            second_half * cosine + first_half * sine_part,
        ],
        axis=-1,
    )


def swiglu_back(grad_middle, gate_pre, up_pre):
    sigmoid_gate = jax.nn.sigmoid(gate_pre)
    activated = gate_pre * sigmoid_gate
    grad_gate = grad_middle * up_pre * sigmoid_gate * (1.0 + gate_pre * (1.0 - sigmoid_gate))
    grad_up = grad_middle * activated
    return (grad_gate.astype(jnp.bfloat16), grad_up.astype(jnp.bfloat16))


def from_behind(value, axis, steps):
    count = lax.axis_size(axis)
    first, last = (max(0, -steps), min(count, count - steps))
    return lax.ppermute(value, axis, [(source, source + steps) for source in range(first, last)])


def send(source, target, send_sem, recv_sem, peer):
    pltpu.make_async_remote_copy(
        src_ref=source,
        dst_ref=target,
        send_sem=send_sem,
        recv_sem=recv_sem,
        device_id=peer,
        device_id_type=MESH,
    ).start()


def wait_for(ref, sem):
    pltpu.make_async_copy(ref, ref, sem).wait()


def first_kernel(*refs):
    count = len(NAMES)
    own = dict(zip(NAMES, refs[:count]))
    segment_row, segment_col, padding_row, cosine_ref, sine_ref = refs[count : count + 5]
    refs = refs[count + 5 :]
    full = dict(zip(NAMES, refs[:count]))
    gain_ref, normed_ref, query_ref, key_ref, value_ref, lse_ref, attended_ref, mixed_ref, ffn_ref = refs[count : count + 9]
    (own_sem, y_send, y_recv, x_send, x_recv, z_send, z_recv, core_send, core_recv) = refs[count + 9 :]
    number = {name: index for index, name in enumerate(NAMES)}
    expert, shard = (lax.axis_index("expert"), lax.axis_index("shard"))
    zed, ex = (expert // 2, expert % 2)
    other = (shard + 2) % 4
    y_peer = (expert, other)
    core_peer = (expert, shard + 1 - 2 * (shard % 2))
    x_peer = (expert + 1 - 2 * ex, shard)
    z_up, z_down = (((expert + 2) % 8, shard), ((expert + 6) % 8, shard))

    barrier = pltpu.get_barrier_semaphore()
    for peer in (y_peer, core_peer, x_peer):
        pl.semaphore_signal(barrier, inc=1, device_id=peer, device_id_type=MESH)

    @pl.when(zed < 3)
    def _():
        pl.semaphore_signal(barrier, inc=1, device_id=z_up, device_id_type=MESH)

    @pl.when(zed > 0)
    def _():
        pl.semaphore_signal(barrier, inc=1, device_id=z_down, device_id_type=MESH)

    pl.semaphore_wait(barrier, 3 + jnp.minimum(3 - zed, 1) + jnp.minimum(zed, 1))

    def part_of(block, base, name, at_z, at_x):
        rows = own[name].shape[0]
        if at_z is None and at_x is None:
            return block.at[pl.ds(base, rows)]
        if name in EARLY:
            return block.at[pl.ds(base + at_x * (rows // 2), rows // 2)]
        if name in ("sg", "su"):
            half = block.shape[1] // 8
            return block.at[pl.ds(base, rows), pl.ds((at_z * 2 + at_x) * half, half)]
        size = rows // 4
        if name == "sd":
            return block.at[pl.ds(base + at_z * size + at_x * (size // 2), size // 2)]
        return block.at[pl.ds(base + at_z * size, size)]

    def place(name, slot, at_z=None, at_x=None):
        return part_of(full[name], slot * own[name].shape[0], name, at_z, at_x)

    def mine(name, at_z=None, at_x=None):
        return part_of(own[name], 0, name, at_z, at_x)

    def ex_of(name):
        return ex if name in SPLIT_X else None

    def cross(name, at_z=None, at_x=None):
        n = number[name]
        send(mine(name, at_z, at_x), place(name, shard, at_z, at_x), y_send.at[n], y_recv.at[n], y_peer)

    def to_core(name, step, at_z=None, at_x=None):
        n = number[name]
        part = place(name, other, at_z, at_x)
        send(part, part, core_send.at[n, 1 + step], core_recv.at[n, 1 + step], core_peer)

    far = shard + 1 - 2 * (shard % 2)
    far_other = (far + 2) % 4

    def settle_own(names):
        for name in names:
            n = number[name]
            pltpu.make_async_copy(own[name], place(name, shard), own_sem.at[n]).wait()
            wait_for(place(name, far), core_recv.at[n, 0])
            wait_for(own[name], core_send.at[n, 0])

    def settle_core(name, step, at_z=None, at_x=None):
        n = number[name]
        wait_for(place(name, far_other, at_z, at_x), core_recv.at[n, 1 + step])
        wait_for(place(name, other, at_z, at_x), core_send.at[n, 1 + step])

    for name in DIRECT:
        cross(name)
    for name in EARLY:
        cross(name, None, ex)
    for name in SPREAD:
        cross(name, zed, ex_of(name))
    for name in NAMES:
        n = number[name]
        send(own[name], place(name, shard), core_send.at[n, 0], core_recv.at[n, 0], core_peer)
        pltpu.make_async_copy(own[name], place(name, shard), own_sem.at[n]).start()

    for name in DIRECT:
        wait_for(place(name, other), y_recv.at[number[name]])
        to_core(name, 0)
    for name in EARLY:
        n = number[name]
        part = place(name, other, None, ex)
        wait_for(part, y_recv.at[n])
        send(part, part, x_send.at[n, 0], x_recv.at[n, 0], x_peer)
        to_core(name, 0, None, ex)
    for name in LATE:
        cross(name)

    def on_part(name, at_z, step):
        n = number[name]
        part = place(name, other, at_z, ex_of(name))
        if name in SPLIT_X:
            send(part, part, x_send.at[n, step], x_recv.at[n, step], x_peer)
        to_core(name, step, at_z, ex_of(name))

    def forward(step, direction, condition, at_z, peer):
        @pl.when(condition)
        def _():
            for name in SPREAD:
                n = number[name]
                part = place(name, other, at_z, ex_of(name))
                send(part, part, z_send.at[n, direction, step], z_recv.at[n, direction, step], peer)

    def arrive(step, direction, condition, at_z):
        @pl.when(condition)
        def _():
            for name in SPREAD:
                n = number[name]
                wait_for(place(name, other, at_z, ex_of(name)), z_recv.at[n, direction, step])
                on_part(name, at_z, 1 + direction * 3 + step)

    def ring_send(step):
        forward(step, 0, (zed < 3) & (zed >= step), zed - step, z_up)
        forward(step, 1, (zed > 0) & (zed + step <= 3), zed + step, z_down)

    def ring_arrive(step):
        arrive(step, 0, zed >= step + 1, zed - 1 - step)
        arrive(step, 1, zed + 1 + step <= 3, zed + 1 + step)

    for name in SPREAD:
        wait_for(place(name, other, zed, ex_of(name)), y_recv.at[number[name]])
    ring_send(0)
    for name in SPREAD:
        on_part(name, zed, 0)

    settle_own(DIRECT)
    for name in DIRECT:
        settle_core(name, 0)
    tokens, width = own["hid"].shape
    gain_rows = sum(full["gains"][pl.ds(slot * 16, 16), :].astype(jnp.float32) for slot in range(4))
    gain_ref[...] = gain_rows
    gain_first, gain_second = gain_rows[0:1], gain_rows[1:2]

    def norm_block(block, carry):
        rows = pl.ds(pl.multiple_of(block * tokens, tokens), tokens)
        values = full["hid"][rows, :].astype(jnp.float32)
        normed_ref[rows, :] = (values * rms_scale(values) * gain_first).astype(jnp.bfloat16)
        return carry

    lax.fori_loop(0, 4, norm_block, 0)

    for name in EARLY:
        wait_for(place(name, other, None, 1 - ex), x_recv.at[number[name], 0])
        to_core(name, 1, None, 1 - ex)
    settle_own(EARLY)
    for name in EARLY:
        settle_core(name, 0, None, ex)
        settle_core(name, 1, None, 1 - ex)
        wait_for(mine(name, None, ex), y_send.at[number[name]])
        wait_for(place(name, other, None, ex), x_send.at[number[name], 0])

    def key_block(block, carry):
        rows = pl.ds(pl.multiple_of(block * tokens, tokens), tokens)
        normed = normed_ref[rows, :]
        value_ref[rows, :] = dense_product(normed, full["wv"][...]).astype(jnp.bfloat16)
        raw = dense_product(normed, full["wk"][...])
        cosine, sine = cosine_ref[rows, :], sine_ref[rows, :]
        for start in range(0, width, 128):
            key_ref[rows, start : start + 128] = rotate_pair(raw[:, start : start + 128], cosine, sine).astype(jnp.bfloat16)
        return carry

    lax.fori_loop(0, 4, key_block, 0)
    ring_arrive(0)
    ring_send(1)
    here = pl.ds(pl.multiple_of(shard * tokens, tokens), tokens)
    raw = dense_product(normed_ref[here, :], full["wq"][...])
    cosine, sine = cosine_ref[here, :], sine_ref[here, :]
    for start in range(0, width, 128):
        query_ref[:, start : start + 128] = rotate_pair(raw[:, start : start + 128], cosine, sine).astype(jnp.bfloat16)

    def head_pair(pair, carry):
        lanes = pl.ds(pl.multiple_of(pair * 128, 128), 128)
        query, keys, values = query_ref[:, lanes], key_ref[:, lanes], value_ref[:, lanes]
        allowed = allowed_mask(shard * tokens, 0, segment_col[here, :], segment_row[...], padding_row[...])
        lane = lax.broadcasted_iota(jnp.int32, query.shape, 1)
        results = []
        for half in range(2):
            chosen = (lane >= 64) if half else (lane < 64)
            scores = product_t(jnp.where(chosen, query, jnp.zeros_like(query)), keys) * 0.125
            scores = jnp.where(allowed, scores, neg_fill)
            top_score = jnp.max(scores, axis=-1, keepdims=True)
            exponent = jnp.exp(scores - top_score)
            exp_total = jnp.sum(exponent, axis=-1, keepdims=True)
            lse_ref[2 * pair + half] = top_score + jnp.log(exp_total)
            results.append(dense_product((exponent / exp_total).astype(jnp.bfloat16), values))
        attended_ref[:, lanes] = jnp.where(lane < 64, results[0], results[1]).astype(jnp.bfloat16)
        return carry

    lax.fori_loop(0, 3, head_pair, 0)
    ring_arrive(1)
    ring_send(2)
    lax.fori_loop(3, 6, head_pair, 0)
    ring_arrive(2)

    def from_x(condition, at_z, step):
        @pl.when(condition)
        def _():
            for name in SPLIT_X:
                wait_for(place(name, other, at_z, 1 - ex), x_recv.at[number[name], step])
                to_core(name, 7 + step, at_z, 1 - ex)

    from_x(zed >= 0, zed, 0)
    for step in range(3):
        from_x(zed >= step + 1, zed - 1 - step, 1 + step)
        from_x(zed + 1 + step <= 3, zed + 1 + step, 4 + step)

    def settle_spread(names, condition, at_z, step):
        @pl.when(condition)
        def _():
            for name in names:
                settle_core(name, step, at_z, ex_of(name))
                if name in SPLIT_X:
                    wait_for(place(name, other, at_z, ex), x_send.at[number[name], step])
                    settle_core(name, 7 + step, at_z, 1 - ex)

    def settle_ring(names):
        settle_own(names)
        for name in names:
            wait_for(mine(name, zed, ex_of(name)), y_send.at[number[name]])
        settle_spread(names, zed >= 0, zed, 0)
        for step in range(3):
            settle_spread(names, zed >= step + 1, zed - 1 - step, 1 + step)
            settle_spread(names, zed + 1 + step <= 3, zed + 1 + step, 4 + step)

    settle_ring(("wo",))
    rows_in = own["hid"][...].astype(jnp.float32)
    mixed = rows_in + dense_product(attended_ref[...], full["wo"][...])
    mixed_ref[...] = mixed
    ffn_ref[...] = (mixed * rms_scale(mixed) * gain_second).astype(jnp.bfloat16)

    for name in LATE:
        wait_for(place(name, other), y_recv.at[number[name]])
        to_core(name, 0)
    settle_ring(SPLIT_X)

    def sent(step, direction, condition, at_z):
        @pl.when(condition)
        def _():
            for name in SPREAD:
                wait_for(place(name, other, at_z, ex_of(name)), z_send.at[number[name], direction, step])

    for step in range(3):
        sent(step, 0, (zed < 3) & (zed >= step), zed - step)
        sent(step, 1, (zed > 0) & (zed + step <= 3), zed + step)
    for name in DIRECT:
        wait_for(own[name], y_send.at[number[name]])
    settle_own(LATE)
    for name in LATE:
        wait_for(own[name], y_send.at[number[name]])
        settle_core(name, 0)


def allowed_mask(query_start, key_start, query_segment, key_segment, key_padding):
    shape = (query_segment.shape[0], key_segment.shape[1])
    query_at = query_start + lax.broadcasted_iota(jnp.int32, shape, 0)
    key_at = key_start + lax.broadcasted_iota(jnp.int32, shape, 1)
    distance = query_at - key_at
    return (
        (query_segment == key_segment)
        & (distance >= 0)
        & (distance < WINDOW)
        & ((key_padding == 1) | (distance == 0))
    )


def first_part(hidden, gains, dense, experts, segment, padding):
    tokens, width = hidden.shape
    bfloat, single = jnp.bfloat16, jnp.float32
    wq, wk, wv, wo, sg, su, sd = dense
    blocks = dict(hid=hidden, gains=jnp.pad(gains, ((0, 14), (0, 0))), wq=wq, wk=wk, wv=wv, wo=wo, sg=sg, su=su, sd=sd)
    blocks.update(zip(LATE, experts))
    blocks = [blocks[name] for name in NAMES]
    count = len(NAMES)
    cosine, sine = rotary_tables(4 * tokens, width // HEADS)
    in_hbm, in_vmem = pl.BlockSpec(memory_space=pl.ANY), pl.BlockSpec(memory_space=pltpu.VMEM)
    dma = pltpu.SemaphoreType.DMA
    shape = jax.ShapeDtypeStruct
    out = pl.pallas_call(
        first_kernel,
        out_shape=[shape((4 * block.shape[0], block.shape[1]), block.dtype) for block in blocks]
        + [
            shape((16, width), single),
            shape((4 * tokens, width), bfloat),
            shape((tokens, width), bfloat),
            shape((4 * tokens, width), bfloat),
            shape((4 * tokens, width), bfloat),
            shape((HEADS, tokens, 1), single),
            shape((tokens, width), bfloat),
            shape((tokens, width), single),
            shape((tokens, width), bfloat),
        ],
        in_specs=[in_vmem] * (count + 5),
        out_specs=[in_vmem if name in IN_VMEM else in_hbm for name in NAMES] + [in_vmem] * 9,
        scratch_shapes=[
            dma((count,)),
            dma((count,)),
            dma((count,)),
            dma((count, 7)),
            dma((count, 7)),
            dma((count, 2, 3)),
            dma((count, 2, 3)),
            dma((count, 15)),
            dma((count, 15)),
        ],
        compiler_params=pltpu.CompilerParams(collective_id=0, has_side_effects=True, vmem_limit_bytes=56 << 20),
        cost_estimate=pl.CostEstimate(flops=5000000000, bytes_accessed=47000000, transcendentals=3000000),
    )(
        *blocks,
        segment[None, :],
        segment[:, None],
        padding[None, :],
        jnp.asarray(cosine),
        jnp.asarray(sine),
    )
    return dict(zip(NAMES, out[:count])), out[count:]


def swap(value, axis, bit):
    size = lax.axis_size(axis)
    return lax.ppermute(value, axis, [(index, index ^ bit) for index in range(size)])


def halves(value, bit_set, dim):
    half = value.shape[dim] // 2
    keep = lax.dynamic_slice_in_dim(value, bit_set * half, half, dim)
    give = lax.dynamic_slice_in_dim(value, (1 - bit_set) * half, half, dim)
    return keep, give


def fold(value, axis, bit, dim):
    bit_set = (lax.axis_index(axis) // bit) % 2
    keep, give = halves(value, bit_set, dim)
    return (keep.astype(jnp.float32) + swap(give.astype(jnp.bfloat16), axis, bit).astype(jnp.float32)).astype(jnp.bfloat16)


def unfold(value, axis, bit, dim):
    bit_set = (lax.axis_index(axis) // bit) % 2
    come = swap(value, axis, bit)
    return jnp.where(bit_set == 0, jnp.concatenate([value, come], dim), jnp.concatenate([come, value], dim))


def bits_of(axis):
    size = lax.axis_size(axis)
    return [1 << place for place in range(size.bit_length() - 1)]


def scatter_shards(value):
    count = lax.axis_size("shard")
    blocks = value.reshape((count // 2, 2, value.shape[0] // count) + value.shape[1:])
    blocks = fold(blocks, "shard", 1, 1)[:, 0]
    for bit in reversed(bits_of("shard")[1:]):
        blocks = fold(blocks, "shard", bit, 0)
    return blocks[0]


def sum_plane(value, dim):
    bits = bits_of("expert")
    for bit in bits:
        value = fold(value, "expert", bit, dim)
    for bit in reversed(bits):
        value = unfold(value, "expert", bit, dim)
    return value.astype(jnp.float32)


def shards(
    hidden_in,
    gain_attn,
    gain_ffn,
    w_query,
    w_key,
    w_value,
    w_out,
    shared_gate,
    shared_up,
    shared_down,
    expert_gate,
    expert_up,
    expert_down,
    gate_logits,
    routes,
    segment,
    padding,
    cotangent,
):
    bfloat = jnp.bfloat16
    tokens = hidden_in.shape[1]
    model_width = hidden_in.shape[2]
    head_size = model_width // HEADS
    experts = lax.axis_size("expert")
    capacity = max(2, 2 * tokens * TOP // experts)
    shard_count = lax.axis_size("shard")
    shard_index = lax.axis_index("shard")
    score_scale = head_size ** (-0.5)
    head_shape = (tokens, HEADS, head_size)
    fast = (experts, shard_count, WINDOW) == (8, 4, 4 * tokens)
    dense_own = (w_query, w_key, w_value, w_out, shared_gate, shared_up, shared_down)
    expert_own = (expert_gate[0], expert_up[0], expert_down[0])
    rows_in = hidden_in[0].astype(jnp.float32)
    scale_first = rms_scale(rows_in)
    positions = shard_index * tokens + jnp.arange(tokens, dtype=jnp.int32)
    segment_row, padding_row = segment[0], padding[0]
    query_segment = lax.dynamic_slice_in_dim(segment_row, shard_index * tokens, tokens)
    if fast:
        gain_own = lax.dynamic_update_slice(
            jnp.zeros((2, model_width), bfloat),
            jnp.stack([gain_attn, gain_ffn]),
            (0, shard_index * gain_attn.shape[0]),
        )
        full, rest = first_part(hidden_in[0], gain_own, dense_own, expert_own, segment_row, padding_row)
        gains, normed_ctx, query_low, keys_ctx, values_ctx, log_total, attended, mixed_rows, normed_ffn = rest
        gain_first, gain_second = gains[0], gains[1]
        w_q, w_k, w_v, w_o, s_gate, s_up, s_down = (full[name] for name in ("wq", "wk", "wv", "wo", "sg", "su", "sd"))
        e_gate, e_up, e_down = (full[name] for name in LATE)
        reach, key_start = shard_count - 1, 0
        key_segment, key_padding = segment_row, padding_row
        key_positions = jnp.arange(4 * tokens, dtype=jnp.int32)
        allowed = allowed_mask(shard_index * tokens, 0, query_segment[:, None], key_segment[None], key_padding[None])
    else:
        gather = functools.partial(lax.all_gather, axis_name="shard", tiled=True)
        w_q, w_k, w_v, w_o, s_gate, s_up, s_down = (gather(weight) for weight in dense_own)
        e_gate, e_up, e_down = (gather(weight) for weight in expert_own)
        gain_first, gain_second = (gather(gain).astype(jnp.float32) for gain in (gain_attn, gain_ffn))
        reach = min((WINDOW + tokens - 2) // tokens, shard_count - 1)
        lead_rows, key_rows = reach * tokens, (reach + 1) * tokens
        context = [from_behind(hidden_in[0], "shard", offset) for offset in range(reach, 0, -1)] + [hidden_in[0]]
        context = jnp.concatenate(context, axis=0).astype(jnp.float32)
        normed_ctx = (context * rms_scale(context) * gain_first).astype(bfloat)
        key_positions = (shard_index - reach) * tokens + jnp.arange(key_rows, dtype=jnp.int32)
        query_low = rotate(
            dense_product(normed_ctx[lead_rows:], w_q).reshape(head_shape), positions, 1.0
        ).astype(bfloat)
        keys_ctx = rotate(
            dense_product(normed_ctx, w_k).reshape(key_rows, HEADS, head_size), key_positions, 1.0
        ).astype(bfloat)
        values_ctx = dense_product(normed_ctx, w_v).astype(bfloat)
        segment_ext = jnp.concatenate([jnp.full((lead_rows,), -1, jnp.int32), segment_row])
        padding_ext = jnp.concatenate([jnp.zeros((lead_rows,), jnp.int32), padding_row])
        key_segment = lax.dynamic_slice_in_dim(segment_ext, shard_index * tokens, key_rows)
        key_padding = lax.dynamic_slice_in_dim(padding_ext, shard_index * tokens, key_rows)
        allowed = allowed_mask(
            shard_index * tokens,
            (shard_index - reach) * tokens,
            query_segment[:, None],
            key_segment[None],
            key_padding[None],
        )
    key_rows = (reach + 1) * tokens
    query_heads = query_low.reshape(head_shape)
    keys_all = keys_ctx.reshape(key_rows, HEADS, head_size)
    values_all = values_ctx.reshape(key_rows, HEADS, head_size)

    def score_block():
        raw_scores = (
            jnp.einsum("qhd,khd->hqk", query_heads, keys_all, preferred_element_type=jnp.float32)
            * score_scale
        )
        return jnp.where(allowed[None], raw_scores, neg_fill)

    if not fast:
        scores = score_block()
        top_score = jnp.max(scores, axis=-1, keepdims=True)
        exponent = jnp.exp(scores - top_score)
        exp_total = jnp.sum(exponent, axis=-1, keepdims=True)
        log_total = top_score + jnp.log(exp_total)
        attended = (
            jnp.einsum(
                "hqk,khd->qhd",
                (exponent / exp_total).astype(bfloat),
                values_all,
                preferred_element_type=jnp.float32,
            )
            .astype(bfloat)
            .reshape(tokens, model_width)
        )
        mixed_rows = rows_in + dense_product(attended, w_o)
        normed_ffn = (mixed_rows * rms_scale(mixed_rows) * gain_second).astype(bfloat)
    scale_second = rms_scale(mixed_rows)
    shared_pre = dense_product(normed_ffn, s_gate)
    shared_lin = dense_product(normed_ffn, s_up)
    shared_mid = (jax.nn.silu(shared_pre) * shared_lin).astype(bfloat)
    shared_out = dense_product(shared_mid, s_down)
    route_flat = routes[0].reshape(-1)
    route_total = tokens * TOP
    onehot = (route_flat[:, None] == jnp.arange(experts, dtype=jnp.int32)[None, :]).astype(
        jnp.int32
    )
    slot_rank = jnp.sum((jnp.cumsum(onehot, axis=0) - onehot) * onehot, axis=1)
    places = route_flat * capacity + slot_rank
    slot_table = (
        jnp.full((experts * capacity,), route_total, dtype=jnp.int32)
        .at[places]
        .set(jnp.arange(route_total, dtype=jnp.int32))
    )
    padded_rows = jnp.concatenate([normed_ffn, jnp.zeros((1, model_width), bfloat)], axis=0)
    send_rows = padded_rows[slot_table // TOP].reshape(experts, capacity, model_width)
    received = lax.all_to_all(send_rows, "expert", split_axis=0, concat_axis=0, tiled=True)
    gate_pre = jnp.einsum("sid,df->sif", received, e_gate, preferred_element_type=jnp.float32)
    up_pre = jnp.einsum("sid,df->sif", received, e_up, preferred_element_type=jnp.float32)
    middle = (jax.nn.silu(gate_pre) * up_pre).astype(bfloat)
    result = jnp.einsum("sif,fd->sid", middle, e_down, preferred_element_type=jnp.float32).astype(bfloat)
    returned = lax.all_to_all(result, "expert", split_axis=0, concat_axis=0, tiled=True)
    per_route = (
        returned.reshape(experts * capacity, model_width)[places]
        .astype(jnp.float32)
        .reshape(tokens, TOP, model_width)
    )
    gate_probs = jax.nn.softmax(gate_logits[0], axis=-1)
    routed = jnp.sum(gate_probs[:, :, None] * per_route, axis=1)
    output = (mixed_rows + shared_out + routed).astype(bfloat)
    grad_low = cotangent[0]
    grad_out = grad_low.astype(jnp.float32)
    contrib = jnp.sum(per_route * grad_out[:, None, :], axis=-1)
    logit_grad = gate_probs * (contrib - jnp.sum(gate_probs * contrib, axis=-1, keepdims=True))
    route_grad = (
        (gate_probs[:, :, None] * grad_out[:, None, :])
        .astype(bfloat)
        .reshape(route_total, model_width)
    )
    route_padded = jnp.concatenate([route_grad, jnp.zeros((1, model_width), bfloat)], axis=0)
    send_grad = route_padded[slot_table].reshape(experts, capacity, model_width)
    grad_received = lax.all_to_all(send_grad, "expert", split_axis=0, concat_axis=0, tiled=True)
    grad_middle = jnp.einsum(
        "sid,fd->sif", grad_received, e_down, preferred_element_type=jnp.float32
    )
    grad_gate_pre, grad_up_pre = swiglu_back(grad_middle, gate_pre, up_pre)
    expert_down_grad = jnp.einsum(
        "sif,sid->fd", middle, grad_received, preferred_element_type=jnp.float32
    )
    expert_gate_grad = jnp.einsum(
        "sid,sif->df", received, grad_gate_pre, preferred_element_type=jnp.float32
    )
    expert_up_grad = jnp.einsum(
        "sid,sif->df", received, grad_up_pre, preferred_element_type=jnp.float32
    )
    grad_rows = (
        jnp.einsum("sif,df->sid", grad_gate_pre, e_gate, preferred_element_type=jnp.float32)
        + jnp.einsum("sif,df->sid", grad_up_pre, e_up, preferred_element_type=jnp.float32)
    ).astype(bfloat)
    grad_back = lax.all_to_all(grad_rows, "expert", split_axis=0, concat_axis=0, tiled=True)
    expert_grads = tuple(
        scatter_shards(grad.astype(bfloat))[None].astype(jnp.float32)
        for grad in (expert_gate_grad, expert_up_grad, expert_down_grad)
    )
    grad_routes = (
        grad_back.reshape(experts * capacity, model_width)[places]
        .astype(jnp.float32)
        .reshape(tokens, TOP, model_width)
    )
    grad_normed_ffn = jnp.sum(grad_routes, axis=1)
    grad_shared_mid = product_t(grad_low, s_down)
    grad_shared_pre, grad_shared_lin = swiglu_back(grad_shared_mid, shared_pre, shared_lin)
    shared_down_grad = dense_product(shared_mid.T, grad_low)
    shared_gate_grad = dense_product(normed_ffn.T, grad_shared_pre)
    shared_up_grad = dense_product(normed_ffn.T, grad_shared_lin)
    grad_normed_ffn = (
        grad_normed_ffn + product_t(grad_shared_pre, s_gate) + product_t(grad_shared_lin, s_up)
    )
    gain_ffn_grad = jnp.sum(grad_normed_ffn * mixed_rows * scale_second, axis=0)
    scaled_second = grad_normed_ffn * gain_second
    grad_mixed = (
        grad_out
        + scale_second * scaled_second
        - mixed_rows
        * scale_second**3
        * jnp.mean(scaled_second * mixed_rows, axis=-1, keepdims=True)
    )
    grad_mixed_low = grad_mixed.astype(bfloat)
    w_out_grad = dense_product(attended.T, grad_mixed_low)
    grad_attended = product_t(grad_mixed_low, w_o).astype(bfloat).reshape(head_shape)
    attn_probs = jnp.exp(score_block() - log_total)
    grad_probs = jnp.einsum(
        "qhd,khd->hqk", grad_attended, values_all, preferred_element_type=jnp.float32
    )
    delta_rows = jnp.sum(attn_probs * grad_probs, axis=-1, keepdims=True)
    grad_scores = (attn_probs * (grad_probs - delta_rows)).astype(bfloat)
    grad_query = (
        jnp.einsum("hqk,khd->qhd", grad_scores, keys_all, preferred_element_type=jnp.float32)
        * score_scale
    )
    grad_keys = (
        jnp.einsum("hqk,qhd->khd", grad_scores, query_heads, preferred_element_type=jnp.float32)
        * score_scale
    )
    grad_values = jnp.einsum(
        "hqk,qhd->khd", attn_probs.astype(bfloat), grad_attended, preferred_element_type=jnp.float32
    )
    grad_query_low = rotate(grad_query, positions, -1.0).astype(bfloat).reshape(tokens, model_width)
    grad_key_low = rotate(grad_keys, key_positions, -1.0).astype(bfloat).reshape(key_rows, model_width)
    grad_value_low = grad_values.astype(bfloat).reshape(key_rows, model_width)
    if fast:
        normed = lax.dynamic_slice_in_dim(normed_ctx, shard_index * tokens, tokens)
    else:
        normed = normed_ctx[reach * tokens :]
    w_query_grad = dense_product(normed.T, grad_query_low)
    w_key_grad = dense_product(normed_ctx.T, grad_key_low)
    w_value_grad = dense_product(normed_ctx.T, grad_value_low)
    grad_context = product_t(grad_key_low, w_k) + product_t(grad_value_low, w_v)
    grad_normed = product_t(grad_query_low, w_q)
    if fast:
        grad_normed = grad_normed + scatter_shards(grad_context.astype(bfloat)).astype(jnp.float32)
    else:
        grad_normed = grad_normed + grad_context[reach * tokens :]
        for offset in range(1, reach + 1):
            sent = grad_context[(reach - offset) * tokens :][:tokens].astype(bfloat)
            grad_normed = grad_normed + from_behind(sent, "shard", -offset).astype(jnp.float32)
    gain_attn_grad = jnp.sum(grad_normed * rows_in * scale_first, axis=0)
    scaled_first = grad_normed * gain_first
    input_grad = (
        grad_mixed
        + scale_first * scaled_first
        - rows_in * scale_first**3 * jnp.mean(scaled_first * rows_in, axis=-1, keepdims=True)
    )
    gain_rows = jnp.stack([gain_attn_grad, gain_ffn_grad], axis=1).astype(bfloat)
    gain_total = lax.psum(scatter_shards(gain_rows), "expert").astype(jnp.float32)
    attn_grads = jnp.stack([w_query_grad, w_key_grad, w_value_grad, w_out_grad]).astype(bfloat)
    attn_rows = scatter_shards(attn_grads.transpose(1, 0, 2)).transpose(1, 0, 2)
    attn_total = sum_plane(attn_rows.reshape(-1, model_width), 0).reshape(attn_rows.shape)
    return (
        output[None],
        input_grad[None],
        logit_grad[None],
        gain_total[:, 0],
        gain_total[:, 1],
        attn_total[0],
        attn_total[1],
        attn_total[2],
        attn_total[3],
        sum_plane(scatter_shards(shared_gate_grad.astype(bfloat)), 1),
        sum_plane(scatter_shards(shared_up_grad.astype(bfloat)), 1),
        sum_plane(scatter_shards(shared_down_grad.astype(bfloat)), 0),
        expert_grads[0],
        expert_grads[1],
        expert_grads[2],
    )


def solution(mesh):
    placed = (
        P("expert", "shard", None),
        P("shard"),
        P("shard"),
        P("shard", None),
        P("shard", None),
        P("shard", None),
        P("shard", None),
        P("shard", None),
        P("shard", None),
        P("shard", None),
        P("expert", "shard", None),
        P("expert", "shard", None),
        P("expert", "shard", None),
        P("expert", "shard", None),
        P("expert", "shard", None),
        P("expert", None),
        P("expert", None),
        P("expert", "shard", None),
    )
    return jax.shard_map(
        shards,
        mesh=mesh,
        in_specs=placed,
        out_specs=(
            P("expert", "shard", None),
            P("expert", "shard", None),
            P("expert", "shard", None),
            P("shard"),
            P("shard"),
            P("shard", None),
            P("shard", None),
            P("shard", None),
            P("shard", None),
            P("shard", None),
            P("shard", None),
            P("shard", None),
            P("expert", "shard", None),
            P("expert", "shard", None),
            P("expert", "shard", None),
        ),
        check_vma=False,
    )
```

time: 674 us -> 583 us (0.86)
  waiting for transfers between devices: 202 us -> 136 us
  starting transfers between devices: 97.4 us -> 63.5 us
  Pallas kernels: 81.4 us -> 97.4 us
  local copies, waits for them, and re-layouts: 82.6 us -> 67.8 us
    ppermute x40 -> x42, waiting for transfers between devices: 177 us -> 135 us  [swap(): lax.ppermute(value, axis, [(index, index ^ bit) for index in range(size)])]
    ppermute x12 -> x0, starting transfers between devices: 31.5 us -> none  [from_behind(): lax.ppermute(value, axis, [(source, source + steps) for source in range(f...]
    ppermute x12 -> x0, waiting for transfers between devices: 24.9 us -> none  [from_behind(): lax.ppermute(value, axis, [(source, source + steps) for source in range(f...]
    unnamed x244 -> x182, local copies, waits for them, and re-layouts: 27.1 us -> 10.7 us
    pallas_call x1, Pallas kernels: 81.4 us -> 97.4 us  [first_part(): pl.pallas_call(first_kernel, out_shape=[shape((4 * block.shape[0], block....]
    dot_general x9 -> x15, matrix products: 54.7 us -> 68.4 us  [the longest x7 17.7 us: product_t(): lax.dot_general(left, right, (((1,), (1,)), ((), ())), preferred_element_...]
    dot_general x21 -> x10, matrix products: 26.3 us -> 16.2 us  [dense_product(): return jnp.dot(left, right, preferred_element_type=jnp.float32)]
    ppermute x40 -> x42, starting transfers between devices: 46.5 us -> 42 us  [swap(): lax.ppermute(value, axis, [(index, index ^ bit) for index in range(size)])]
  transfers between devices with their start and end apart: 56 -> 46, of which waited for: 26 -> 23; matrix products, arithmetic and copies ran while one was open for 34% -> 39% of each run, Pallas kernels for 0% -> 17%
where the time goes in v2:
time: 583 us; the launch traced here: 573 us
  waiting for transfers between devices  136 us (23%)
  matrix products  118 us (20%)
  Pallas kernels  97.4 us (17%)
  local copies, waits for them, and re-layouts  67.8 us (12%)
  other arithmetic  66.1 us (11%)
  starting transfers between devices  63.5 us (11%)
  blocking collectives  21.6 us (4%)
    ppermute x42, waiting for transfers between devices, swap(): lax.ppermute(value, axis, [(index, index ^ bit) for index in range(size)])  135 us
    pallas_call x1, Pallas kernels, first_part(): pl.pallas_call(first_kernel, out_shape=[shape((4 * block.shape[0], block....  97.4 us
    ppermute x42, starting transfers between devices, swap(): lax.ppermute(value, axis, [(index, index ^ bit) for index in range(size)])  42 us
    psum x1, blocking collectives, shards(): lax.psum(scatter_shards(gain_rows), 'expert').astype(jnp.float32)  21.6 us
    convert_element_type x26, other arithmetic, fold(): (keep.astype(jnp.float32) + swap(give.astype(jnp.bfloat16), axis, bit).as...  21 us
    dot_general x7, matrix products, product_t(): lax.dot_general(left, right, (((1,), (1,)), ((), ())), preferred_element_...  17.7 us
    dot_general x10, matrix products, dense_product(): return jnp.dot(left, right, preferred_element_type=jnp.float32)  16.2 us
    dynamic_slice x30, local copies, waits for them, and re-layouts, halves(): give = lax.dynamic_slice_in_dim(value, (1 - bit_set) * half, half, dim)  15 us
  transfers between devices with their start and end apart: 46, of which 23 were waited for; matrix products, arithmetic and copies ran while one was open for 39% of the time, Pallas kernels for 17%

profile of v2, /device:TPU:0, one launch (start us, length us, event | category | flops | bytes accessed | tf_op | source)
XLA Modules:
  0.0 572.8 jit_solution(11649629670746397649)
XLA Ops:
  16.8 7.4 %all-to-all-start.2 = ((bf16[8,128,768]{2,1,0:T(8,128)(2,1)}), bf16[8,128,768]{2,1,0:T(8,128)(2,1)}, u32[]{:S(2)}, u32[]{:S(2)}) async-start(bf16[8,128,768]{2,1,0:T(8,128)(2,1)} %bitcast.17), calls=%async_computation.2 | async-start | bytes 3145728 | tf_op jit(solution)/shard_map/all_to_all | solution.py:637
  26.1 97.4 %shard_map.310 = (bf16[1024,768]{1,0:T(8,128)(2,1)}, bf16[64,768]{1,0:T(8,128)(2,1)}, bf16[768,768]{1,0:T(8,128)(2,1)}, bf16[768,768]{1,0:T(8,128)(2,1)}, bf16[7...) custom-call(bf16[256,768]{1,0:T(8,128)(2,1)} %bitcast.268, ...), custom_call_target="tpu_custom_call" | custom-call | flops 5000000000 | bytes 47000000 | tf_op jit(solution)/shard_map/pallas_call | solution.py:394
  129.1 5.4 multiply_convert_fusion.4
  159.2 7.9 %fusion.102 = f32[12,256,1024]{2,1,0:T(8,128)} fusion(bf16[256,12,64]{0,2,1:T(8,128)(2,1)S(1)} %bitcast.262, bf16[1024,12,64]{0,2,1:T(8,128)(2,1)} %bitcast.258), kind=kOutput, calls=%fused_computation.263 | convolution fusion | flops 402653184 | bytes 14548992 | tf_op jit(solution)/shard_map/qhd,khd->hqk/dot_general | solution.py:570
  186.9 5.9 %all-to-all-start = ((bf16[8,128,768]{2,1,0:T(8,128)(2,1)}), bf16[8,128,768]{2,1,0:T(8,128)(2,1)}, u32[]{:S(2)}, u32[]{:S(2)}) async-start(bf16[8,128,768]{2,1,0:T(8,128)(2,1)} %bitcast.260), calls=%async_computation | async-start | bytes 3145728 | tf_op jit(solution)/shard_map/all_to_all | solution.py:612
  195.3 6.8 %collective-permute-done.13 = bf16[1,192,2048]{2,1,0:T(8,128)(2,1)} collective-permute-done((bf16[1,192,2048]{2,1,0:T(8,128)(2,1)}, bf16[1,192,2048]{2,1,0:T(8,128)(2,1)}, u32[]{:S(2)}, u32[]{:S(2)}) %collective-permute-start.13) | collective-permute-done | bytes 786464 | tf_op jit(solution)/shard_map/ppermute | solution.py:436
  205.9 13.1 %collective-permute-done.21 = bf16[1,192,2048]{2,1,0:T(8,128)(2,1)} collective-permute-done((bf16[1,192,2048]{2,1,0:T(8,128)(2,1)}, bf16[1,192,2048]{2,1,0:T(8,128)(2,1)}, u32[]{:S(2)}, u32[]{:S(2)}) %collective-permute-start.21) | collective-permute-done | bytes 786464 | tf_op jit(solution)/shard_map/ppermute | solution.py:436
  222.6 12.4 %collective-permute-done.29 = bf16[1,512,768]{2,1,0:T(8,128)(2,1)S(1)} collective-permute-done((bf16[1,512,768]{2,1,0:T(8,128)(2,1)S(1)}, bf16[1,512,768]{2,1,0:T(8,128)(2,1)S(1)}, u32[]{:S(2)}, u32[]{:S(2)}) %collective-permute-start.29) | collective-permute-done | bytes 786464 | tf_op jit(solution)/shard_map/ppermute | solution.py:436
  237.5 7.2 %fusion.5 = f32[8,128,2048]{2,1,0:T(8,128)} fusion(bf16[8,128,768]{2,1,0:T(8,128)(2,1)} %all-to-all-done.2, bf16[2048,768]{1,0:T(8,128)(2,1)S(1)} %copy-done.81), kind=kOutput, calls=%fused_computation.24 | convolution fusion | flops 3221225472 | bytes 13107200 | tf_op jit(solution)/shard_map/sid,fd->sif/dot_general | solution.py:638
  244.7 9.3 %fusion.11 = f32[8,128,2048]{2,1,0:T(8,128)} fusion(bf16[8,128,768]{2,1,0:T(8,128)(2,1)} %all-to-all-done, bf16[768,2048]{1,0:T(8,128)(2,1)} %get-tuple-element.40), kind=kOutput, calls=%fused_computation.30 | convolution fusion | flops 3221225472 | bytes 13107200 | tf_op jit(solution)/shard_map/sid,df->sif/dot_general | solution.py:614
  254.0 12.4 %multiply_convert_fusion.2 = (bf16[8,128,2048]{2,1,0:T(8,128)(2,1)S(1)}, bf16[8,128,2048]{2,1,0:T(8,128)(2,1)S(1)}, bf16[8,128,2048]{2,1,0:T(8,128)(2,1)}) fusion(f32[8,128,2048]{2,1,0:T(8,128)} %fusion.5, f32[8,128,2048]{2,1,0:T(8,128)} %fusion.11, bf16[8,128,768]{2,1,0:T(8,128)(2,1)} %all-to-all-done, bf16[768,2048]{1,0:T(8,128)(2,1)S(1)} %copy-done.83), kind=kOutput, calls=%fused_computation.9 | convolution fusion | flops 3252682752 | bytes 34078720 | tf_op jit(solution)/shard_map/sid,df->sif/dot_general | solution.py:613
  290.7 5.2 bitcast_convert_fusion.2
  296.2 5.3 bitcast_convert_fusion.1
  307.4 7.2 %collective-permute-done.15 = bf16[192,512]{1,0:T(8,128)(2,1)S(1)} collective-permute-done((bf16[192,512]{1,0:T(8,128)(2,1)S(1)}, bf16[192,512]{1,0:T(8,128)(2,1)S(1)}, u32[]{:S(2)}, u32[]{:S(2)}) %collective-permute-start.15) | collective-permute-done | bytes 196640 | tf_op jit(solution)/shard_map/ppermute | solution.py:436
  329.6 8.2 %collective-permute-done.24 = bf16[192,256]{1,0:T(8,128)(2,1)S(1)} collective-permute-done((bf16[192,256]{1,0:T(8,128)(2,1)S(1)}, bf16[192,256]{1,0:T(8,128)(2,1)S(1)}, u32[]{:S(2)}, u32[]{:S(2)}) %collective-permute-start.24) | collective-permute-done | bytes 98336 | tf_op jit(solution)/shard_map/ppermute | solution.py:436
  366.5 6.3 %collective-permute-done.35 = bf16[256,768]{1,0:T(8,128)(2,1)S(1)} collective-permute-done((bf16[256,768]{1,0:T(8,128)(2,1)S(1)}, bf16[256,768]{1,0:T(8,128)(2,1)S(1)}, u32[]{:S(2)}, u32[]{:S(2)}) %collective-permute-start.35) | collective-permute-done | bytes 393248 | tf_op jit(solution)/shard_map/ppermute | solution.py:436
  408.9 12.1 %multiply_reduce_fusion = (f32[12,256]{1,0:T(8,128)S(1)}, f32[12,256,1024]{2,1,0:T(8,128)}) fusion(f32[12,256,1024]{2,1,0:T(8,128)} %fusion.102, f32[12,256]{1,0:T(8,128)S(1)} %reduce.8, pred[256,1024]{1,0:T(8,128)(4,1)S(1)} %copy-done.38, bf16[256,12,64]{0,2,1:T(8,128)(2,1)} %bitcast.279, bf16[1024,12,64]{0,2,1:T(8,128)(2,1)} %bitcast.261), kind=kOutput, calls=%fused_computation.6 | convolution fusion | flops 418378752 | bytes 27418624 | tf_op jit(solution)/shard_map/qhd,khd->hqk/dot_general | solution.py:687
  422.1 7.2 %multiply_convert_fusion = bf16[12,256,1024]{2,1,0:T(8,128)(2,1)S(1)} fusion(f32[12,256,1024]{2,1,0:T(8,128)} %get-tuple-element.105, f32[12,256,1024]{2,1,0:T(8,128)S(1)} %bitcast.247, f32[12,256]{1,0:T(8,128)S(1)} %get-tuple-element.104, f32[12,256]{1,0:T(8,128)S(1)} %reduce.8, pred[256,1024]{1,0:T(8,128)(4,1)S(1)} %copy-done.38), kind=kLoop, calls=%fused_computation.5 | loop fusion | flops 18874368 | bytes 31744000 | tf_op jit(solution)/shard_map/convert_element_type | solution.py:691
  450.9 13.2 %collective-permute-done.39 = bf16[1,192,2048]{2,1,0:T(8,128)(2,1)S(1)} collective-permute-done((bf16[1,192,2048]{2,1,0:T(8,128)(2,1)S(1)}, bf16[1,192,2048]{2,1,0:T(8,128)(2,1)S(1)}, u32[]{:S(2)}, u32[]{:S(2)}) %collective-permute-start.39) | collective-permute-done | bytes 786464 | tf_op jit(solution)/shard_map/ppermute | solution.py:436
  490.3 6.6 %collective-permute-done.5 = bf16[1,192,4,768]{3,1,2,0:T(8,128)(2,1)} collective-permute-done((bf16[1,192,4,768]{3,1,2,0:T(8,128)(2,1)}, bf16[1,192,4,768]{3,1,2,0:T(8,128)(2,1)}, u32[]{:S(2)}, u32[]{:S(2)}) %collective-permute-start.5) | collective-permute-done | bytes 1179680 | tf_op jit(solution)/shard_map/ppermute | solution.py:436
  505.4 7.2 %collective-permute-done.6 = bf16[384,768]{1,0:T(8,128)(2,1)} collective-permute-done((bf16[384,768]{1,0:T(8,128)(2,1)}, bf16[384,768]{1,0:T(8,128)(2,1)}, u32[]{:S(2)}, u32[]{:S(2)}) %collective-permute-start.6) | collective-permute-done | bytes 589856 | tf_op jit(solution)/shard_map/ppermute | solution.py:436
  525.4 6.6 %collective-permute-done.8 = bf16[96,768]{1,0:T(8,128)(2,1)S(1)} collective-permute-done((bf16[96,768]{1,0:T(8,128)(2,1)S(1)}, bf16[96,768]{1,0:T(8,128)(2,1)S(1)}, u32[]{:S(2)}, u32[]{:S(2)}) %collective-permute-start.8) | collective-permute-done | bytes 147488 | tf_op jit(solution)/shard_map/ppermute | solution.py:436
  533.1 5.9 %collective-permute-done.9 = bf16[96,768]{1,0:T(8,128)(2,1)S(1)} collective-permute-done((bf16[96,768]{1,0:T(8,128)(2,1)S(1)}, bf16[96,768]{1,0:T(8,128)(2,1)S(1)}, u32[]{:S(2)}, u32[]{:S(2)}) %collective-permute-start.9) | collective-permute-done | bytes 147488 | tf_op jit(solution)/shard_map/ppermute | solution.py:436
  548.8 21.6 %psum.7 = bf16[192,2]{0,1:T(2,128)(2,1)S(1)} all-reduce(bf16[192,2]{0,1:T(2,128)(2,1)S(1)} %bitcast.287), channel_id=1, replica_groups=mesh['expert'=8,'shard'=4] {'expert'}, use_global_device_ids=true, to_apply=%region_17.18 | all-reduce | flops 384 | bytes 1536 | tf_op jit(solution)/shard_map/psum | solution.py:730
  (438 shorter events, 272.4 us)
Async XLA Ops:
  16.8 170.1 %all-to-all-start.2 = ((bf16[8,128,768]{2,1,0:T(8,128)(2,1)}), bf16[8,128,768]{2,1,0:T(8,128)(2,1)}, u32[]{:S(2)}, u32[]{:S(2)}) async-start(bf16[8,128,768]{2,1,0:T(8,128)(2,1)} %bitcast.17), calls=%async_computation.2 | async-start | bytes 3145728 | tf_op jit(solution)/shard_map/all_to_all | solution.py:637
  138.7 39.0 %collective-permute-start.12 = (bf16[2,1,192,2048]{3,2,1,0:T(8,128)(2,1)}, bf16[2,1,192,2048]{3,2,1,0:T(8,128)(2,1)}, u32[]{:S(2)}, u32[]{:S(2)}) collective-permute-start(bf16[2,1,192,2048]{3,2,1,0:T(8,128)(2,1)} %constant_dynamic-slice_fusion.11), channel_id=1, source_target_pairs={{0,1},{1,0},{2,3},{3,2},{4,5},{5,4},{6,7},{7,6},{8,9},{9,8},{10,11... | collective-permute-start | bytes 4718600 | tf_op jit(solution)/shard_map/ppermute | solution.py:436
  142.3 39.7 %collective-permute-start.20 = (bf16[2,1,192,2048]{3,2,1,0:T(8,128)(2,1)}, bf16[2,1,192,2048]{3,2,1,0:T(8,128)(2,1)}, u32[]{:S(2)}, u32[]{:S(2)}) collective-permute-start(bf16[2,1,192,2048]{3,2,1,0:T(8,128)(2,1)} %constant_dynamic-slice_fusion.8), channel_id=1, source_target_pairs={{0,1},{1,0},{2,3},{3,2},{4,5},{5,4},{6,7},{7,6},{8,9},{9,8},{10,11... | collective-permute-start | bytes 4718600 | tf_op jit(solution)/shard_map/ppermute | solution.py:436
  144.8 47.9 %collective-permute-start.28 = (bf16[2,1,512,768]{3,2,1,0:T(8,128)(2,1)}, bf16[2,1,512,768]{3,2,1,0:T(8,128)(2,1)}, u32[]{:S(2)}, u32[]{:S(2)}) collective-permute-start(bf16[2,1,512,768]{3,2,1,0:T(8,128)(2,1)} %constant_dynamic-slice_fusion.5), channel_id=1, source_target_pairs={{0,1},{1,0},{2,3},{3,2},{4,5},{5,4},{6,7},{7,6},{8,9},{9,8},{10,11... | collective-permute-start | bytes 4718600 | tf_op jit(solution)/shard_map/ppermute | solution.py:436
  185.4 33.6 %collective-permute-start.21 = (bf16[1,192,2048]{2,1,0:T(8,128)(2,1)}, bf16[1,192,2048]{2,1,0:T(8,128)(2,1)}, u32[]{:S(2)}, u32[]{:S(2)}) collective-permute-start(bf16[1,192,2048]{2,1,0:T(8,128)(2,1)} %dynamic-slice_bitcast_fusion.5), channel_id=1, source_target_pairs={{0,2},{1,3},{2,0},{3,1},{4,6},{5,7},{6,4},{7,5},{8,10},{9,11},{10,... | collective-permute-start | bytes 2359304 | tf_op jit(solution)/shard_map/ppermute | solution.py:436
  186.9 57.8 %all-to-all-start = ((bf16[8,128,768]{2,1,0:T(8,128)(2,1)}), bf16[8,128,768]{2,1,0:T(8,128)(2,1)}, u32[]{:S(2)}, u32[]{:S(2)}) async-start(bf16[8,128,768]{2,1,0:T(8,128)(2,1)} %bitcast.260), calls=%async_computation | async-start | bytes 3145728 | tf_op jit(solution)/shard_map/all_to_all | solution.py:612
  194.7 40.4 %collective-permute-start.29 = (bf16[1,512,768]{2,1,0:T(8,128)(2,1)S(1)}, bf16[1,512,768]{2,1,0:T(8,128)(2,1)S(1)}, u32[]{:S(2)}, u32[]{:S(2)}) collective-permute-start(bf16[1,512,768]{2,1,0:T(8,128)(2,1)S(1)} %dynamic-slice_bitcast_fusion.4), channel_id=1, source_target_pairs={{0,2},{1,3},{2,0},{3,1},{4,6},{5,7},{6,4},{7,5},{8,10},{9,11},{10,... | collective-permute-start | bytes 2359304 | tf_op jit(solution)/shard_map/ppermute | solution.py:436
  204.4 79.3 %collective-permute-start.14 = (bf16[192,1024]{1,0:T(8,128)(2,1)}, bf16[192,1024]{1,0:T(8,128)(2,1)}, u32[]{:S(2)}, u32[]{:S(2)}) collective-permute-start(bf16[192,1024]{1,0:T(8,128)(2,1)} %dynamic-slice_bitcast_fusion.9), channel_id=1, source_target_pairs={{0,4},{4,0},{8,12},{12,8},{16,20},{20,16},{24,28},{28,24},{1,5},{5... | collective-permute-start | bytes 1179656 | tf_op jit(solution)/shard_map/ppermute | solution.py:436
  221.2 66.1 %collective-permute-start.22 = (bf16[192,1024]{1,0:T(8,128)(2,1)}, bf16[192,1024]{1,0:T(8,128)(2,1)}, u32[]{:S(2)}, u32[]{:S(2)}) collective-permute-start(bf16[192,1024]{1,0:T(8,128)(2,1)} %dynamic-slice_bitcast_fusion.8), channel_id=1, source_target_pairs={{0,4},{4,0},{8,12},{12,8},{16,20},{20,16},{24,28},{28,24},{1,5},{5... | collective-permute-start | bytes 1179656 | tf_op jit(solution)/shard_map/ppermute | solution.py:436
  236.0 52.5 %collective-permute-start.30 = (bf16[256,768]{1,0:T(8,128)(2,1)}, bf16[256,768]{1,0:T(8,128)(2,1)S(1)}, u32[]{:S(2)}, u32[]{:S(2)}) collective-permute-start(bf16[256,768]{1,0:T(8,128)(2,1)} %dynamic-slice_bitcast_fusion.7), channel_id=1, source_target_pairs={{0,4},{4,0},{8,12},{12,8},{16,20},{20,16},{24,28},{28,24},{1,5},{5... | collective-permute-start | bytes 1179656 | tf_op jit(solution)/shard_map/ppermute | solution.py:436
  279.2 108.0 %all-to-all-start.3 = ((bf16[8,128,768]{2,1,0:T(8,128)(2,1)}), bf16[8,128,768]{2,1,0:T(8,128)(2,1)S(1)}, u32[]{:S(2)}, u32[]{:S(2)}) async-start(bf16[8,128,768]{2,1,0:T(8,128)(2,1)} %add_convert_fusion.8), calls=%async_computation.3 | async-start | bytes 3145728 | tf_op jit(solution)/shard_map/all_to_all | solution.py:655
  285.1 29.4 %collective-permute-start.15 = (bf16[192,512]{1,0:T(8,128)(2,1)S(1)}, bf16[192,512]{1,0:T(8,128)(2,1)S(1)}, u32[]{:S(2)}, u32[]{:S(2)}) collective-permute-start(bf16[192,512]{1,0:T(8,128)(2,1)S(1)} %constant_dynamic-slice_fusion.10), channel_id=1, source_target_pairs={{0,8},{4,12},{8,0},{12,4},{16,24},{20,28},{24,16},{28,20},{1,9},{5... | collective-permute-start | bytes 589832 | tf_op jit(solution)/shard_map/ppermute | solution.py:436
  288.4 35.9 %collective-permute-start.23 = (bf16[192,512]{1,0:T(8,128)(2,1)S(1)}, bf16[192,512]{1,0:T(8,128)(2,1)S(1)}, u32[]{:S(2)}, u32[]{:S(2)}) collective-permute-start(bf16[192,512]{1,0:T(8,128)(2,1)S(1)} %constant_dynamic-slice_fusion.7), channel_id=1, source_target_pairs={{0,8},{4,12},{8,0},{12,4},{16,24},{20,28},{24,16},{28,20},{1,9},{5... | collective-permute-start | bytes 589832 | tf_op jit(solution)/shard_map/ppermute | solution.py:436
  288.6 37.8 %collective-permute-start.31 = (bf16[128,768]{1,0:T(8,128)(2,1)S(1)}, bf16[128,768]{1,0:T(8,128)(2,1)S(1)}, u32[]{:S(2)}, u32[]{:S(2)}) collective-permute-start(bf16[128,768]{1,0:T(8,128)(2,1)S(1)} %constant_dynamic-slice_fusion.4), channel_id=1, source_target_pairs={{0,8},{4,12},{8,0},{12,4},{16,24},{20,28},{24,16},{28,20},{1,9},{5... | collective-permute-start | bytes 589832 | tf_op jit(solution)/shard_map/ppermute | solution.py:436
  296.1 84.1 %collective-permute-start.36 = (bf16[2,1,192,2048]{3,2,1,0:T(8,128)(2,1)S(1)}, bf16[2,1,192,2048]{3,2,1,0:T(8,128)(2,1)S(1)}, u32[]{:S(2)}, u32[]{:S(2)}) collective-permute-start(bf16[2,1,192,2048]{3,2,1,0:T(8,128)(2,1)S(1)} %constant_dynamic-slice_fusion.2), channel_id=1, source_target_pairs={{0,1},{1,0},{2,3},{3,2},{4,5},{5,4},{6,7},{7,6},{8,9},{9,8},{10,11... | collective-permute-start | bytes 4718600 | tf_op jit(solution)/shard_map/ppermute | solution.py:436
  301.7 83.8 %collective-permute-start.38 = (bf16[2,1,192,2048]{3,2,1,0:T(8,128)(2,1)S(1)}, bf16[2,1,192,2048]{3,2,1,0:T(8,128)(2,1)S(1)}, u32[]{:S(2)}, u32[]{:S(2)}) collective-permute-start(bf16[2,1,192,2048]{3,2,1,0:T(8,128)(2,1)S(1)} %constant_dynamic-slice_fusion.1), channel_id=1, source_target_pairs={{0,1},{1,0},{2,3},{3,2},{4,5},{5,4},{6,7},{7,6},{8,9},{9,8},{10,11... | collective-permute-start | bytes 4718600 | tf_op jit(solution)/shard_map/ppermute | solution.py:436
  359.9 22.6 %collective-permute-start.40 = (bf16[2,1,512,768]{3,2,1,0:T(8,128)(2,1)S(1)}, bf16[2,1,512,768]{3,2,1,0:T(8,128)(2,1)S(1)}, u32[]{:S(2)}, u32[]{:S(2)}) collective-permute-start(bf16[2,1,512,768]{3,2,1,0:T(8,128)(2,1)S(1)} %constant_dynamic-slice_fusion), channel_id=1, source_target_pairs={{0,1},{1,0},{2,3},{3,2},{4,5},{5,4},{6,7},{7,6},{8,9},{9,8},{10,11... | collective-permute-start | bytes 4718600 | tf_op jit(solution)/shard_map/ppermute | solution.py:436
  381.9 66.5 %collective-permute-start.37 = (bf16[1,192,2048]{2,1,0:T(8,128)(2,1)}, bf16[1,192,2048]{2,1,0:T(8,128)(2,1)}, u32[]{:S(2)}, u32[]{:S(2)}) collective-permute-start(bf16[1,192,2048]{2,1,0:T(8,128)(2,1)} %dynamic-slice_bitcast_fusion.3), channel_id=1, source_target_pairs={{0,2},{1,3},{2,0},{3,1},{4,6},{5,7},{6,4},{7,5},{8,10},{9,11},{10,... | collective-permute-start | bytes 2359304 | tf_op jit(solution)/shard_map/ppermute | solution.py:436
  384.0 61.9 %collective-permute-start.41 = (bf16[1,512,768]{2,1,0:T(8,128)(2,1)}, bf16[1,512,768]{2,1,0:T(8,128)(2,1)}, u32[]{:S(2)}, u32[]{:S(2)}) collective-permute-start(bf16[1,512,768]{2,1,0:T(8,128)(2,1)} %dynamic-slice_bitcast_fusion.1), channel_id=1, source_target_pairs={{0,2},{1,3},{2,0},{3,1},{4,6},{5,7},{6,4},{7,5},{8,10},{9,11},{10,... | collective-permute-start | bytes 2359304 | tf_op jit(solution)/shard_map/ppermute | solution.py:436
  387.2 84.6 %all-to-all-start.1 = ((bf16[8,128,768]{2,1,0:T(8,128)(2,1)}), bf16[8,128,768]{2,1,0:T(8,128)(2,1)S(1)}, u32[]{:S(2)}, u32[]{:S(2)}) async-start(bf16[8,128,768]{2,1,0:T(8,128)(2,1)} %fusion.21), calls=%async_computation.1 | async-start | bytes 3145728 | tf_op jit(solution)/shard_map/all_to_all | solution.py:617
  443.9 24.6 %collective-permute-start.4 = (bf16[2,1,192,4,768]{4,2,1,0,3:T(8,128)(2,1)S(1)}, bf16[2,1,192,4,768]{4,2,1,0,3:T(8,128)(2,1)S(1)}, u32[]{:S(2)}, u32[]{:S(2)}) collective-permute-start(bf16[2,1,192,4,768]{4,2,1,0,3:T(8,128)(2,1)S(1)} %constant_dynamic-slice_fusion.15), channel_id=1, source_target_pairs={{0,1},{1,0},{2,3},{3,2},{4,5},{5,4},{6,7},{7,6},{8,9},{9,8},{10,11... | collective-permute-start | bytes 7077896 | tf_op jit(solution)/shard_map/ppermute | solution.py:436
  470.3 26.6 %collective-permute-start.5 = (bf16[1,192,4,768]{3,1,2,0:T(8,128)(2,1)}, bf16[1,192,4,768]{3,1,2,0:T(8,128)(2,1)}, u32[]{:S(2)}, u32[]{:S(2)}) collective-permute-start(bf16[1,192,4,768]{3,1,2,0:T(8,128)(2,1)} %dynamic-slice_bitcast_fusion), channel_id=1, source_target_pairs={{0,2},{1,3},{2,0},{3,1},{4,6},{5,7},{6,4},{7,5},{8,10},{9,11},{10,... | collective-permute-start | bytes 3538952 | tf_op jit(solution)/shard_map/ppermute | solution.py:436
  477.6 23.8 %collective-permute-start = (bf16[2,1,256,768]{3,2,1,0:T(8,128)(2,1)}, bf16[2,1,256,768]{3,2,1,0:T(8,128)(2,1)}, u32[]{:S(2)}, u32[]{:S(2)}) collective-permute-start(bf16[2,1,256,768]{3,2,1,0:T(8,128)(2,1)} %constant_dynamic-slice_fusion.20), channel_id=1, source_target_pairs={{0,1},{1,0},{2,3},{3,2},{4,5},{5,4},{6,7},{7,6},{8,9},{9,8},{10,11... | collective-permute-start | bytes 2359304 | tf_op jit(solution)/shard_map/ppermute | solution.py:436
  546.1 24.9 %collective-permute-start.11 = (bf16[384,768]{1,0:T(8,128)(2,1)S(1)}, bf16[384,768]{1,0:T(8,128)(2,1)S(1)}, u32[]{:S(2)}, u32[]{:S(2)}) collective-permute-start(bf16[384,768]{1,0:T(8,128)(2,1)S(1)} %maximum_select_fusion.4), channel_id=1, source_target_pairs={{0,4},{4,0},{8,12},{12,8},{16,20},{20,16},{24,28},{28,24},{1,5},{5... | collective-permute-start | bytes 1769480 | tf_op jit(solution)/shard_map/ppermute | solution.py:436
  (111 other events, 1032.4 us)

commit v3 on v2

--- a/solution.py
+++ b/solution.py
@@ -22,7 +22,8 @@
 SPLIT_X = ("sg", "su", "sd")
 LATE = ("eg", "eu", "ed")
 NAMES = DIRECT + EARLY + SPREAD + LATE
-IN_VMEM = DIRECT + EARLY + ("wo",)
+PASSING = DIRECT + ("sg", "su", "sd")
+KEPT = EARLY + ("wo",) + LATE
 
 
 def dense_product(left, right):
@@ -104,11 +105,22 @@
 def first_kernel(*refs):
     count = len(NAMES)
     own = dict(zip(NAMES, refs[:count]))
-    segment_row, segment_col, padding_row, cosine_ref, sine_ref = refs[count : count + 5]
-    refs = refs[count + 5 :]
-    full = dict(zip(NAMES, refs[:count]))
-    gain_ref, normed_ref, query_ref, key_ref, value_ref, lse_ref, attended_ref, mixed_ref, ffn_ref = refs[count : count + 9]
-    (own_sem, y_send, y_recv, x_send, x_recv, z_send, z_recv, core_send, core_recv) = refs[count + 9 :]
+    segment_row, segment_col, padding_row, cosine_ref, sine_ref, cot_ref, logit_ref, route_ref, lane_route_ref = refs[
+        count : count + 9
+    ]
+    refs = refs[count + 9 :]
+    full = dict(zip(KEPT, refs[: len(KEPT)]))
+    refs = refs[len(KEPT) :]
+    gain_ref, normed_ref, query_ref, key_ref, value_ref, lse_ref, attended_ref, mixed_ref, ffn_ref = refs[:9]
+    rows_got, grads_got, shared_ref, ffn_grad_ref, *shared_work = refs[9:16]
+    refs = refs[16:]
+    full.update(zip(PASSING, refs[: len(PASSING)]))
+    refs = refs[len(PASSING) :]
+    shared_core = refs[:3]
+    refs = refs[3:]
+    rows_put, grads_put = refs[:2]
+    (own_sem, y_send, y_recv, x_send, x_recv, z_send, z_recv, core_send, core_recv) = refs[2:11]
+    row_sems, grad_sems, share_send, share_recv = refs[11:13], refs[13:15], refs[15], refs[16]
     number = {name: index for index, name in enumerate(NAMES)}
     expert, shard = (lax.axis_index("expert"), lax.axis_index("shard"))
     zed, ex = (expert // 2, expert % 2)
@@ -119,18 +131,9 @@
     z_up, z_down = (((expert + 2) % 8, shard), ((expert + 6) % 8, shard))
 
     barrier = pltpu.get_barrier_semaphore()
-    for peer in (y_peer, core_peer, x_peer):
+    for peer in (y_peer, core_peer) + tuple(((expert + step) % 8, shard) for step in range(1, 8)):
         pl.semaphore_signal(barrier, inc=1, device_id=peer, device_id_type=MESH)
-
-    @pl.when(zed < 3)
-    def _():
-        pl.semaphore_signal(barrier, inc=1, device_id=z_up, device_id_type=MESH)
-
-    @pl.when(zed > 0)
-    def _():
-        pl.semaphore_signal(barrier, inc=1, device_id=z_down, device_id_type=MESH)
-
-    pl.semaphore_wait(barrier, 3 + jnp.minimum(3 - zed, 1) + jnp.minimum(zed, 1))
+    pl.semaphore_wait(barrier, 9)
 
     def part_of(block, base, name, at_z, at_x):
         rows = own[name].shape[0]
@@ -264,6 +267,40 @@
         settle_core(name, 1, None, 1 - ex)
         wait_for(mine(name, None, ex), y_send.at[number[name]])
         wait_for(place(name, other, None, ex), x_send.at[number[name], 0])
+
+    lane_routes = lane_route_ref[...]
+    expert_at = lax.broadcasted_iota(jnp.int32, (8, tokens), 0)
+    named = ((lane_routes[0:1] == expert_at) | (lane_routes[1:2] == expert_at)).astype(jnp.float32)
+    before = lax.broadcasted_iota(jnp.int32, (tokens, tokens), 0) < lax.broadcasted_iota(jnp.int32, (tokens, tokens), 1)
+    rank = dense_product(named.astype(jnp.bfloat16), before.astype(jnp.bfloat16))
+    slot_of = jnp.where(named > 0.0, rank, -1.0).astype(jnp.int32)
+    capacity = rows_put.shape[1]
+
+    def picks(target):
+        slot_at = lax.broadcasted_iota(jnp.int32, (capacity, tokens), 0)
+        return slot_at == slot_of[target : target + 1]
+
+    def dispatch(put, got, sems):
+        for step in range(1, 8):
+            target = (expert + step) % 8
+            send(put.at[target], got.at[expert], sems[0].at[step], sems[1].at[step], (target, shard))
+        got[pl.ds(expert, 1)] = put[pl.ds(expert, 1)]
+
+    def settle_dispatch(put, got, sems):
+        for step in range(1, 8):
+            wait_for(put.at[(expert + step) % 8], sems[0].at[step])
+            wait_for(got.at[(expert + 8 - step) % 8], sems[1].at[step])
+
+    gate_probs = gate_columns(logit_ref[...])
+    cot = cot_ref[...]
+    route_grads = [(gate * cot.astype(jnp.float32)).astype(jnp.bfloat16) for gate in gate_probs]
+    for target in range(8):
+        chosen = picks(target)
+        grads_put[target] = sum(
+            dense_product((chosen & (lane_routes[k : k + 1] == target)).astype(jnp.bfloat16), route_grads[k])
+            for k in range(TOP)
+        ).astype(jnp.bfloat16)
+    dispatch(grads_put, grads_got, grad_sems)
 
     def key_block(block, carry):
         rows = pl.ds(pl.multiple_of(block * tokens, tokens), tokens)
@@ -342,11 +379,12 @@
     rows_in = own["hid"][...].astype(jnp.float32)
     mixed = rows_in + dense_product(attended_ref[...], full["wo"][...])
     mixed_ref[...] = mixed
-    ffn_ref[...] = (mixed * rms_scale(mixed) * gain_second).astype(jnp.bfloat16)
-
-    for name in LATE:
-        wait_for(place(name, other), y_recv.at[number[name]])
-        to_core(name, 0)
+    ffn = (mixed * rms_scale(mixed) * gain_second).astype(jnp.bfloat16)
+    ffn_ref[...] = ffn
+    for target in range(8):
+        rows_put[target] = dense_product(picks(target).astype(jnp.bfloat16), ffn).astype(jnp.bfloat16)
+    dispatch(rows_put, rows_got, row_sems)
+
     settle_ring(SPLIT_X)
 
     def sent(step, direction, condition, at_z):
@@ -358,12 +396,66 @@
     for step in range(3):
         sent(step, 0, (zed < 3) & (zed >= step), zed - step)
         sent(step, 1, (zed > 0) & (zed + step <= 3), zed + step)
+    shared_ref[...] = jnp.zeros_like(shared_ref)
+    ffn_grad_ref[...] = jnp.zeros_like(ffn_grad_ref)
+
+    def shared_block(block, carry):
+        cut = pl.ds(pl.multiple_of(block * 512, 512), 512)
+        normed = ffn_ref[...]
+        gate, up, down = full["sg"][:, cut], full["su"][:, cut], full["sd"][cut, :]
+        pre, lin = dense_product(normed, gate), dense_product(normed, up)
+        middle = (jax.nn.silu(pre) * lin).astype(jnp.bfloat16)
+        shared_ref[...] += dense_product(middle, down)
+        pre_grad, lin_grad = swiglu_back(product_t(cot_ref[...], down), pre, lin)
+        ffn_grad_ref[...] += product_t(pre_grad, gate) + product_t(lin_grad, up)
+        full["sg"][:, cut] = t_product(normed, pre_grad).astype(jnp.bfloat16)
+        full["su"][:, cut] = t_product(normed, lin_grad).astype(jnp.bfloat16)
+        full["sd"][cut, :] = t_product(middle, cot_ref[...]).astype(jnp.bfloat16)
+        return carry
+
+    lax.fori_loop(0, full["sg"].shape[1] // 512, shared_block, 0)
+
+    def shard_rows(ref, y_of, core_of):
+        rows = ref.shape[0] // 4
+        return ref.at[pl.ds((y_of * 2 + core_of) * rows, rows)]
+
+    core = shard % 2
+    shared_grads = (full["sg"], full["su"], full["sd"])
+    for index in range(3):
+        for y_of in range(2):
+            send(
+                shard_rows(shared_grads[index], y_of, 1 - core),
+                shared_core[index].at[y_of],
+                share_send.at[index, y_of],
+                share_recv.at[index, y_of],
+                core_peer,
+            )
+
+    for name in LATE:
+        wait_for(place(name, other), y_recv.at[number[name]])
+        to_core(name, 0)
+
     for name in DIRECT:
         wait_for(own[name], y_send.at[number[name]])
     settle_own(LATE)
     for name in LATE:
         wait_for(own[name], y_send.at[number[name]])
         settle_core(name, 0)
+    for index in range(3):
+        for y_of in range(2):
+            wait_for(shared_core[index].at[y_of], share_recv.at[index, y_of])
+            add_rows(shared_work[index].at[y_of], shard_rows(shared_grads[index], y_of, core), shared_core[index].at[y_of])
+            wait_for(shard_rows(shared_grads[index], y_of, 1 - core), share_send.at[index, y_of])
+    settle_dispatch(grads_put, grads_got, grad_sems)
+    settle_dispatch(rows_put, rows_got, row_sems)
+
+
+def gate_columns(logits):
+    first, second = logits[:, 0:1], logits[:, 1:2]
+    top = jnp.maximum(first, second)
+    first, second = jnp.exp(first - top), jnp.exp(second - top)
+    total = first + second
+    return first / total, second / total
 
 
 def allowed_mask(query_start, key_start, query_segment, key_segment, key_padding):
@@ -379,7 +471,7 @@
     )
 
 
-def first_part(hidden, gains, dense, experts, segment, padding):
+def first_part(hidden, gains, dense, experts, segment, padding, cotangent, logits, routes):
     tokens, width = hidden.shape
     bfloat, single = jnp.bfloat16, jnp.float32
     wq, wk, wv, wo, sg, su, sd = dense
@@ -391,9 +483,14 @@
     in_hbm, in_vmem = pl.BlockSpec(memory_space=pl.ANY), pl.BlockSpec(memory_space=pltpu.VMEM)
     dma = pltpu.SemaphoreType.DMA
     shape = jax.ShapeDtypeStruct
+    whole = {name: shape((4 * block.shape[0], block.shape[1]), block.dtype) for name, block in zip(NAMES, blocks)}
+    middle = sg.shape[1]
+    capacity = max(2, 2 * tokens * TOP // 8)
+    routed = (8, capacity, width)
+    halved = [(2,) + block.shape for block in (sg, su, sd)]
     out = pl.pallas_call(
         first_kernel,
-        out_shape=[shape((4 * block.shape[0], block.shape[1]), block.dtype) for block in blocks]
+        out_shape=[whole[name] for name in KEPT]
         + [
             shape((16, width), single),
             shape((4 * tokens, width), bfloat),
@@ -404,10 +501,18 @@
             shape((tokens, width), bfloat),
             shape((tokens, width), single),
             shape((tokens, width), bfloat),
-        ],
-        in_specs=[in_vmem] * (count + 5),
-        out_specs=[in_vmem if name in IN_VMEM else in_hbm for name in NAMES] + [in_vmem] * 9,
-        scratch_shapes=[
+            shape(routed, bfloat),
+            shape(routed, bfloat),
+            shape((tokens, width), single),
+            shape((tokens, width), single),
+        ]
+        + [shape(one, bfloat) for one in halved],
+        in_specs=[in_vmem] * (count + 9),
+        out_specs=[in_hbm if name in LATE else in_vmem for name in KEPT] + [in_vmem] * 16,
+        scratch_shapes=[pltpu.VMEM(whole[name].shape, whole[name].dtype) for name in PASSING]
+        + [pltpu.VMEM(one, bfloat) for one in halved]
+        + [pltpu.VMEM(routed, bfloat)] * 2
+        + [
             dma((count,)),
             dma((count,)),
             dma((count,)),
@@ -417,9 +522,11 @@
             dma((count, 2, 3)),
             dma((count, 15)),
             dma((count, 15)),
-        ],
-        compiler_params=pltpu.CompilerParams(collective_id=0, has_side_effects=True, vmem_limit_bytes=56 << 20),
-        cost_estimate=pl.CostEstimate(flops=5000000000, bytes_accessed=47000000, transcendentals=3000000),
+        ]
+        + [dma((8,))] * 4
+        + [dma((3, 2))] * 2,
+        compiler_params=pltpu.CompilerParams(collective_id=0, has_side_effects=True, vmem_limit_bytes=60 << 20),
+        cost_estimate=pl.CostEstimate(flops=15000000000, bytes_accessed=47000000, transcendentals=3000000),
     )(
         *blocks,
         segment[None, :],
@@ -427,8 +534,332 @@
         padding[None, :],
         jnp.asarray(cosine),
         jnp.asarray(sine),
-    )
-    return dict(zip(NAMES, out[:count])), out[count:]
+        cotangent,
+        logits,
+        routes,
+        routes.T,
+    )
+    return dict(zip(KEPT, out)), out[len(KEPT) :]
+
+
+def add_into(target, first, second):
+    rows = first.shape[-2]
+    strip = 64
+
+    def body(index, carry):
+        at = pl.ds(pl.multiple_of(index * strip, strip), strip)
+        for lead in range(first.shape[0]):
+            total = first[lead, at, :].astype(jnp.float32) + second[lead, at, :].astype(jnp.float32)
+            target[lead, at, :] = total.astype(target.dtype)
+        return carry
+
+    lax.fori_loop(0, rows // strip, body, 0)
+
+
+class PlaneSum:
+    def __init__(self, work, out, receive, send_sem, recv_sem, bits, peers, order, by_rows):
+        self.work, self.out, self.receive = work, out, receive
+        self.send_sem, self.recv_sem, self.bits, self.peers, self.order = send_sem, recv_sem, bits, peers, order
+        self.by_rows = by_rows
+        self.whole_y = True
+        self.size = work.shape[1 if by_rows else 2]
+        self.offset = 0
+        self.trail = []
+
+    def region(self, ref, offset, size, y=None):
+        lead = pl.ds(0, ref.shape[0]) if y is None else pl.ds(y, 1)
+        unit = 16 if self.by_rows else 128
+        at = pl.ds(offset if isinstance(offset, int) else pl.multiple_of(offset, unit), size)
+        return ref.at[lead, at, :] if self.by_rows else ref.at[lead, :, at]
+
+    def halves(self, axis):
+        bit = self.bits[axis]
+        if axis == "y":
+            return (self.offset, self.size, bit), (self.offset, self.size, 1 - bit)
+        half = self.size // 2
+        y = None if self.whole_y else self.bits["y"]
+        return (self.offset + bit * half, half, y), (self.offset + (1 - bit) * half, half, y)
+
+    def start(self, step):
+        axis = self.order[step]
+        _, give = self.halves(axis)
+        send(
+            self.region(self.work, *give),
+            self.receive[step],
+            self.send_sem.at[step],
+            self.recv_sem.at[step],
+            self.peers[axis],
+        )
+
+    def finish(self, step):
+        axis = self.order[step]
+        keep, give = self.halves(axis)
+        wait_for(self.receive[step], self.recv_sem.at[step])
+        last = step == len(self.order) - 1
+        kept = self.region(self.work, *keep)
+        target = self.region(self.out, keep[0], keep[1]) if last else kept
+        add_into(target, kept, self.receive[step])
+        wait_for(self.region(self.work, *give), self.send_sem.at[step])
+        if axis == "y":
+            self.whole_y = False
+        else:
+            self.trail.append((axis, self.offset, self.size))
+            self.offset, self.size = keep[0], keep[1]
+
+    def back_start(self, step):
+        axis, _, _ = self.trail[-1 - step]
+        part = self.region(self.out, self.offset, self.size)
+        at = len(self.order) + step
+        send(part, part, self.send_sem.at[at], self.recv_sem.at[at], self.peers[axis])
+
+    def back_finish(self, step):
+        axis, offset, size = self.trail[-1 - step]
+        at = len(self.order) + step
+        half = size // 2
+        wait_for(self.region(self.out, self.offset, self.size), self.send_sem.at[at])
+        wait_for(self.region(self.out, offset + (1 - self.bits[axis]) * half, half), self.recv_sem.at[at])
+        self.offset, self.size = offset, size
+
+
+def receive_shapes(shape, order, by_rows):
+    lead, rows, columns = shape
+    result = []
+    for axis in order:
+        if axis == "y":
+            lead = 1
+        elif by_rows:
+            rows //= 2
+        else:
+            columns //= 2
+        result.append((lead, rows, columns))
+    return result
+
+
+SHARED_ORDER = (("y", "x", "z1", "z2"), ("x", "z1", "y", "z2"), ("z1", "y", "x", "z2"))
+
+
+def plane_places():
+    expert, shard = (lax.axis_index("expert"), lax.axis_index("shard"))
+    zed, ex, why, core = (expert // 2, expert % 2, shard // 2, shard % 2)
+    bits = {"x": ex, "z1": zed % 2, "z2": zed // 2, "y": why}
+    peers = {
+        "x": (expert + 1 - 2 * ex, shard),
+        "z1": (expert + 2 - 4 * (zed % 2), shard),
+        "z2": ((expert + 4) % 8, shard),
+        "y": (expert, (shard + 2) % 4),
+        "core": (expert, shard + 1 - 2 * core),
+    }
+    return expert, shard, zed, core, bits, peers
+
+
+def enter(peers):
+    barrier = pltpu.get_barrier_semaphore()
+    for peer in peers:
+        pl.semaphore_signal(barrier, inc=1, device_id=peer, device_id_type=MESH)
+    pl.semaphore_wait(barrier, len(peers))
+
+
+def second_kernel(*refs):
+    rows_ref, grads_ref, *weights_in = refs[:5]
+    shared_in = refs[5:8]
+    rows_back, grads_back = refs[8:10]
+    expert_out, shared_out = refs[10:13], refs[13:16]
+    weights, shared_work = refs[16:19], refs[19:22]
+    rows_put, grads_put, middle_ref, pre_ref, lin_ref, out_sum, grad_sum = refs[22:29]
+    expert_core, expert_y = refs[29:32], refs[32:35]
+    receive = [refs[35 + 4 * index : 39 + 4 * index] for index in range(3)]
+    load_sem, shared_sem, out_send, out_recv, grad_send, grad_recv, core_send, core_recv, y_send, y_recv, sum_send, sum_recv = refs[47:]
+    expert, shard, zed, core, bits, peers = plane_places()
+    why = bits["y"]
+    for index in range(3):
+        pltpu.make_async_copy(weights_in[index], weights[index], load_sem.at[index]).start()
+        pltpu.make_async_copy(shared_in[index], shared_work[index], shared_sem.at[index]).start()
+    enter((peers["y"], peers["core"]) + tuple(((expert + step) % 8, shard) for step in range(1, 8)))
+    sums = [
+        PlaneSum(
+            shared_work[index],
+            shared_out[index],
+            receive[index],
+            sum_send.at[index],
+            sum_recv.at[index],
+            bits,
+            peers,
+            SHARED_ORDER[index],
+            index == 2,
+        )
+        for index in range(3)
+    ]
+    for index in range(3):
+        pltpu.make_async_copy(shared_in[index], shared_work[index], shared_sem.at[index]).wait()
+        sums[index].start(0)
+    for index in range(3):
+        pltpu.make_async_copy(weights_in[index], weights[index], load_sem.at[index]).wait()
+
+    _, capacity, width = rows_ref.shape
+    gate_ref, up_ref, down_ref = weights
+    middle = gate_ref.shape[1]
+    cuts = middle // 512
+
+    def block(z_from):
+        pair = pl.ds(2 * z_from, 2)
+        rows = rows_ref[pair].reshape(2 * capacity, width)
+        grads = grads_ref[pair].reshape(2 * capacity, width)
+        here = pl.ds(pl.multiple_of(z_from * 2 * capacity, 2 * capacity), 2 * capacity)
+        out_sum[...] = jnp.zeros_like(out_sum)
+        grad_sum[...] = jnp.zeros_like(grad_sum)
+
+        def body(index, carry):
+            cut = pl.ds(pl.multiple_of(index * 512, 512), 512)
+            gate, up, down = gate_ref[:, cut], up_ref[:, cut], down_ref[cut, :]
+            pre, lin = dense_product(rows, gate), dense_product(rows, up)
+            mid = (jax.nn.silu(pre) * lin).astype(jnp.bfloat16)
+            out_sum[...] += dense_product(mid, down)
+            pre_grad, lin_grad = swiglu_back(product_t(grads, down), pre, lin)
+            grad_sum[...] += product_t(pre_grad, gate) + product_t(lin_grad, up)
+            middle_ref[here, cut] = mid
+            pre_ref[here, cut] = pre_grad
+            lin_ref[here, cut] = lin_grad
+            return carry
+
+        lax.fori_loop(0, cuts, body, 0)
+        rows_put[pair] = out_sum[...].astype(jnp.bfloat16).reshape(2, capacity, width)
+        grads_put[pair] = grad_sum[...].astype(jnp.bfloat16).reshape(2, capacity, width)
+        for side in range(2):
+            source = 2 * z_from + side
+
+            @pl.when(source != expert)
+            def _():
+                send(grads_put.at[source], grads_back.at[expert], grad_send.at[source], grad_recv.at[expert], (source, shard))
+                send(rows_put.at[source], rows_back.at[expert], out_send.at[source], out_recv.at[expert], (source, shard))
+
+            @pl.when(source == expert)
+            def _():
+                rows_back[pl.ds(source, 1)] = rows_put[pl.ds(source, 1)]
+                grads_back[pl.ds(source, 1)] = grads_put[pl.ds(source, 1)]
+
+    z_order = ((zed + 2) % 4, 3 - zed, zed + 1 - 2 * (zed % 2), zed)
+    for step in range(4):
+        block(z_order[step])
+        for one in sums:
+            one.finish(step)
+            if step < 3:
+                one.start(step + 1)
+            else:
+                one.back_start(0)
+
+    rows_all, grads_all = rows_ref, grads_ref
+
+    def weight_grad(index):
+        def body(step, carry):
+            cut = pl.ds(pl.multiple_of(step * 512, 512), 512)
+            if index == 2:
+                left, right = middle_ref[:, cut], grads_all[...].reshape(8 * capacity, width)
+                down_ref[cut, :] = t_product(left, right).astype(jnp.bfloat16)
+            else:
+                left, right = rows_all[...].reshape(8 * capacity, width), (pre_ref, lin_ref)[index][:, cut]
+                weights[index][:, cut] = t_product(left, right).astype(jnp.bfloat16)
+            return carry
+
+        lax.fori_loop(0, cuts, body, 0)
+
+    def shard_rows(index, y_of, core_of):
+        rows = weights[index].shape[0] // 4
+        return weights[index].at[pl.ds((y_of * 2 + core_of) * rows, rows)]
+
+    def core_start(index):
+        for y_of in range(2):
+            send(
+                shard_rows(index, y_of, 1 - core),
+                expert_core[index].at[y_of],
+                core_send.at[index, y_of],
+                core_recv.at[index, y_of],
+                peers["core"],
+            )
+
+    def core_finish(index):
+        for y_of in range(2):
+            wait_for(expert_core[index].at[y_of], core_recv.at[index, y_of])
+            wait_for(shard_rows(index, y_of, 1 - core), core_send.at[index, y_of])
+        for y_of in range(2):
+            kept = shard_rows(index, y_of, core)
+            add_rows(expert_core[index].at[y_of], kept, expert_core[index].at[y_of])
+        send(expert_core[index].at[1 - why], expert_y[index], y_send.at[index], y_recv.at[index], peers["y"])
+
+    def y_finish(index):
+        wait_for(expert_y[index], y_recv.at[index])
+        add_rows(expert_out[index], expert_core[index].at[why], expert_y[index])
+        wait_for(expert_core[index].at[1 - why], y_send.at[index])
+
+    weight_grad(0)
+    core_start(0)
+    weight_grad(1)
+    core_finish(0)
+    core_start(1)
+    for one in sums:
+        one.back_finish(0)
+        one.back_start(1)
+    weight_grad(2)
+    core_finish(1)
+    core_start(2)
+    for one in sums:
+        one.back_finish(1)
+        one.back_start(2)
+    core_finish(2)
+    for one in sums:
+        one.back_finish(2)
+    for step in range(1, 8):
+        target, origin = (expert + step) % 8, (expert + 8 - step) % 8
+        wait_for(rows_put.at[target], out_send.at[target])
+        wait_for(grads_put.at[target], grad_send.at[target])
+        wait_for(rows_back.at[origin], out_recv.at[origin])
+        wait_for(grads_back.at[origin], grad_recv.at[origin])
+    for index in range(3):
+        y_finish(index)
+
+
+def add_rows(target, first, second):
+    def body(index, carry):
+        at = pl.ds(pl.multiple_of(index * 64, 64), 64)
+        target[at, :] = (first[at, :].astype(jnp.float32) + second[at, :].astype(jnp.float32)).astype(target.dtype)
+        return carry
+
+    lax.fori_loop(0, first.shape[0] // 64, body, 0)
+
+
+def second_part(rows, grads, weights, shared):
+    in_hbm, in_vmem = pl.BlockSpec(memory_space=pl.ANY), pl.BlockSpec(memory_space=pltpu.VMEM)
+    dma, bfloat = pltpu.SemaphoreType.DMA, jnp.bfloat16
+    shape = jax.ShapeDtypeStruct
+    count, capacity, width = rows.shape
+    middle = weights[0].shape[1]
+    quarter = [(weight.shape[0] // 4, weight.shape[1]) for weight in weights]
+    own = [(1,) + work.shape[1:] for work in shared]
+    blocks = (count * capacity, middle)
+    return pl.pallas_call(
+        second_kernel,
+        out_shape=[shape(rows.shape, bfloat)] * 2
+        + [shape(one, bfloat) for one in quarter]
+        + [shape(one, bfloat) for one in own],
+        in_specs=[in_vmem] * 2 + [in_hbm] * 6,
+        out_specs=[in_vmem] * 8,
+        scratch_shapes=[pltpu.VMEM(weight.shape, bfloat) for weight in weights]
+        + [pltpu.VMEM(work.shape, bfloat) for work in shared]
+        + [pltpu.VMEM(rows.shape, bfloat)] * 2
+        + [pltpu.VMEM(blocks, bfloat)] * 3
+        + [pltpu.VMEM((2 * capacity, width), jnp.float32)] * 2
+        + [pltpu.VMEM((2,) + one, bfloat) for one in quarter]
+        + [pltpu.VMEM(one, bfloat) for one in quarter]
+        + [
+            pltpu.VMEM(one, bfloat)
+            for index in range(3)
+            for one in receive_shapes(shared[index].shape, SHARED_ORDER[index], index == 2)
+        ]
+        + [dma((3,)), dma((3,))]
+        + [dma((8,))] * 4
+        + [dma((3, 2)), dma((3, 2)), dma((3,)), dma((3,)), dma((3, 7)), dma((3, 7))],
+        compiler_params=pltpu.CompilerParams(collective_id=1, has_side_effects=True, vmem_limit_bytes=62 << 20),
+        cost_estimate=pl.CostEstimate(flops=29000000000, bytes_accessed=30000000, transcendentals=2000000),
+    )(rows, grads, *weights, *shared)
 
 
 def swap(value, axis, bit):
@@ -522,10 +953,21 @@
             jnp.stack([gain_attn, gain_ffn]),
             (0, shard_index * gain_attn.shape[0]),
         )
-        full, rest = first_part(hidden_in[0], gain_own, dense_own, expert_own, segment_row, padding_row)
-        gains, normed_ctx, query_low, keys_ctx, values_ctx, log_total, attended, mixed_rows, normed_ffn = rest
+        full, rest = first_part(
+            hidden_in[0],
+            gain_own,
+            dense_own,
+            expert_own,
+            segment_row,
+            padding_row,
+            cotangent[0],
+            gate_logits[0],
+            routes[0],
+        )
+        gains, normed_ctx, query_low, keys_ctx, values_ctx, log_total, attended, mixed_rows, normed_ffn = rest[:9]
+        received, grad_received, shared_out, ffn_grad_shared, *shared_work = rest[9:]
         gain_first, gain_second = gains[0], gains[1]
-        w_q, w_k, w_v, w_o, s_gate, s_up, s_down = (full[name] for name in ("wq", "wk", "wv", "wo", "sg", "su", "sd"))
+        w_q, w_k, w_v, w_o = (full[name] for name in ("wq", "wk", "wv", "wo"))
         e_gate, e_up, e_down = (full[name] for name in LATE)
         reach, key_start = shard_count - 1, 0
         key_segment, key_padding = segment_row, padding_row
@@ -591,10 +1033,9 @@
         mixed_rows = rows_in + dense_product(attended, w_o)
         normed_ffn = (mixed_rows * rms_scale(mixed_rows) * gain_second).astype(bfloat)
     scale_second = rms_scale(mixed_rows)
-    shared_pre = dense_product(normed_ffn, s_gate)
-    shared_lin = dense_product(normed_ffn, s_up)
-    shared_mid = (jax.nn.silu(shared_pre) * shared_lin).astype(bfloat)
-    shared_out = dense_product(shared_mid, s_down)
+    grad_low = cotangent[0]
+    grad_out = grad_low.astype(jnp.float32)
+    gate_probs = jax.nn.softmax(gate_logits[0], axis=-1)
     route_flat = routes[0].reshape(-1)
     route_total = tokens * TOP
     onehot = (route_flat[:, None] == jnp.arange(experts, dtype=jnp.int32)[None, :]).astype(
@@ -602,75 +1043,85 @@
     )
     slot_rank = jnp.sum((jnp.cumsum(onehot, axis=0) - onehot) * onehot, axis=1)
     places = route_flat * capacity + slot_rank
-    slot_table = (
-        jnp.full((experts * capacity,), route_total, dtype=jnp.int32)
-        .at[places]
-        .set(jnp.arange(route_total, dtype=jnp.int32))
-    )
-    padded_rows = jnp.concatenate([normed_ffn, jnp.zeros((1, model_width), bfloat)], axis=0)
-    send_rows = padded_rows[slot_table // TOP].reshape(experts, capacity, model_width)
-    received = lax.all_to_all(send_rows, "expert", split_axis=0, concat_axis=0, tiled=True)
-    gate_pre = jnp.einsum("sid,df->sif", received, e_gate, preferred_element_type=jnp.float32)
-    up_pre = jnp.einsum("sid,df->sif", received, e_up, preferred_element_type=jnp.float32)
-    middle = (jax.nn.silu(gate_pre) * up_pre).astype(bfloat)
-    result = jnp.einsum("sif,fd->sid", middle, e_down, preferred_element_type=jnp.float32).astype(bfloat)
-    returned = lax.all_to_all(result, "expert", split_axis=0, concat_axis=0, tiled=True)
+    if not fast:
+        shared_pre = dense_product(normed_ffn, s_gate)
+        shared_lin = dense_product(normed_ffn, s_up)
+        shared_mid = (jax.nn.silu(shared_pre) * shared_lin).astype(bfloat)
+        shared_out = dense_product(shared_mid, s_down)
+        grad_shared_mid = product_t(grad_low, s_down)
+        grad_shared_pre, grad_shared_lin = swiglu_back(grad_shared_mid, shared_pre, shared_lin)
+        shared_down_grad = dense_product(shared_mid.T, grad_low)
+        shared_gate_grad = dense_product(normed_ffn.T, grad_shared_pre)
+        shared_up_grad = dense_product(normed_ffn.T, grad_shared_lin)
+        ffn_grad_shared = product_t(grad_shared_pre, s_gate) + product_t(grad_shared_lin, s_up)
+        slot_table = (
+            jnp.full((experts * capacity,), route_total, dtype=jnp.int32)
+            .at[places]
+            .set(jnp.arange(route_total, dtype=jnp.int32))
+        )
+        padded_rows = jnp.concatenate([normed_ffn, jnp.zeros((1, model_width), bfloat)], axis=0)
+        send_rows = padded_rows[slot_table // TOP].reshape(experts, capacity, model_width)
+        received = lax.all_to_all(send_rows, "expert", split_axis=0, concat_axis=0, tiled=True)
+        route_grad = (
+            (gate_probs[:, :, None] * grad_out[:, None, :])
+            .astype(bfloat)
+            .reshape(route_total, model_width)
+        )
+        route_padded = jnp.concatenate([route_grad, jnp.zeros((1, model_width), bfloat)], axis=0)
+        send_grad = route_padded[slot_table].reshape(experts, capacity, model_width)
+        grad_received = lax.all_to_all(send_grad, "expert", split_axis=0, concat_axis=0, tiled=True)
+    if fast:
+        returned, grad_back, *sums = second_part(received, grad_received, (e_gate, e_up, e_down), shared_work)
+        expert_grads = tuple(grad[None].astype(jnp.float32) for grad in sums[:3])
+        shared_grads = tuple(grad[0].astype(jnp.float32) for grad in sums[3:])
+    else:
+        gate_pre = jnp.einsum("sid,df->sif", received, e_gate, preferred_element_type=jnp.float32)
+        up_pre = jnp.einsum("sid,df->sif", received, e_up, preferred_element_type=jnp.float32)
+        middle = (jax.nn.silu(gate_pre) * up_pre).astype(bfloat)
+        result = jnp.einsum("sif,fd->sid", middle, e_down, preferred_element_type=jnp.float32).astype(bfloat)
+        returned = lax.all_to_all(result, "expert", split_axis=0, concat_axis=0, tiled=True)
+        grad_middle = jnp.einsum(
+            "sid,fd->sif", grad_received, e_down, preferred_element_type=jnp.float32
+        )
+        grad_gate_pre, grad_up_pre = swiglu_back(grad_middle, gate_pre, up_pre)
+        expert_down_grad = jnp.einsum(
+            "sif,sid->fd", middle, grad_received, preferred_element_type=jnp.float32
+        )
+        expert_gate_grad = jnp.einsum(
+            "sid,sif->df", received, grad_gate_pre, preferred_element_type=jnp.float32
+        )
+        expert_up_grad = jnp.einsum(
+            "sid,sif->df", received, grad_up_pre, preferred_element_type=jnp.float32
+        )
+        grad_rows = (
+            jnp.einsum("sif,df->sid", grad_gate_pre, e_gate, preferred_element_type=jnp.float32)
+            + jnp.einsum("sif,df->sid", grad_up_pre, e_up, preferred_element_type=jnp.float32)
+        ).astype(bfloat)
+        grad_back = lax.all_to_all(grad_rows, "expert", split_axis=0, concat_axis=0, tiled=True)
+        expert_grads = tuple(
+            scatter_shards(grad.astype(bfloat))[None].astype(jnp.float32)
+            for grad in (expert_gate_grad, expert_up_grad, expert_down_grad)
+        )
+        shared_grads = (
+            sum_plane(scatter_shards(shared_gate_grad.astype(bfloat)), 1),
+            sum_plane(scatter_shards(shared_up_grad.astype(bfloat)), 1),
+            sum_plane(scatter_shards(shared_down_grad.astype(bfloat)), 0),
+        )
     per_route = (
         returned.reshape(experts * capacity, model_width)[places]
         .astype(jnp.float32)
         .reshape(tokens, TOP, model_width)
     )
-    gate_probs = jax.nn.softmax(gate_logits[0], axis=-1)
     routed = jnp.sum(gate_probs[:, :, None] * per_route, axis=1)
     output = (mixed_rows + shared_out + routed).astype(bfloat)
-    grad_low = cotangent[0]
-    grad_out = grad_low.astype(jnp.float32)
     contrib = jnp.sum(per_route * grad_out[:, None, :], axis=-1)
     logit_grad = gate_probs * (contrib - jnp.sum(gate_probs * contrib, axis=-1, keepdims=True))
-    route_grad = (
-        (gate_probs[:, :, None] * grad_out[:, None, :])
-        .astype(bfloat)
-        .reshape(route_total, model_width)
-    )
-    route_padded = jnp.concatenate([route_grad, jnp.zeros((1, model_width), bfloat)], axis=0)
-    send_grad = route_padded[slot_table].reshape(experts, capacity, model_width)
-    grad_received = lax.all_to_all(send_grad, "expert", split_axis=0, concat_axis=0, tiled=True)
-    grad_middle = jnp.einsum(
-        "sid,fd->sif", grad_received, e_down, preferred_element_type=jnp.float32
-    )
-    grad_gate_pre, grad_up_pre = swiglu_back(grad_middle, gate_pre, up_pre)
-    expert_down_grad = jnp.einsum(
-        "sif,sid->fd", middle, grad_received, preferred_element_type=jnp.float32
-    )
-    expert_gate_grad = jnp.einsum(
-        "sid,sif->df", received, grad_gate_pre, preferred_element_type=jnp.float32
-    )
-    expert_up_grad = jnp.einsum(
-        "sid,sif->df", received, grad_up_pre, preferred_element_type=jnp.float32
-    )
-    grad_rows = (
-        jnp.einsum("sif,df->sid", grad_gate_pre, e_gate, preferred_element_type=jnp.float32)
-        + jnp.einsum("sif,df->sid", grad_up_pre, e_up, preferred_element_type=jnp.float32)
-    ).astype(bfloat)
-    grad_back = lax.all_to_all(grad_rows, "expert", split_axis=0, concat_axis=0, tiled=True)
-    expert_grads = tuple(
-        scatter_shards(grad.astype(bfloat))[None].astype(jnp.float32)
-        for grad in (expert_gate_grad, expert_up_grad, expert_down_grad)
-    )
     grad_routes = (
         grad_back.reshape(experts * capacity, model_width)[places]
         .astype(jnp.float32)
         .reshape(tokens, TOP, model_width)
     )
-    grad_normed_ffn = jnp.sum(grad_routes, axis=1)
-    grad_shared_mid = product_t(grad_low, s_down)
-    grad_shared_pre, grad_shared_lin = swiglu_back(grad_shared_mid, shared_pre, shared_lin)
-    shared_down_grad = dense_product(shared_mid.T, grad_low)
-    shared_gate_grad = dense_product(normed_ffn.T, grad_shared_pre)
-    shared_up_grad = dense_product(normed_ffn.T, grad_shared_lin)
-    grad_normed_ffn = (
-        grad_normed_ffn + product_t(grad_shared_pre, s_gate) + product_t(grad_shared_lin, s_up)
-    )
+    grad_normed_ffn = jnp.sum(grad_routes, axis=1) + ffn_grad_shared
     gain_ffn_grad = jnp.sum(grad_normed_ffn * mixed_rows * scale_second, axis=0)
     scaled_second = grad_normed_ffn * gain_second
     grad_mixed = (
@@ -741,9 +1192,9 @@
         attn_total[1],
         attn_total[2],
         attn_total[3],
-        sum_plane(scatter_shards(shared_gate_grad.astype(bfloat)), 1),
-        sum_plane(scatter_shards(shared_up_grad.astype(bfloat)), 1),
-        sum_plane(scatter_shards(shared_down_grad.astype(bfloat)), 0),
+        shared_grads[0],
+        shared_grads[1],
+        shared_grads[2],
         expert_grads[0],
         expert_grads[1],
         expert_grads[2],

time: 583 us -> 533 us (0.914)
  Pallas kernels: 97.4 us -> 308 us
  waiting for transfers between devices: 136 us -> 55.8 us
  matrix products: 118 us -> 39.6 us
  starting transfers between devices: 63.5 us -> 10.9 us
  local copies, waits for them, and re-layouts: 67.8 us -> 42.4 us
  other arithmetic: 66.1 us -> 45.7 us
    pallas_call x1 -> x2, Pallas kernels: 97.4 us -> 308 us  [the longest x1 160 us: second_part(): pl.pallas_call(second_kernel, out_shape=[shape(rows.shape, bfloat)] * 2 +...]
    ppermute x42 -> x12, waiting for transfers between devices: 135 us -> 55.8 us  [swap(): lax.ppermute(value, axis, [(index, index ^ bit) for index in range(size)])]
    dot_general x9 -> x0, matrix products: 57.2 us -> none  [the longest x1 12.4 us: shards(): jnp.einsum('sid,df->sif', received, e_gate, preferred_element_type=jnp.fl...]
    ppermute x42 -> x12, starting transfers between devices: 42 us -> 10.9 us  [swap(): lax.ppermute(value, axis, [(index, index ^ bit) for index in range(size)])]
    all_to_all x4 -> x0, starting transfers between devices: 21.6 us -> none  [the longest x1 7.39 us: shards(): lax.all_to_all(send_grad, 'expert', split_axis=0, concat_axis=0, tiled=True)]
    convert_element_type x26 -> x8, other arithmetic: 21 us -> 6.18 us  [fold(): (keep.astype(jnp.float32) + swap(give.astype(jnp.bfloat16), axis, bit).as...]
    dot_general x7 -> x4, matrix products: 17.7 us -> 6.11 us  [product_t(): lax.dot_general(left, right, (((1,), (1,)), ((), ())), preferred_element_...]
    dynamic_slice x30 -> x9, local copies, waits for them, and re-layouts: 15 us -> 4.37 us  [halves(): give = lax.dynamic_slice_in_dim(value, (1 - bit_set) * half, half, dim)]
  transfers between devices with their start and end apart: 46 -> 12, of which waited for: 23 -> 6; matrix products, arithmetic and copies ran while one was open for 39% -> 5% of each run, Pallas kernels for 17% -> 0%
where the time goes in v3:
time: 533 us; the launch traced here: 526 us
  Pallas kernels  308 us (58%)
  waiting for transfers between devices  55.8 us (10%)
  other arithmetic  45.7 us (9%)
  local copies, waits for them, and re-layouts  42.4 us (8%)
  matrix products  39.6 us (7%)
  blocking collectives  22 us (4%)
  starting transfers between devices  10.9 us (2%)
    pallas_call x1, Pallas kernels, second_part(): pl.pallas_call(second_kernel, out_shape=[shape(rows.shape, bfloat)] * 2 +...  160 us
    pallas_call x1, Pallas kernels, first_part(): pl.pallas_call(first_kernel, out_shape=[whole[name] for name in KEPT] + [...  148 us
    ppermute x12, waiting for transfers between devices, swap(): lax.ppermute(value, axis, [(index, index ^ bit) for index in range(size)])  55.8 us
    psum x1, blocking collectives, shards(): lax.psum(scatter_shards(gain_rows), 'expert').astype(jnp.float32)  22 us
    dot_general x1, matrix products, shards(): jnp.einsum('qhd,khd->hqk', grad_attended, values_all, preferred_element_t...  11.5 us
    ppermute x12, starting transfers between devices, swap(): lax.ppermute(value, axis, [(index, index ^ bit) for index in range(size)])  10.9 us
    unnamed x107, local copies, waits for them, and re-layouts  10.9 us
  transfers between devices with their start and end apart: 12, of which 6 were waited for; matrix products, arithmetic and copies ran while one was open for 5% of the time, Pallas kernels for 0%

profile of v3, /device:TPU:0, one launch (start us, length us, event | category | flops | bytes accessed | tf_op | source)
XLA Modules:
  0.0 525.9 jit_solution(15342732746351044630)
XLA Ops:
  13.7 148.3 %shard_map.310 = (bf16[768,768]{1,0:T(8,128)(2,1)}, bf16[768,768]{1,0:T(8,128)(2,1)}, bf16[768,768]{1,0:T(8,128)(2,1)}, bf16[768,768]{1,0:T(8,128)(2,1)}, bf16[7...) custom-call(bf16[256,768]{1,0:T(8,128)(2,1)} %bitcast.160, ...), custom_call_target="tpu_custom_call" | custom-call | flops 15000000512 | bytes 47000000 | tf_op jit(solution)/shard_map/pallas_call | solution.py:491
  162.1 159.6 %shard_map.311 = (bf16[8,128,768]{2,1,0:T(8,128)(2,1)}, bf16[8,128,768]{2,1,0:T(8,128)(2,1)}, bf16[192,2048]{1,0:T(8,128)(2,1)}, bf16[192,2048]{1,0:T(8,128)(2,1...) custom-call(bf16[8,128,768]{2,1,0:T(8,128)(2,1)} %get-tuple-element., ...), custom_call_target="tpu_custom_call" | custom-call | flops 28999999488 | bytes 30000000 | tf_op jit(solution)/shard_map/pallas_call | solution.py:838
  321.7 4.0 gather_fusion
  328.4 2.7 gather_fusion.1
  331.2 2.2 reshape.518
  336.9 2.1 multiply_reduce_fusion.3
  339.0 3.6 multiply_reduce_fusion.1
  351.0 6.3 %fusion.56 = f32[12,256,1024]{2,1,0:T(8,128)} fusion(bf16[256,12,64]{0,2,1:T(8,128)(2,1)S(1)} %bitcast.154, bf16[1024,12,64]{0,2,1:T(8,128)(2,1)S(1)} %bitcast.151), kind=kOutput, calls=%fused_computation.146 | convolution fusion | flops 402653184 | bytes 14548992 | tf_op jit(solution)/shard_map/qhd,khd->hqk/dot_general | solution.py:1012
  360.7 11.5 %multiply_reduce_fusion = (f32[12,256]{1,0:T(8,128)S(1)}, f32[12,256,1024]{2,1,0:T(8,128)}) fusion(f32[12,256,1024]{2,1,0:T(8,128)} %fusion.56, f32[12,256]{1,0:T(8,128)S(1)} %reduce.8, pred[256,1024]{1,0:T(8,128)(4,1)S(1)} %fusion.19, bf16[256,12,64]{0,2,1:T(8,128)(2,1)} %bitcast.167, bf16[1024,12,64]{0,2,1:T(8,128)(2,1)S(1)} %bitcast.153), kind=kOutput, calls=%fused_computation.3 | convolution fusion | flops 418378752 | bytes 27418624 | tf_op jit(solution)/shard_map/qhd,khd->hqk/dot_general | solution.py:1138
  373.4 6.7 %multiply_convert_fusion = bf16[12,256,1024]{2,1,0:T(8,128)(2,1)S(1)} fusion(f32[12,256,1024]{2,1,0:T(8,128)} %get-tuple-element.150, f32[12,256,1024]{2,1,0:T(8,128)S(1)} %bitcast.146, f32[12,256]{1,0:T(8,128)S(1)} %get-tuple-element.149, f32[12,256]{1,0:T(8,128)S(1)} %reduce.8, pred[256,1024]{1,0:T(8,128)(4,1)S(1)} %fusion.19), kind=kLoop, calls=%fused_computation.2 | loop fusion | flops 18874368 | bytes 31744000 | tf_op jit(solution)/shard_map/convert_element_type | solution.py:1142
  380.1 2.9 fusion.12
  384.3 4.6 fusion.5
  393.3 2.4 fusion.8
  395.8 2.4 fusion.9
  412.7 2.7 fusion.57
  419.4 2.2 add_convert_fusion
  426.6 23.6 %collective-permute-done.5 = bf16[1,192,4,768]{3,1,2,0:T(8,128)(2,1)S(1)} collective-permute-done((bf16[1,192,4,768]{3,1,2,0:T(8,128)(2,1)S(1)}, bf16[1,192,4,768]{3,1,2,0:T(8,128)(2,1)S(1)}, u32[]{:S(2)}, u32[]{:S(2)}) %collective-permute-start.5) | collective-permute-done | bytes 1179680 | tf_op jit(solution)/shard_map/ppermute | solution.py:867
  455.9 10.6 %collective-permute-done.6 = bf16[384,768]{1,0:T(8,128)(2,1)} collective-permute-done((bf16[384,768]{1,0:T(8,128)(2,1)}, bf16[384,768]{1,0:T(8,128)(2,1)}, u32[]{:S(2)}, u32[]{:S(2)}) %collective-permute-start.6) | collective-permute-done | bytes 589856 | tf_op jit(solution)/shard_map/ppermute | solution.py:867
  470.8 4.7 collective-permute-done.7
  476.6 3.5 collective-permute-start.8
  480.2 4.9 collective-permute-done.8
  486.4 6.3 %collective-permute-done.9 = bf16[96,768]{1,0:T(8,128)(2,1)S(1)} collective-permute-done((bf16[96,768]{1,0:T(8,128)(2,1)S(1)}, bf16[96,768]{1,0:T(8,128)(2,1)S(1)}, u32[]{:S(2)}, u32[]{:S(2)}) %collective-permute-start.9) | collective-permute-done | bytes 147488 | tf_op jit(solution)/shard_map/ppermute | solution.py:867
  494.0 5.5 %collective-permute-done.10 = bf16[192,768]{1,0:T(8,128)(2,1)S(1)} collective-permute-done((bf16[192,768]{1,0:T(8,128)(2,1)S(1)}, bf16[192,768]{1,0:T(8,128)(2,1)S(1)}, u32[]{:S(2)}, u32[]{:S(2)}) %collective-permute-start.10) | collective-permute-done | bytes 294944 | tf_op jit(solution)/shard_map/ppermute | solution.py:867
  501.5 22.0 %psum.7 = bf16[192,2]{0,1:T(2,128)(2,1)S(1)} all-reduce(bf16[192,2]{0,1:T(2,128)(2,1)S(1)} %bitcast.176), channel_id=1, replica_groups=mesh['expert'=8,'shard'=4] {'expert'}, use_global_device_ids=true, to_apply=%region_16.17 | all-reduce | flops 384 | bytes 1536 | tf_op jit(solution)/shard_map/psum | solution.py:1181
  (218 shorter events, 78.6 us)
Async XLA Ops:
  0.6 11.6 %copy-start.18 = (bf16[1,256,768]{2,1,0:T(8,128)(2,1)S(1)}, bf16[1,256,768]{2,1,0:T(8,128)(2,1)}, u32[]{:S(2)}) copy-start(bf16[1,256,768]{2,1,0:T(8,128)(2,1)} %param.37) | copy-start | bytes 1179652
  0.7 12.5 %copy-start.42 = (s32[1,1024]{1,0:T(1,128)S(1)}, s32[1,1024]{1,0:T(1,128)}, u32[]{:S(2)}) copy-start(s32[1,1024]{1,0:T(1,128)} %refs_14_.1) | copy-start | bytes 12292
  360.7 11.5 %slice-start = ((s8[12582912]{0:T(1024)(128)(4,1)}), s8[4194304]{0:T(1024)(128)(4,1)S(1)}, s32[]{:S(2)}) async-start(s8[12582912]{0:T(1024)(128)(4,1)} %bitcast.145), calls=%async_computation | async-start | bytes 8388608
  360.7 11.5 %slice-start.1 = ((s8[12582912]{0:T(1024)(128)(4,1)}), s8[4194304]{0:T(1024)(128)(4,1)S(1)}, s32[]{:S(2)}) async-start(s8[12582912]{0:T(1024)(128)(4,1)} %bitcast.145), calls=%async_computation.1 | async-start | bytes 8388608
  360.7 12.7 %slice-start.2 = ((s8[12582912]{0:T(1024)(128)(4,1)}), s8[4194304]{0:T(1024)(128)(4,1)S(1)}, s32[]{:S(2)}) async-start(s8[12582912]{0:T(1024)(128)(4,1)} %bitcast.145), calls=%async_computation.2 | async-start | bytes 8388608
  384.3 4.7 copy-start.41
  384.3 4.7 copy-start.43
  404.7 14.7 %collective-permute-start.4 = (bf16[2,1,192,4,768]{4,2,1,0,3:T(8,128)(2,1)}, bf16[2,1,192,4,768]{4,2,1,0,3:T(8,128)(2,1)S(1)}, u32[]{:S(2)}, u32[]{:S(2)}) collective-permute-start(bf16[2,1,192,4,768]{4,2,1,0,3:T(8,128)(2,1)} %constant_dynamic-slice_fusion.3), channel_id=1, source_target_pairs={{0,1},{1,0},{2,3},{3,2},{4,5},{5,4},{6,7},{7,6},{8,9},{9,8},{10,11... | collective-permute-start | bytes 7077896 | tf_op jit(solution)/shard_map/ppermute | solution.py:867
  410.6 41.4 %collective-permute-start = (bf16[2,1,256,768]{3,2,1,0:T(8,128)(2,1)}, bf16[2,1,256,768]{3,2,1,0:T(8,128)(2,1)}, u32[]{:S(2)}, u32[]{:S(2)}) collective-permute-start(bf16[2,1,256,768]{3,2,1,0:T(8,128)(2,1)} %constant_dynamic-slice_fusion.8), channel_id=1, source_target_pairs={{0,1},{1,0},{2,3},{3,2},{4,5},{5,4},{6,7},{7,6},{8,9},{9,8},{10,11... | collective-permute-start | bytes 2359304 | tf_op jit(solution)/shard_map/ppermute | solution.py:867
  411.5 3.9 copy-start.29
  421.7 28.4 %collective-permute-start.5 = (bf16[1,192,4,768]{3,1,2,0:T(8,128)(2,1)S(1)}, bf16[1,192,4,768]{3,1,2,0:T(8,128)(2,1)S(1)}, u32[]{:S(2)}, u32[]{:S(2)}) collective-permute-start(bf16[1,192,4,768]{3,1,2,0:T(8,128)(2,1)S(1)} %dynamic-slice_bitcast_fusion), channel_id=1, source_target_pairs={{0,2},{1,3},{2,0},{3,1},{4,6},{5,7},{6,4},{7,5},{8,10},{9,11},{10,... | collective-permute-start | bytes 3538952 | tf_op jit(solution)/shard_map/ppermute | solution.py:867
  426.6 25.4 %copy-start.14 = (bf16[1024,768]{1,0:T(8,128)(2,1)S(1)}, bf16[1024,768]{1,0:T(8,128)(2,1)}, u32[]{:S(2)}) copy-start(bf16[1024,768]{1,0:T(8,128)(2,1)} %copy-done.13) | copy-start | bytes 4718596
  451.3 3.8 copy-start.40
  451.3 15.2 %collective-permute-start.6 = (bf16[384,768]{1,0:T(8,128)(2,1)}, bf16[384,768]{1,0:T(8,128)(2,1)}, u32[]{:S(2)}, u32[]{:S(2)}) collective-permute-start(bf16[384,768]{1,0:T(8,128)(2,1)} %constant_dynamic-slice_fusion.2), channel_id=1, source_target_pairs={{0,4},{4,0},{8,12},{12,8},{16,20},{20,16},{24,28},{28,24},{1,5},{5... | collective-permute-start | bytes 1769480 | tf_op jit(solution)/shard_map/ppermute | solution.py:867
  453.3 16.0 %copy-start.33 = (f32[768]{0:T(1024)S(1)}, f32[768]{0:T(1024)}, u32[]{:S(2)}) copy-start(f32[768]{0:T(1024)} %get-tuple-element.126) | copy-start | bytes 9220
  454.1 15.2 %collective-permute-start.1 = (bf16[1,256,768]{2,1,0:T(8,128)(2,1)}, bf16[1,256,768]{2,1,0:T(8,128)(2,1)}, u32[]{:S(2)}, u32[]{:S(2)}) collective-permute-start(bf16[1,256,768]{2,1,0:T(8,128)(2,1)} %dynamic-slice_bitcast_fusion.1), channel_id=1, source_target_pairs={{0,2},{1,3},{2,0},{3,1},{4,6},{5,7},{6,4},{7,5},{8,10},{9,11},{10,... | collective-permute-start | bytes 1179656 | tf_op jit(solution)/shard_map/ppermute | solution.py:867
  455.9 13.5 %copy-start.9 = (f32[256,768]{1,0:T(8,128)S(1)}, f32[256,768]{1,0:T(8,128)}, u32[]{:S(2)}) copy-start(f32[256,768]{1,0:T(8,128)} %fusion.57) | copy-start | bytes 2359300
  467.8 7.8 %collective-permute-start.7 = (bf16[192,768]{1,0:T(8,128)(2,1)S(1)}, bf16[192,768]{1,0:T(8,128)(2,1)S(1)}, u32[]{:S(2)}, u32[]{:S(2)}) collective-permute-start(bf16[192,768]{1,0:T(8,128)(2,1)S(1)} %constant_dynamic-slice_fusion.1), channel_id=1, source_target_pairs={{0,8},{4,12},{8,0},{12,4},{16,24},{20,28},{24,16},{28,20},{1,9},{5... | collective-permute-start | bytes 884744 | tf_op jit(solution)/shard_map/ppermute | solution.py:867
  476.6 8.5 %collective-permute-start.8 = (bf16[96,768]{1,0:T(8,128)(2,1)S(1)}, bf16[96,768]{1,0:T(8,128)(2,1)S(1)}, u32[]{:S(2)}, u32[]{:S(2)}) collective-permute-start(bf16[96,768]{1,0:T(8,128)(2,1)S(1)} %constant_dynamic-slice_fusion), channel_id=1, source_target_pairs={{0,16},{4,20},{8,24},{12,28},{16,0},{20,4},{24,8},{28,12},{1,17},{... | collective-permute-start | bytes 442376 | tf_op jit(solution)/shard_map/ppermute | solution.py:867
  480.1 12.7 %collective-permute-start.2 = (bf16[2,1,192,2]{2,1,0,3:T(2,128)(2,1)S(1)}, bf16[2,1,192,2]{2,1,0,3:T(2,128)(2,1)S(1)}, u32[]{:S(2)}, u32[]{:S(2)}) collective-permute-start(bf16[2,1,192,2]{2,1,0,3:T(2,128)(2,1)S(1)} %constant_dynamic-slice_fusion.6), channel_id=1, source_target_pairs={{0,1},{1,0},{2,3},{3,2},{4,5},{5,4},{6,7},{7,6},{8,9},{9,8},{10,11... | collective-permute-start | bytes 4616 | tf_op jit(solution)/shard_map/ppermute | solution.py:867
  485.2 7.5 %collective-permute-start.9 = (bf16[96,768]{1,0:T(8,128)(2,1)S(1)}, bf16[96,768]{1,0:T(8,128)(2,1)S(1)}, u32[]{:S(2)}, u32[]{:S(2)}) collective-permute-start(bf16[96,768]{1,0:T(8,128)(2,1)S(1)} %add_convert_fusion.8), channel_id=1, source_target_pairs={{0,16},{4,20},{8,24},{12,28},{16,0},{20,4},{24,8},{28,12},{1,17},{... | collective-permute-start | bytes 442376 | tf_op jit(solution)/shard_map/ppermute | solution.py:867
  492.8 6.8 %collective-permute-start.10 = (bf16[192,768]{1,0:T(8,128)(2,1)S(1)}, bf16[192,768]{1,0:T(8,128)(2,1)S(1)}, u32[]{:S(2)}, u32[]{:S(2)}) collective-permute-start(bf16[192,768]{1,0:T(8,128)(2,1)S(1)} %maximum_select_fusion.2), channel_id=1, source_target_pairs={{0,8},{4,12},{8,0},{12,4},{16,24},{20,28},{24,16},{28,20},{1,9},{5... | collective-permute-start | bytes 884744 | tf_op jit(solution)/shard_map/ppermute | solution.py:867
  492.9 8.5 %collective-permute-start.3 = (bf16[1,192,2]{1,0,2:T(2,128)(2,1)S(1)}, bf16[1,192,2]{1,0,2:T(2,128)(2,1)S(1)}, u32[]{:S(2)}, u32[]{:S(2)}) collective-permute-start(bf16[1,192,2]{1,0,2:T(2,128)(2,1)S(1)} %fusion.50), channel_id=1, source_target_pairs={{0,2},{1,3},{2,0},{3,1},{4,6},{5,7},{6,4},{7,5},{8,10},{9,11},{10,... | collective-permute-start | bytes 2312 | tf_op jit(solution)/shard_map/ppermute | solution.py:867
  499.7 24.3 %collective-permute-start.11 = (bf16[384,768]{1,0:T(8,128)(2,1)S(1)}, bf16[384,768]{1,0:T(8,128)(2,1)S(1)}, u32[]{:S(2)}, u32[]{:S(2)}) collective-permute-start(bf16[384,768]{1,0:T(8,128)(2,1)S(1)} %maximum_select_fusion.1), channel_id=1, source_target_pairs={{0,4},{4,0},{8,12},{12,8},{16,20},{20,16},{24,28},{28,24},{1,5},{5... | collective-permute-start | bytes 1769480 | tf_op jit(solution)/shard_map/ppermute | solution.py:867
  (39 other events, 79.9 us)

commit v4 on v3

--- a/solution.py
+++ b/solution.py
@@ -1,4 +1,5 @@
 import functools
+import math
 
 import jax
 import jax.numpy as jnp
@@ -544,7 +545,7 @@
 
 def add_into(target, first, second):
     rows = first.shape[-2]
-    strip = 64
+    strip = math.gcd(rows, 64)
 
     def body(index, carry):
         at = pl.ds(pl.multiple_of(index * strip, strip), strip)
@@ -557,85 +558,84 @@
 
 
 class PlaneSum:
-    def __init__(self, work, out, receive, send_sem, recv_sem, bits, peers, order, by_rows):
+    def __init__(self, work, out, receive, send_sem, recv_sem, bits, peers, order):
         self.work, self.out, self.receive = work, out, receive
         self.send_sem, self.recv_sem, self.bits, self.peers, self.order = send_sem, recv_sem, bits, peers, order
-        self.by_rows = by_rows
-        self.whole_y = True
-        self.size = work.shape[1 if by_rows else 2]
-        self.offset = 0
+        self.at = [(0, 2), (0, work.shape[1]), (0, work.shape[2])]
         self.trail = []
 
-    def region(self, ref, offset, size, y=None):
-        lead = pl.ds(0, ref.shape[0]) if y is None else pl.ds(y, 1)
-        unit = 16 if self.by_rows else 128
-        at = pl.ds(offset if isinstance(offset, int) else pl.multiple_of(offset, unit), size)
-        return ref.at[lead, at, :] if self.by_rows else ref.at[lead, :, at]
-
-    def halves(self, axis):
-        bit = self.bits[axis]
-        if axis == "y":
-            return (self.offset, self.size, bit), (self.offset, self.size, 1 - bit)
-        half = self.size // 2
-        y = None if self.whole_y else self.bits["y"]
-        return (self.offset + bit * half, half, y), (self.offset + (1 - bit) * half, half, y)
+    def region(self, ref, at):
+        starts = [pl.multiple_of(start, unit) if unit > 1 and not isinstance(start, int) else start for (start, _), unit in zip(at, (1, 16, 128))]
+        first = pl.ds(0, 1) if ref.shape[0] == 1 else pl.ds(starts[0], at[0][1])
+        return ref.at[first, pl.ds(starts[1], at[1][1]), pl.ds(starts[2], at[2][1])]
+
+    def halves(self, step):
+        axis, dim = self.order[step]
+        bit, half = self.bits[axis], self.at[dim][1] // 2
+        keep, give = list(self.at), list(self.at)
+        keep[dim] = (self.at[dim][0] + bit * half, half)
+        give[dim] = (self.at[dim][0] + (1 - bit) * half, half)
+        return keep, give
 
     def start(self, step):
-        axis = self.order[step]
-        _, give = self.halves(axis)
-        send(
-            self.region(self.work, *give),
-            self.receive[step],
-            self.send_sem.at[step],
-            self.recv_sem.at[step],
-            self.peers[axis],
-        )
+        _, give = self.halves(step)
+        peer = self.peers[self.order[step][0]]
+        send(self.region(self.work, give), self.receive[step], self.send_sem.at[step], self.recv_sem.at[step], peer)
 
     def finish(self, step):
-        axis = self.order[step]
-        keep, give = self.halves(axis)
+        keep, give = self.halves(step)
         wait_for(self.receive[step], self.recv_sem.at[step])
-        last = step == len(self.order) - 1
-        kept = self.region(self.work, *keep)
-        target = self.region(self.out, keep[0], keep[1]) if last else kept
+        kept = self.region(self.work, keep)
+        target = self.region(self.out, keep) if step == len(self.order) - 1 else kept
         add_into(target, kept, self.receive[step])
-        wait_for(self.region(self.work, *give), self.send_sem.at[step])
-        if axis == "y":
-            self.whole_y = False
-        else:
-            self.trail.append((axis, self.offset, self.size))
-            self.offset, self.size = keep[0], keep[1]
+        wait_for(self.region(self.work, give), self.send_sem.at[step])
+        if self.order[step][0] != "y":
+            self.trail.append((step, self.at))
+        self.at = keep
 
     def back_start(self, step):
-        axis, _, _ = self.trail[-1 - step]
-        part = self.region(self.out, self.offset, self.size)
+        forth, _ = self.trail[-1 - step]
+        part, at = self.region(self.out, self.at), len(self.order) + step
+        send(part, part, self.send_sem.at[at], self.recv_sem.at[at], self.peers[self.order[forth][0]])
+
+    def back_finish(self, step):
+        forth, whole = self.trail[-1 - step]
         at = len(self.order) + step
-        send(part, part, self.send_sem.at[at], self.recv_sem.at[at], self.peers[axis])
-
-    def back_finish(self, step):
-        axis, offset, size = self.trail[-1 - step]
-        at = len(self.order) + step
-        half = size // 2
-        wait_for(self.region(self.out, self.offset, self.size), self.send_sem.at[at])
-        wait_for(self.region(self.out, offset + (1 - self.bits[axis]) * half, half), self.recv_sem.at[at])
-        self.offset, self.size = offset, size
-
-
-def receive_shapes(shape, order, by_rows):
-    lead, rows, columns = shape
-    result = []
-    for axis in order:
-        if axis == "y":
-            lead = 1
-        elif by_rows:
-            rows //= 2
-        else:
-            columns //= 2
-        result.append((lead, rows, columns))
+        wait_for(self.region(self.out, self.at), self.send_sem.at[at])
+        dim = self.order[forth][1]
+        start, size = self.at[dim]
+        other = list(self.at)
+        other[dim] = (2 * whole[dim][0] + size - start, size)
+        wait_for(self.region(self.out, other), self.recv_sem.at[at])
+        self.at = list(self.at)
+        self.at[dim] = whole[dim]
+
+
+def receive_shapes(shape, order):
+    result, shape = [], list(shape)
+    for _, dim in order:
+        shape[dim] //= 2
+        result.append(tuple(shape))
     return result
 
 
-SHARED_ORDER = (("y", "x", "z1", "z2"), ("x", "z1", "y", "z2"), ("z1", "y", "x", "z2"))
+def ordered(axes, dims):
+    return tuple((axis, 0 if axis == "y" else dims[axis]) for axis in axes)
+
+
+BY_COLUMNS, BY_ROWS = dict(x=2, z1=2, z2=2), dict(x=1, z1=1, z2=1)
+BY_BOTH = dict(x=2, z1=1, z2=1)
+SHARED_ORDER = (
+    ordered(("y", "x", "z1", "z2"), BY_COLUMNS),
+    ordered(("x", "z1", "y", "z2"), BY_COLUMNS),
+    ordered(("z1", "y", "x", "z2"), BY_ROWS),
+)
+ATTENTION_ORDER = (
+    ordered(("y", "x", "z1", "z2"), BY_BOTH),
+    ordered(("x", "z1", "y", "z2"), BY_BOTH),
+    ordered(("z1", "y", "x", "z2"), BY_BOTH),
+    ordered(("y", "x", "z1", "z2"), BY_BOTH),
+)
 
 
 def plane_places():
@@ -685,7 +685,6 @@
             bits,
             peers,
             SHARED_ORDER[index],
-            index == 2,
         )
         for index in range(3)
     ]
@@ -852,7 +851,7 @@
         + [
             pltpu.VMEM(one, bfloat)
             for index in range(3)
-            for one in receive_shapes(shared[index].shape, SHARED_ORDER[index], index == 2)
+            for one in receive_shapes(shared[index].shape, SHARED_ORDER[index])
         ]
         + [dma((3,)), dma((3,))]
         + [dma((8,))] * 4
@@ -860,6 +859,274 @@
         compiler_params=pltpu.CompilerParams(collective_id=1, has_side_effects=True, vmem_limit_bytes=62 << 20),
         cost_estimate=pl.CostEstimate(flops=29000000000, bytes_accessed=30000000, transcendentals=2000000),
     )(rows, grads, *weights, *shared)
+
+
+def third_kernel(*refs):
+    rows_back, grads_back, mixed_ref, shared_ref, ffn_grad_ref, cot_ref, hidden_ref, logit_ref, route_ref, gain_ref = refs[:10]
+    normed_ref, query_ref, key_ref, value_ref, lse_ref, attended_ref = refs[10:16]
+    segment_row, segment_col, padding_row, cosine_ref, sine_ref = refs[16:21]
+    wq_ref, wk_ref, wv_ref, wo_ref = refs[21:25]
+    output_ref, input_grad_ref, logit_grad_ref, gain_out = refs[25:29]
+    sums_out = refs[29:33]
+    query_grad, key_grad, value_grad, context_grad, attended_grad, mixed_grad_ref = refs[33:39]
+    weight_grads = refs[39:43]
+    weight_work = refs[43:47]
+    context_core, context_y = refs[47:49]
+    receive = [refs[49 + 4 * index : 53 + 4 * index] for index in range(4)]
+    gain_parts, gain_recv = refs[65:67]
+    core_send, core_recv, sum_send, sum_recv, ctx_send, ctx_recv, gain_send, gain_got = refs[67:]
+    expert, shard, zed, core, bits, peers = plane_places()
+    why = bits["y"]
+    enter(tuple(peers[axis] for axis in ("core", "y", "x", "z1", "z2")))
+    tokens, width = hidden_ref.shape
+    here = pl.ds(pl.multiple_of(shard * tokens, tokens), tokens)
+    single, bfloat = jnp.float32, jnp.bfloat16
+
+    experts, capacity = rows_back.shape[0], rows_back.shape[1]
+    slots = experts * capacity
+    expert_at = lax.broadcasted_iota(jnp.int32, (tokens, 128), 1)
+    choices = [route_ref[:, k : k + 1] for k in range(TOP)]
+    named = ((choices[0] == expert_at) | (choices[1] == expert_at)).astype(bfloat)
+    before = lax.broadcasted_iota(jnp.int32, (tokens, tokens), 1) < lax.broadcasted_iota(jnp.int32, (tokens, tokens), 0)
+    rank = dense_product(before.astype(bfloat), named)
+    slot_at = lax.broadcasted_iota(jnp.int32, (tokens, slots), 1)
+
+    def slot_column(k):
+        slot = rank + expert_at.astype(single) * float(capacity)
+        return jnp.sum(jnp.where(choices[k] == expert_at, slot, 0.0), axis=1, keepdims=True).astype(jnp.int32)
+
+    picks = [slot_at == slot_column(k) for k in range(TOP)]
+    gate_probs = gate_columns(logit_ref[...])
+    grad_out = cot_ref[...].astype(single)
+    results = rows_back[...].reshape(slots, width)
+    per_route = [dense_product(pick.astype(bfloat), results) for pick in picks]
+    mixed = mixed_ref[...]
+    routed = gate_probs[0] * per_route[0] + gate_probs[1] * per_route[1]
+    output_ref[...] = (mixed + shared_ref[...] + routed).astype(bfloat)
+    contrib = [jnp.sum(rows * grad_out, axis=1, keepdims=True) for rows in per_route]
+    mean_contrib = gate_probs[0] * contrib[0] + gate_probs[1] * contrib[1]
+    logit_grad = [gate * (value - mean_contrib) for gate, value in zip(gate_probs, contrib)]
+    choice_at = lax.broadcasted_iota(jnp.int32, logit_grad_ref.shape, 1)
+    logit_grad_ref[...] = jnp.where(choice_at == 0, logit_grad[0], logit_grad[1])
+
+    ffn_grad = ffn_grad_ref[...] + dense_product((picks[0] | picks[1]).astype(bfloat), grads_back[...].reshape(slots, width))
+    scale_second = rms_scale(mixed)
+    gain_parts[0] = jnp.zeros_like(gain_parts[0])
+    gain_parts[0, 1:2, :] = jnp.sum(ffn_grad * mixed * scale_second, axis=0, keepdims=True)
+    scaled = ffn_grad * gain_ref[1:2, :]
+    mixed_grad = (
+        grad_out
+        + scale_second * scaled
+        - mixed * (scale_second * scale_second * scale_second) * jnp.mean(scaled * mixed, axis=-1, keepdims=True)
+    )
+    mixed_grad_ref[...] = mixed_grad
+    mixed_low = mixed_grad.astype(bfloat)
+    attended_grad[...] = product_t(mixed_low, wo_ref[...]).astype(bfloat)
+
+    def shard_rows(ref, y_of, core_of):
+        rows = ref.shape[0] // 4
+        return ref.at[pl.ds((y_of * 2 + core_of) * rows, rows)]
+
+    def core_start(index):
+        for y_of in range(2):
+            send(
+                shard_rows(weight_grads[index], y_of, 1 - core),
+                weight_work[index].at[y_of],
+                core_send.at[index, y_of],
+                core_recv.at[index, y_of],
+                peers["core"],
+            )
+
+    def core_finish(index):
+        for y_of in range(2):
+            wait_for(weight_work[index].at[y_of], core_recv.at[index, y_of])
+            wait_for(shard_rows(weight_grads[index], y_of, 1 - core), core_send.at[index, y_of])
+            add_rows(weight_work[index].at[y_of], shard_rows(weight_grads[index], y_of, core), weight_work[index].at[y_of])
+
+    sums = [
+        PlaneSum(
+            weight_work[index],
+            sums_out[index],
+            receive[index],
+            sum_send.at[index],
+            sum_recv.at[index],
+            bits,
+            peers,
+            ATTENTION_ORDER[index],
+        )
+        for index in range(4)
+    ]
+    weight_grads[3][...] = t_product(attended_ref[...], mixed_low).astype(bfloat)
+    core_start(3)
+
+    def head_pair(pair, carry):
+        lanes = pl.ds(pl.multiple_of(pair * 128, 128), 128)
+        query, keys, values, grads = query_ref[:, lanes], key_ref[:, lanes], value_ref[:, lanes], attended_grad[:, lanes]
+        allowed = allowed_mask(shard * tokens, 0, segment_col[here, :], segment_row[...], padding_row[...])
+        lane = lax.broadcasted_iota(jnp.int32, query.shape, 1)
+        from_keys = []
+        key_total = value_total = None
+        for half in range(2):
+            chosen = (lane >= 64) if half else (lane < 64)
+            one_query = jnp.where(chosen, query, jnp.zeros_like(query))
+            one_grad = jnp.where(chosen, grads, jnp.zeros_like(grads))
+            scores = jnp.where(allowed, product_t(one_query, keys) * 0.125, neg_fill)
+            probs = jnp.exp(scores - lse_ref[2 * pair + half])
+            probs_grad = product_t(one_grad, values)
+            delta = jnp.sum(probs * probs_grad, axis=1, keepdims=True)
+            scores_grad = (probs * (probs_grad - delta)).astype(bfloat)
+            from_keys.append(dense_product(scores_grad, keys))
+            key_part = t_product(scores_grad, one_query)
+            value_part = t_product(probs.astype(bfloat), one_grad)
+            key_total = key_part if key_total is None else key_total + key_part
+            value_total = value_part if value_total is None else value_total + value_part
+        back = jnp.where(lane < 64, from_keys[0], from_keys[1]) * 0.125
+        query_grad[:, lanes] = rotate_pair(back, cosine_ref[here, :], -sine_ref[here, :]).astype(bfloat)
+        key_grad[:, lanes] = rotate_pair(key_total * 0.125, cosine_ref[...], -sine_ref[...]).astype(bfloat)
+        value_grad[:, lanes] = value_total.astype(bfloat)
+        return carry
+
+    lax.fori_loop(0, 3, head_pair, 0)
+    core_finish(3)
+    sums[3].start(0)
+    lax.fori_loop(3, 6, head_pair, 0)
+
+    weight_grads[1][...] = t_product(normed_ref[...], key_grad[...]).astype(bfloat)
+    core_start(1)
+    weight_grads[2][...] = t_product(normed_ref[...], value_grad[...]).astype(bfloat)
+    core_start(2)
+    core_finish(1)
+    sums[1].start(0)
+    weight_grads[0][...] = t_product(normed_ref[here, :], query_grad[...]).astype(bfloat)
+    core_start(0)
+    core_finish(2)
+    sums[2].start(0)
+
+    def context_block(block, carry):
+        rows = pl.ds(pl.multiple_of(block * tokens, tokens), tokens)
+        total = product_t(key_grad[rows, :], wk_ref[...]) + product_t(value_grad[rows, :], wv_ref[...])
+        context_grad[rows, :] = total.astype(bfloat)
+        return carry
+
+    lax.fori_loop(0, 4, context_block, 0)
+    for y_of in range(2):
+        send(
+            shard_rows(context_grad, y_of, 1 - core),
+            context_core.at[y_of],
+            ctx_send.at[y_of],
+            ctx_recv.at[y_of],
+            peers["core"],
+        )
+    core_finish(0)
+    sums[0].start(0)
+    for y_of in range(2):
+        wait_for(context_core.at[y_of], ctx_recv.at[y_of])
+        wait_for(shard_rows(context_grad, y_of, 1 - core), ctx_send.at[y_of])
+        add_rows(context_core.at[y_of], shard_rows(context_grad, y_of, core), context_core.at[y_of])
+    send(context_core.at[1 - why], context_y, ctx_send.at[2], ctx_recv.at[2], peers["y"])
+    normed_grad = product_t(query_grad[...], wq_ref[...])
+
+    def step_all(step):
+        for one in (sums[3], sums[1], sums[2], sums[0]):
+            one.finish(step)
+            if step < 3:
+                one.start(step + 1)
+            else:
+                one.back_start(0)
+
+    step_all(0)
+    wait_for(context_y, ctx_recv.at[2])
+    wait_for(context_core.at[1 - why], ctx_send.at[2])
+    normed_grad = normed_grad + context_core[pl.ds(why, 1)].reshape(tokens, width).astype(single) + context_y[...].astype(single)
+    rows_in = hidden_ref[...].astype(single)
+    scale_first = rms_scale(rows_in)
+    gain_parts[0, 0:1, :] = jnp.sum(normed_grad * rows_in * scale_first, axis=0, keepdims=True)
+
+    def gain_start(step):
+        peer = peers[("core", "y", "x", "z1", "z2")[step]]
+        send(gain_parts.at[step], gain_recv.at[step], gain_send.at[step], gain_got.at[step], peer)
+
+    def gain_finish(step):
+        wait_for(gain_recv.at[step], gain_got.at[step])
+        gain_parts[step + 1] = gain_parts[step] + gain_recv[step]
+
+    gain_start(0)
+    scaled = normed_grad * gain_ref[0:1, :]
+    input_grad_ref[...] = (
+        mixed_grad_ref[...]
+        + scale_first * scaled
+        - rows_in * (scale_first * scale_first * scale_first) * jnp.mean(scaled * rows_in, axis=-1, keepdims=True)
+    )
+    gain_finish(0)
+    gain_start(1)
+    step_all(1)
+    gain_finish(1)
+    gain_start(2)
+    step_all(2)
+    gain_finish(2)
+    gain_start(3)
+    step_all(3)
+    gain_finish(3)
+    gain_start(4)
+    for step in range(3):
+        for one in (sums[3], sums[1], sums[2], sums[0]):
+            one.back_finish(step)
+            if step < 2:
+                one.back_start(step + 1)
+    gain_finish(4)
+    gain_out[...] = gain_parts[5]
+    for step in range(5):
+        wait_for(gain_parts.at[step], gain_send.at[step])
+
+
+def third_part(back, mixed, shared_out, ffn_grad, cotangent, hidden, logits, routes, gains, kept, segment, padding, weights):
+    tokens, width = hidden.shape
+    bfloat, single = jnp.bfloat16, jnp.float32
+    in_vmem = pl.BlockSpec(memory_space=pltpu.VMEM)
+    dma, shape, vmem = pltpu.SemaphoreType.DMA, jax.ShapeDtypeStruct, pltpu.VMEM
+    cosine, sine = rotary_tables(4 * tokens, width // HEADS)
+    work = (2, width // 4, width)
+    arguments = (
+        *back,
+        mixed,
+        shared_out,
+        ffn_grad,
+        cotangent,
+        hidden,
+        logits,
+        routes,
+        gains,
+        *kept,
+        segment[None, :],
+        segment[:, None],
+        padding[None, :],
+        jnp.asarray(cosine),
+        jnp.asarray(sine),
+        *weights,
+    )
+    return pl.pallas_call(
+        third_kernel,
+        out_shape=[
+            shape((tokens, width), bfloat),
+            shape((tokens, width), single),
+            shape((tokens, TOP), single),
+            shape((8, width), single),
+        ]
+        + [shape((1,) + work[1:], bfloat)] * 4,
+        in_specs=[in_vmem] * len(arguments),
+        out_specs=[in_vmem] * 8,
+        scratch_shapes=[vmem((tokens, width), bfloat)]
+        + [vmem((4 * tokens, width), bfloat)] * 3
+        + [vmem((tokens, width), bfloat), vmem((tokens, width), single)]
+        + [vmem((width, width), bfloat)] * 4
+        + [vmem(work, bfloat)] * 4
+        + [vmem((2, tokens, width), bfloat), vmem((tokens, width), bfloat)]
+        + [vmem(one, bfloat) for order in ATTENTION_ORDER for one in receive_shapes(work, order)]
+        + [vmem((6, 8, width), single), vmem((5, 8, width), single)]
+        + [dma((4, 2)), dma((4, 2)), dma((4, 7)), dma((4, 7)), dma((3,)), dma((3,)), dma((5,)), dma((5,))],
+        compiler_params=pltpu.CompilerParams(collective_id=2, has_side_effects=True, vmem_limit_bytes=60 << 20),
+        cost_estimate=pl.CostEstimate(flops=12000000000, bytes_accessed=25000000, transcendentals=3000000),
+    )(*arguments)
 
 
 def swap(value, axis, bit):
@@ -1072,8 +1339,32 @@
         grad_received = lax.all_to_all(send_grad, "expert", split_axis=0, concat_axis=0, tiled=True)
     if fast:
         returned, grad_back, *sums = second_part(received, grad_received, (e_gate, e_up, e_down), shared_work)
-        expert_grads = tuple(grad[None].astype(jnp.float32) for grad in sums[:3])
-        shared_grads = tuple(grad[0].astype(jnp.float32) for grad in sums[3:])
+        output, input_grad, logit_grad, gain_grads, *attention_grads = third_part(
+            (returned, grad_back),
+            mixed_rows,
+            shared_out,
+            ffn_grad_shared,
+            grad_low,
+            hidden_in[0],
+            gate_logits[0],
+            routes[0],
+            gains,
+            (normed_ctx, query_low, keys_ctx, values_ctx, log_total, attended),
+            segment_row,
+            padding_row,
+            (w_q, w_k, w_v, w_o),
+        )
+        gain_grads = lax.dynamic_slice_in_dim(gain_grads, shard_index * gain_attn.shape[0], gain_attn.shape[0], 1)
+        return (
+            output[None],
+            input_grad[None],
+            logit_grad[None],
+            gain_grads[0],
+            gain_grads[1],
+            *(grad[0].astype(jnp.float32) for grad in attention_grads),
+            *(grad[0].astype(jnp.float32) for grad in sums[3:]),
+            *(grad[None].astype(jnp.float32) for grad in sums[:3]),
+        )
     else:
         gate_pre = jnp.einsum("sid,df->sif", received, e_gate, preferred_element_type=jnp.float32)
         up_pre = jnp.einsum("sid,df->sif", received, e_up, preferred_element_type=jnp.float32)

time: 533 us -> 428 us (0.80)
  Pallas kernels: 308 us -> 398 us
  waiting for transfers between devices: 55.8 us -> 0 us
  matrix products: 39.6 us -> 0 us
  other arithmetic: 45.7 us -> 11.4 us
  local copies, waits for them, and re-layouts: 42.4 us -> 10.5 us
  blocking collectives: 22 us -> 0 us
  starting transfers between devices: 10.9 us -> 0 us
    pallas_call x0 -> x1, Pallas kernels: none -> 90.5 us  [third_part(): pl.pallas_call(third_kernel, out_shape=[shape((tokens, width), bfloat), s...]
    ppermute x12 -> x0, waiting for transfers between devices: 55.8 us -> none  [swap(): lax.ppermute(value, axis, [(index, index ^ bit) for index in range(size)])]
    dot_general x13 -> x0, matrix products: 39.6 us -> none  [the longest x1 11.5 us: shards(): jnp.einsum('qhd,khd->hqk', grad_attended, values_all, preferred_element_t...]
    psum x1 -> x0, blocking collectives: 22 us -> none  [shards(): lax.psum(scatter_shards(gain_rows), 'expert').astype(jnp.float32)]
    ppermute x12 -> x0, starting transfers between devices: 10.9 us -> none  [swap(): lax.ppermute(value, axis, [(index, index ^ bit) for index in range(size)])]
    reduce_sum x9 -> x0, other arithmetic: 10.8 us -> none  [the longest x1 3.65 us: shards(): contrib = jnp.sum(per_route * grad_out[:, None, :], axis=-1)]
    convert_element_type x17 -> x6, other arithmetic: 20.6 us -> 11.4 us  [the longest x4 6.62 us: shards(): grad[0].astype(jnp.float32)]
    gather x2 -> x0, local copies, waits for them, and re-layouts: 6.71 us -> none  [the longest x1 4 us: shards(): returned.reshape(experts * capacity, model_width)[places]]
  transfers between devices with their start and end apart: 12 -> 0, of which waited for: 6 -> 0; matrix products, arithmetic and copies ran while one was open for 5% -> 0% of each run, Pallas kernels for 0% -> 0%
where the time goes in v4:
time: 428 us; the launch traced here: 422 us
  Pallas kernels  398 us (93%)
  other arithmetic  11.4 us (3%)
  local copies, waits for them, and re-layouts  10.5 us (2%)
    pallas_call x1, Pallas kernels, second_part(): pl.pallas_call(second_kernel, out_shape=[shape(rows.shape, bfloat)] * 2 +...  159 us
    pallas_call x1, Pallas kernels, first_part(): pl.pallas_call(first_kernel, out_shape=[whole[name] for name in KEPT] + [...  149 us
    pallas_call x1, Pallas kernels, third_part(): pl.pallas_call(third_kernel, out_shape=[shape((tokens, width), bfloat), s...  90.5 us

profile of v4, /device:TPU:0, one launch (start us, length us, event | category | flops | bytes accessed | tf_op | source)
XLA Modules:
  0.0 421.6 jit_solution(2086293025149238247)
XLA Ops:
  0.6 0.7 stack.10
  1.3 0.7 stack.9
  2.0 0.2 dynamic_update_slice.3
  2.2 0.6 pad.4.refs_1_
  2.8 0.8 copy.42
  3.6 0.0 copy-start.5
  3.6 1.7 copy.43.refs_13_.refs_17_
  5.3 0.7 copy.44.refs_20_
  6.0 1.5 copy.41
  7.5 0.0 copy-done.5
  7.5 148.7 %shard_map.325 = (bf16[768,768]{1,0:T(8,128)(2,1)}, bf16[768,768]{1,0:T(8,128)(2,1)}, bf16[768,768]{1,0:T(8,128)(2,1)}, bf16[768,768]{1,0:T(8,128)(2,1)}, bf16[7...) custom-call(bf16[256,768]{1,0:T(8,128)(2,1)} %bitcast.59, ...), custom_call_target="tpu_custom_call" | custom-call | flops 15000000512 | bytes 47000000 | tf_op jit(solution)/shard_map/pallas_call | solution.py:492
  156.2 159.2 %shard_map.326 = (bf16[8,128,768]{2,1,0:T(8,128)(2,1)}, bf16[8,128,768]{2,1,0:T(8,128)(2,1)}, bf16[192,2048]{1,0:T(8,128)(2,1)}, bf16[192,2048]{1,0:T(8,128)(2,1...) custom-call(bf16[8,128,768]{2,1,0:T(8,128)(2,1)} %get-tuple-element., ...), custom_call_target="tpu_custom_call" | custom-call | flops 28999999488 | bytes 30000000 | tf_op jit(solution)/shard_map/pallas_call | solution.py:837
  315.4 3.5 bitcast_convert_fusion.1
  318.9 0.0 copy-done
  318.9 2.0 bitcast_convert_fusion.4
  320.9 90.5 %shard_map.327 = (bf16[256,768]{1,0:T(8,128)(2,1)}, f32[256,768]{1,0:T(8,128)}, f32[256,2]{1,0:T(8,128)}, f32[8,768]{1,0:T(8,128)}, bf16[1,192,768]{2,1,0:T(8,12...) custom-call(bf16[8,128,768]{2,1,0:T(8,128)(2,1)} %get-tuple-element.61.refs_0_, ...), custom_call_target="tpu_custom_call" | custom-call | flops 12000000000 | bytes 25000000 | tf_op jit(solution)/shard_map/pallas_call | solution.py:1107
  411.5 2.2 bitcast_convert_fusion.6
  413.8 1.1 bitcast_convert_fusion.8
  414.9 1.4 fusion
  416.3 0.7 copy.46
  417.0 1.3 bitcast_convert_fusion
  418.2 1.3 bitcast_convert_fusion.3
  419.5 0.7 copy.50
  420.2 0.9 copy.51
  (19 shorter events, 0.1 us)
Async XLA Ops:
  3.6 3.9 copy-start.5
  315.3 3.5 copy-start
  315.4 3.5 copy-start.1
  411.5 2.3 copy-start.7
  411.5 2.3 copy-start.8
  411.5 4.8 %copy-start.9 = (f32[256,2]{1,0:T(8,128)S(1)}, f32[256,2]{1,0:T(8,128)}, u32[]{:S(2)}) copy-start(f32[256,2]{1,0:T(8,128)} %get-tuple-element.79) | copy-start | bytes 6148
  411.5 5.5 %copy-start.4 = (bf16[512,768]{1,0:T(8,128)(2,1)S(1)}, bf16[512,768]{1,0:T(8,128)(2,1)}, u32[]{:S(2)}) copy-start(bf16[512,768]{1,0:T(8,128)(2,1)} %get-tuple-element.90) | copy-start | bytes 2359300
  414.9 3.4 copy-start.3
  418.2 1.3 copy-start.6
  418.2 2.0 copy-start.2
